TPU v7x, 512 devices: a whole 4x8x8 slice. The times are simulated.
512 devices in a mesh: half: 4 (over x), row: 8 (over z), col: 16 (over y, core).
Axes of the slice: x: 4, y: 8, z: 8, core: 2. Of those that a mesh axis runs over, the one named last changes fastest.
Arguments:
- image_map: bfloat16 [4, 128, 256, 512], P('half', 'row', 'col'), may hold values from -15 to 15
- qkv_weight: bfloat16 [512, 1536], replicated, may hold values from -0.25 to 0.25
- proj_weight: bfloat16 [512, 512], replicated, may hold values from -0.25 to 0.25
- head_scale: float32 [16], replicated, may hold values from 2 to 20
- bias_table: float32 [16, 961], replicated, may hold values from -4 to 4
- attn_gain: float32 [512], replicated, may hold values from 0.25 to 1.75
- expert_ids: int32 [4, 128, 256, 1], P('half', 'row', 'col'), may hold values from 0 to 31
- gate_prob: float32 [4, 128, 256], P('half', 'row', 'col'), may hold values from 0.3 to 1
- w_in: bfloat16 [128, 512, 512], P(('row', 'col')), may hold values from -0.25 to 0.25
- w_out: bfloat16 [128, 512, 512], P(('row', 'col')), may hold values from -0.125 to 0.125
- expert_gain: float32 [512], replicated, may hold values from 0.25 to 1.75
- grad_out: bfloat16 [4, 128, 256, 512], P('half', 'row', 'col'), may hold values from -6 to 6
Outputs:
- block_out: bfloat16 [4, 128, 256, 512], P('half', 'row', 'col')
- grad_map: bfloat16 [4, 128, 256, 512], P('half', 'row', 'col')
- grad_w_in: float32 [128, 512, 512], P(('row', 'col'), 'half')
- grad_w_out: float32 [128, 512, 512], P(('row', 'col'), 'half')
All inputs are finite; a program needn't handle non-finite values.
Results may differ from a plain program's by a relative error of at most 0.022.
Values may be sent and summed in bfloat16 or wider, within the bound.
No kernel may reach another device: no remote copies, remote signals or barrier semaphores. Data moves between devices by JAX's collectives and lax.ppermute only.
A program may use at most 192 MiB of HBM per device.

v0:
```python
import jax
import jax.numpy as jnp
from jax import lax
from jax.experimental import pallas as pl
from jax.experimental.pallas import tpu as pltpu
from jax.sharding import PartitionSpec as P

SPLIT = 4
WIN = 16
HALF = WIN // 2
CELLS = WIN * WIN
HEAD_W = 32
EPS = 1e-05
TURNS = 2
BF16 = jnp.bfloat16
F32 = jnp.float32
VMEM_BYTES = 56 * 1024 * 1024


def dotg(a, b, ca, cb):
    return lax.dot_general(a, b, (((ca,), (cb,)), ((), ())), preferred_element_type=F32)


def call(body, outs, scratch=(), smem=0, total=0, gflop=1.0):
    in_specs = [pl.BlockSpec(memory_space=pltpu.SMEM)] * smem
    in_specs += [pl.BlockSpec(memory_space=pltpu.VMEM)] * (total - smem)
    return pl.pallas_call(
        body,
        out_shape=tuple(jax.ShapeDtypeStruct(s, d) for s, d in outs),
        in_specs=in_specs,
        out_specs=tuple(pl.BlockSpec(memory_space=pltpu.VMEM) for _ in outs),
        scratch_shapes=list(scratch),
        compiler_params=pltpu.CompilerParams(vmem_limit_bytes=VMEM_BYTES),
        cost_estimate=pl.CostEstimate(
            flops=int(gflop * 1e9), bytes_accessed=1 << 20, transcendentals=0
        ),
    )


def assemble(parts):
    a, b, c, d = (part.astype(F32) for part in parts)
    whole = jnp.concatenate([jnp.concatenate([a, b], 1), jnp.concatenate([c, d], 1)], 0)
    return whole.reshape(CELLS, whole.shape[-1])


def store_parts(whole, refs):
    tile = whole.reshape(WIN, WIN, whole.shape[-1])
    for i, ref in enumerate(refs):
        r, c = HALF * (i // 2), HALF * (i % 2)
        ref[...] = tile[r : r + HALF, c : c + HALF].astype(BF16)


def spread_table(table, low, high):
    heads, entries = table.shape
    lanes = 2 * CELLS
    padded = jnp.concatenate([table[...], jnp.zeros((heads, 2 * lanes - entries), F32)], 1)
    row = lax.broadcasted_iota(jnp.int32, (heads, lanes), 1) >> 4
    low_rows = jnp.zeros((heads, lanes), F32)
    high_rows = jnp.zeros((heads, lanes), F32)
    for j in range(2 * WIN - 1):
        left = (WIN - 1) * j
        first = pltpu.roll(padded, (2 * lanes - left) % (2 * lanes), 1)[:, :lanes]
        other = pltpu.roll(padded, 2 * lanes - left - WIN, 1)[:, :lanes]
        low_rows = jnp.where(row == j, first, low_rows)
        high_rows = jnp.where(row == j, other, high_rows)
    low[...] = low_rows
    high[...] = high_rows


def attention_forward(
    edge, scale, img, beside, below, corner, wqkv, proj, table,
    out0, out1, out2, out3, qs, ku, vt, weights, aux, ho, prj, strips, mask, low, high,
):
    heads = scale.shape[0]
    width = heads * HEAD_W
    own = img[...].astype(F32)[HALF:, HALF:]
    x = assemble((own, beside[...], below[...], corner[...])).astype(BF16)
    prj[...] = dotg(wqkv[...], x, 0, 1)
    spread_table(table, low, high)
    key = lax.broadcasted_iota(jnp.int32, (CELLS, CELLS), 0)
    qry = lax.broadcasted_iota(jnp.int32, (CELLS, CELLS), 1)
    row_diff = jnp.where((key >> 7) != (qry >> 7), edge[0], 0)
    col_diff = jnp.where(((key >> 3) & 1) != ((qry >> 3) & 1), edge[1], 0)
    mask[...] = jnp.where(row_diff + col_diff > 0, -100.0, 0.0)
    lanes = 2 * CELLS
    sub = lax.broadcasted_iota(jnp.int32, (WIN, lanes), 0)
    lane = lax.broadcasted_iota(jnp.int32, (WIN, lanes), 1)
    from_low = (lane & (WIN - 1)) <= sub

    def head(h, turn):
        at = pl.multiple_of(h * HEAD_W, HEAD_W)
        q = prj[pl.ds(at, HEAD_W), :]
        k = prj[pl.ds(width + at, HEAD_W), :]
        v = prj[pl.ds(2 * width + at, HEAD_W), :].astype(BF16)
        q_sq = jnp.sum(q * q, 0, keepdims=True)
        k_sq = jnp.sum(k * k, 0, keepdims=True)
        q = (q * (lax.rsqrt(jnp.maximum(q_sq, 1.0)) * scale[h])).astype(BF16)
        k = (k * lax.rsqrt(jnp.maximum(k_sq, 1.0))).astype(BF16)
        qs[pl.ds(at, HEAD_W), :] = q
        ku[pl.ds(at, HEAD_W), :] = k
        vt[pl.ds(at, HEAD_W), :] = v
        scores = dotg(k, q, 0, 0)
        low_rows = jnp.broadcast_to(low[pl.ds(h, 1), :], (WIN, lanes))
        high_rows = jnp.broadcast_to(high[pl.ds(h, 1), :], (WIN, lanes))
        strip = jnp.where(
            from_low,
            pltpu.roll(low_rows, lanes - WIN + 1, 1, stride=1, stride_axis=0),
            pltpu.roll(high_rows, 1, 1, stride=1, stride_axis=0),
        )
        strips[turn, 0] = strip
        for m in range(1, 8):
            strips[turn, m] = pltpu.roll(strip, lanes - WIN * m, 1)
        total = jnp.zeros((WIN, CELLS), F32)
        for a in range(WIN):
            far, m = divmod((WIN - 1 - a), 8)
            rows = slice(WIN * a, WIN * (a + 1))
            bias = strips[turn, m, :, 128 * far : 128 * far + CELLS]
            w = jnp.exp(scores[rows] + bias + mask[rows, :])
            total = total + w
            weights[h, rows, :] = w.astype(BF16)
        inv = 1.0 / jnp.sum(total, 0, keepdims=True)
        aux[h, 0:1, :] = inv
        aux[h, 1:2, :] = q_sq
        aux[h, 2:3, :] = k_sq
        ho[pl.ds(at, HEAD_W), :] = (dotg(v, weights[h], 1, 0) * inv).astype(BF16)

    def heads_of(i, carry):
        for turn in range(TURNS):
            head(i * TURNS + turn, turn)
        return carry

    lax.fori_loop(0, heads // TURNS, heads_of, 0)
    store_parts(dotg(ho[...], proj[...], 0, 0), (out0, out1, out2, out3))


def attention_backward(
    scale, d0, d1, d2, d3, wqkv, proj, qs, ku, vt, weights, aux, ho,
    out0, out1, out2, out3, dho, dprj,
):
    heads = scale.shape[0]
    width = heads * HEAD_W
    d_out = assemble((d0[...], d1[...], d2[...], d3[...])).astype(BF16)
    dho[...] = dotg(proj[...], d_out, 1, 1)

    def unit_grad(d_unit, unit, sq):
        inner = jnp.sum(d_unit * unit, 0, keepdims=True)
        share = jnp.where(sq > 1.0, 1.0, jnp.where(sq == 1.0, 0.5, 0.0))
        return (d_unit - unit * (inner * share)) * lax.rsqrt(jnp.maximum(sq, 1.0))

    def head(h):
        at = pl.multiple_of(h * HEAD_W, HEAD_W)
        here = pl.ds(at, HEAD_W)
        q, k, v = qs[here, :], ku[here, :], vt[here, :]
        inv = aux[h, 0:1, :]
        d_ho = dho[here, :].astype(BF16).astype(F32)
        delta = jnp.sum(d_ho * ho[here, :].astype(F32), 0, keepdims=True) * inv
        d_ho = (d_ho * inv).astype(BF16)
        w = weights[h]
        d_w = dotg(v, d_ho, 0, 0)
        d_s = (w.astype(F32) * (d_w - delta)).astype(BF16)
        d_q = dotg(k, d_s, 1, 0) * scale[h]
        d_k = dotg(q, d_s, 1, 1)
        d_v = dotg(d_ho, w, 1, 1)
        q_unit = q.astype(F32) * (1.0 / scale[h])
        dprj[here, :] = unit_grad(d_q, q_unit, aux[h, 1:2, :]).astype(BF16)
        dprj[pl.ds(width + at, HEAD_W), :] = unit_grad(d_k, k.astype(F32), aux[h, 2:3, :]).astype(BF16)
        dprj[pl.ds(2 * width + at, HEAD_W), :] = d_v.astype(BF16)

    def heads_of(i, carry):
        for turn in range(TURNS):
            head(i * TURNS + turn)
        return carry

    lax.fori_loop(0, heads // TURNS, heads_of, 0)
    store_parts(dotg(dprj[...], wqkv[...], 0, 1), (out0, out1, out2, out3))


def normal(values):
    center = values - jnp.mean(values, -1, keepdims=True)
    rstd = lax.rsqrt(jnp.mean(center * center, -1, keepdims=True) + EPS)
    return center * rstd, rstd


def norm_grad(unit, rstd, d_unit):
    return rstd * (
        d_unit
        - jnp.mean(d_unit, -1, keepdims=True)
        - unit * jnp.mean(d_unit * unit, -1, keepdims=True)
    )


def column(field):
    row = lax.broadcasted_iota(jnp.int32, (CELLS, WIN), 0)
    col = lax.broadcasted_iota(jnp.int32, (CELLS, WIN), 1)
    pick = jnp.where((row >> 4) == col, 1.0, 0.0)
    rows = lax.dot_general(
        pick, field, (((1,), (0,)), ((), ())),
        preferred_element_type=F32, precision=lax.Precision.HIGHEST,
    )
    return jnp.sum(jnp.where((row & (WIN - 1)) == col, rows, 0.0), 1, keepdims=True)


def place_tokens(ids, gate, grad, place, packed, experts, cap):
    expert = column(ids[...].astype(F32)).astype(jnp.int32)
    matches = expert == lax.broadcasted_iota(jnp.int32, (CELLS, experts), 1)
    later = lax.broadcasted_iota(jnp.int32, (CELLS, CELLS), 0)
    sooner = lax.broadcasted_iota(jnp.int32, (CELLS, CELLS), 1)
    earlier = jnp.where(later > sooner, 1.0, 0.0).astype(BF16)
    before = dotg(earlier, jnp.where(matches, 1.0, 0.0).astype(BF16), 1, 0)
    slot = jnp.sum(jnp.where(matches, before, 0.0), 1, keepdims=True).astype(jnp.int32)
    target = jnp.where(slot < cap, expert * cap + slot, -1)
    slots = lax.broadcasted_iota(jnp.int32, (CELLS, experts * cap), 1)
    where_to = jnp.where(target == slots, 1.0, 0.0).astype(BF16)
    place[...] = where_to
    weighted = (grad[...].astype(F32) * column(gate[...])).astype(BF16)
    packed[...] = dotg(where_to, weighted, 0, 0).astype(BF16).reshape(packed.shape)


def pack_residual(att0, att1, att2, att3, img, gain, place, packed, att):
    attention = assemble((att0[...], att1[...], att2[...], att3[...]))
    att[...] = attention.astype(BF16)
    unit, _ = normal(attention)
    routed = (img[...].astype(F32) + unit * gain[...]).astype(BF16)
    packed[...] = dotg(place[...], routed, 0, 0).astype(BF16).reshape(packed.shape)


def residual_grad(att, gain, place, grad, back, d_resid, d0, d1, d2, d3):
    unit, rstd = normal(att[...].astype(F32))
    total = grad[...].astype(F32) + dotg(place[...], back[...].reshape(grad.shape), 1, 0)
    d_resid[...] = total
    store_parts(norm_grad(unit, rstd, total * gain[...]), (d0, d1, d2, d3))


def finish_block(att, img, gain, place, gate, mixed, out):
    unit, _ = normal(att[...].astype(F32))
    residual = img[...].astype(F32) + unit * gain[...]
    added = column(gate[...]) * dotg(place[...], mixed[...].reshape(img.shape), 1, 0)
    out[...] = (residual + added).astype(BF16)


def gelu_parts(hidden):
    cdf = 0.5 * (1.0 + lax.erf(hidden * 0.7071067811865476))
    pdf = jnp.exp(hidden * hidden * -0.5) * 0.3989422804014327
    return hidden * cdf, cdf + hidden * pdf


def expert_rows(rows, grad, gain, near, far, mixed, d_expert, d_rows, slope):
    half = near.shape[1] // 2
    flat = d_expert.shape
    here = rows[...].reshape(flat)
    blocks = [(ref, i) for ref in (near, far) for i in range(2)]
    total = jnp.zeros(flat, F32)
    for s, (ref, i) in enumerate(blocks):
        act, slope[s] = gelu_parts(dotg(here, ref[i, :half, :], 1, 0))
        total = total + dotg(act.astype(BF16), ref[i, half:, :], 1, 0).astype(BF16).astype(F32)
    unit, rstd = normal(total)
    mixed[...] = (unit * gain[...]).astype(BF16).reshape(mixed.shape)
    d_out = norm_grad(unit, rstd, grad[...].reshape(flat).astype(F32) * gain[...]).astype(BF16)
    d_expert[...] = d_out
    total = jnp.zeros(flat, F32)
    for s, (ref, i) in enumerate(blocks):
        d_hidden = (dotg(d_out, ref[i, half:, :], 1, 1) * slope[s]).astype(BF16)
        total = total + dotg(d_hidden, ref[i, :half, :], 1, 1).astype(BF16).astype(F32)
    d_rows[...] = total.astype(BF16).reshape(d_rows.shape)


def expert_grads(place, rows, grad0, grad1, grad2, grad3, w_in, w_out, both):
    count, width = grad0.shape
    d_in = jnp.zeros(w_in.shape, F32)
    d_out = jnp.zeros(w_out.shape, F32)
    for s, grad in enumerate((grad0, grad1, grad2, grad3)):
        part = rows[pl.ds(pl.multiple_of((place[0] ^ s) * count, count), count), :]
        act, slope = gelu_parts(dotg(part, w_in[...], 1, 0))
        d_out = d_out + dotg(act.astype(BF16), grad[...], 0, 0)
        d_hidden = (dotg(grad[...], w_out[...], 1, 1) * slope).astype(BF16)
        d_in = d_in + dotg(part, d_hidden, 0, 0)
    both[:, : w_in.shape[1]] = d_in.astype(BF16)
    both[:, w_in.shape[1] :] = d_out.astype(BF16)


def send(piece, down, right):
    rows, cols = lax.axis_size("row"), lax.axis_size("col")
    if right == 0:
        return lax.ppermute(piece, "row", [(i, (i + down) % rows) for i in range(rows)])
    if down == 0:
        return lax.ppermute(piece, "col", [(i, (i + right) % cols) for i in range(cols)])
    route = [
        (r * cols + c, (r + down) % rows * cols + (c + right) % cols)
        for r in range(rows)
        for c in range(cols)
    ]
    return lax.ppermute(piece, ("row", "col"), route)


def to_window(part0, part1, part2, part3):
    return part3, send(part2, 0, -1), send(part1, -1, 0), send(part0, -1, -1)


def from_window(part0, part1, part2, part3):
    return send(part3, 1, 1), send(part2, 1, 0), send(part1, 0, 1), part0


def exchange(parts):
    return lax.all_to_all(parts, ("row", "col"), split_axis=0, concat_axis=0, tiled=True)


def group_gather(rows):
    cols = lax.axis_size("col")
    groups = [[g + i for i in range(SPLIT)] for g in range(0, cols, SPLIT)]
    return lax.all_gather(rows, "col", axis_index_groups=groups, axis=0, tiled=True)


def swap(piece, bit):
    return lax.ppermute(piece, "col", [(i, i ^ bit) for i in range(lax.axis_size("col"))])


def gather_blocks(blocks):
    cols = lax.axis_size("col")
    groups = [[g + i, g + i + 2] for g in range(0, cols, SPLIT) for i in range(2)]
    return lax.all_gather(blocks, "col", axis_index_groups=groups, axis=0, tiled=False)


def shards(
    image_map,
    qkv_weight,
    proj_weight,
    head_scale,
    bias_table,
    attn_gain,
    expert_ids,
    gate_prob,
    w_in,
    w_out,
    expert_gain,
    grad_out,
):
    width = image_map.shape[3]
    heads = head_scale.shape[0]
    row_count, col_count = lax.axis_size("row"), lax.axis_size("col")
    devices = row_count * col_count
    experts = devices // SPLIT
    cap = CELLS // experts
    slots = experts * cap
    tile = (WIN, WIN, width)
    quarter = (HALF, HALF, width)
    flat = (CELLS, width)
    parts = (devices, slots // devices, width)
    tile_img = image_map[0]
    img = tile_img.reshape(flat)
    grad = grad_out[0].reshape(flat)
    ids = expert_ids.reshape(WIN, WIN)
    gate = gate_prob.reshape(WIN, WIN)
    a_gain = attn_gain.reshape(1, width)
    e_gain = expert_gain.reshape(1, width)

    pieces = (tile_img[:HALF, :HALF], tile_img[:HALF, HALF:], tile_img[HALF:, :HALF])
    _, beside, below, corner = to_window(*pieces, None)
    place, grad_packed = call(
        lambda *refs: place_tokens(*refs, experts=experts, cap=cap),
        [((CELLS, slots), BF16), (parts, BF16)],
        total=3,
    )(ids, gate, grad)
    grad_slots = exchange(grad_packed)
    first_w, second_w, _ = lax.optimization_barrier((w_in[0], w_out[0], pieces))
    near = gather_blocks(jnp.concatenate([first_w, second_w], 0))
    edge = jnp.stack(
        [lax.axis_index("row") == row_count - 1, lax.axis_index("col") == col_count - 1]
    ).astype(jnp.int32)
    corner, _ = lax.optimization_barrier((corner, grad_packed))
    *attn_parts, qs, ku, vt, weights, aux, ho = call(
        attention_forward,
        [(quarter, BF16)] * 4
        + [((width, CELLS), BF16)] * 3
        + [
            ((heads, CELLS, CELLS), BF16),
            ((heads, 8, CELLS), F32),
            ((width, CELLS), BF16),
        ],
        [
            pltpu.VMEM((3 * width, CELLS), F32),
            pltpu.VMEM((TURNS, 8, WIN, 2 * CELLS), F32),
            pltpu.VMEM((CELLS, CELLS), F32),
            pltpu.VMEM((heads, 2 * CELLS), F32),
            pltpu.VMEM((heads, 2 * CELLS), F32),
        ],
        smem=2,
        total=9,
        gflop=8.0,
    )(edge, head_scale, tile_img, beside, below, corner, qkv_weight, proj_weight, bias_table)
    att_parts = from_window(*attn_parts)
    *att_parts, grad_slots = lax.optimization_barrier((*att_parts, grad_slots))
    packed, att = call(pack_residual, [(parts, BF16), (flat, BF16)], total=7)(
        *att_parts, img, a_gain, place
    )
    near, _ = lax.optimization_barrier((near, packed))
    far = swap(near, 1)
    rows = exchange(packed)
    all_rows = group_gather(rows.reshape(flat))
    mixed, d_expert, d_rows = call(
        expert_rows,
        [(parts, BF16), (flat, BF16), (parts, BF16)],
        [pltpu.VMEM((SPLIT,) + flat, F32)],
        total=5,
        gflop=2.0,
    )(rows, grad_slots, e_gain, near, far)
    back = exchange(d_rows)
    across = swap(d_expert, 2)
    grads = (d_expert, swap(d_expert, 1), across, swap(across, 1))
    place_in_group = (lax.axis_index("col") % SPLIT).astype(jnp.int32).reshape(1)
    (both,) = call(
        expert_grads, [((w_in.shape[1], 2 * w_in.shape[2]), BF16)], smem=1, total=8, gflop=0.01
    )(place_in_group, all_rows, *grads, w_in[0], w_out[0])
    back, both = lax.optimization_barrier((back, both))
    both = lax.psum_scatter(both, "half", scatter_dimension=0, tiled=True).astype(F32)
    grad_w_in, grad_w_out = both[None, :, : w_in.shape[2]], both[None, :, w_in.shape[2] :]
    d_resid, *d_att = call(residual_grad, [(flat, F32)] + [(quarter, BF16)] * 4, total=5)(
        att, a_gain, place, grad, back
    )
    mixed, *d_att = lax.optimization_barrier((mixed, *d_att))
    mixed_back = exchange(mixed)
    d_rolled = call(
        attention_backward,
        [(quarter, BF16)] * 4,
        [pltpu.VMEM((width, CELLS), F32), pltpu.VMEM((3 * width, CELLS), BF16)],
        smem=1,
        total=13,
        gflop=8.0,
    )(head_scale, *to_window(*d_att), qkv_weight, proj_weight, qs, ku, vt, weights, aux, ho)
    *d_rolled, mixed_back = lax.optimization_barrier((*d_rolled, mixed_back))
    (block_out,) = call(finish_block, [(flat, BF16)], total=6)(
        att, img, a_gain, place, gate, mixed_back
    )
    top_left, top_right, bottom_left, bottom_right = from_window(*d_rolled)
    returned = jnp.concatenate(
        [
            jnp.concatenate([top_left, top_right], 1),
            jnp.concatenate([bottom_left, bottom_right], 1),
        ],
        0,
    )
    grad_map = (d_resid.reshape(tile) + returned.astype(F32)).astype(BF16)
    return (block_out.reshape(image_map.shape), grad_map[None], grad_w_in, grad_w_out)


def solution(mesh):
    tokens = P("half", "row", "col", None)
    in_specs = (
        tokens,
        P(),
        P(),
        P(),
        P(),
        P(),
        tokens,
        P("half", "row", "col"),
        P(("row", "col"), None, None),
        P(("row", "col"), None, None),
        P(),
        tokens,
    )
    out_specs = (
        tokens,
        tokens,
        P(("row", "col"), "half", None),
        P(("row", "col"), "half", None),
    )
    return jax.shard_map(shards, mesh=mesh, in_specs=in_specs, out_specs=out_specs, check_vma=False)
```

profile of v0, /device:TPU:2, one launch (start us, length us, event | category | flops | bytes accessed | tf_op | source)
XLA Modules:
  0.0 189.8 jit_solution(18047208624659370264)
XLA Ops:
  8.0 0.9 fusion
  9.0 2.3 %pad_maximum_fusion = bf16[1024,512]{1,0:T(8,128)(2,1)} fusion(bf16[512,512]{1,0:T(8,128)(2,1)} %bitcast.23, bf16[512,512]{1,0:T(8,128)(2,1)} %bitcast.25), kind=kLoop, calls=%fused_computation | loop fusion | flops 2097152 | bytes 2097152 | tf_op jit(solution)/shard_map/concatenate | solution.py:365
  11.2 2.9 %collective-permute-start = (bf16[8,8,512]{2,1,0:T(8,128)(2,1)S(1)}, bf16[8,8,512]{2,1,0:T(8,128)(2,1)S(1)}, u32[]{:S(2)}, u32[]{:S(2)}) collective-permute-start(bf16[8,8,512]{2,1,0:T(8,128)(2,1)S(1)} %get-tuple-element.102), channel_id=1, source_target_pairs={{0,15},{1,0},{2,1},{3,2},{4,3},{5,4},{6,5},{7,6},{8,7},{9,8},{10,9... | collective-permute-start | bytes 196616 | tf_op jit(solution)/shard_map/ppermute | solution.py:286
  14.2 10.9 %collective-permute-start.1 = (bf16[8,8,512]{2,1,0:T(8,128)(2,1)S(1)}, bf16[8,8,512]{2,1,0:T(8,128)(2,1)S(1)}, u32[]{:S(2)}, u32[]{:S(2)}) collective-permute-start(bf16[8,8,512]{2,1,0:T(8,128)(2,1)S(1)} %get-tuple-element.101), channel_id=1, source_target_pairs={{0,112},{16,0},{32,16},{48,32},{64,48},{80,64},{96,80},{112,96},{1... | collective-permute-start | bytes 196616 | tf_op jit(solution)/shard_map/ppermute | solution.py:284
  25.1 2.3 %collective-permute-start.2 = (bf16[8,8,512]{2,1,0:T(8,128)(2,1)S(1)}, bf16[8,8,512]{2,1,0:T(8,128)(2,1)S(1)}, u32[]{:S(2)}, u32[]{:S(2)}) collective-permute-start(bf16[8,8,512]{2,1,0:T(8,128)(2,1)S(1)} %get-tuple-element.100), channel_id=1, source_target_pairs={{0,127},{1,112},{2,113},{3,114},{4,115},{5,116},{6,117},{7,118},{8... | collective-permute-start | bytes 196616 | tf_op jit(solution)/shard_map/ppermute | solution.py:292
  27.4 2.8 %shard_map.147 = (bf16[256,256]{1,0:T(8,128)(2,1)}, bf16[128,2,512]{2,1,0:T(2,128)(2,1)}) custom-call(s32[16,16]{1,0:T(8,128)} %bitcast.36, f32[16,16]{1,0:T(8,128)} %bitcast.37, bf16[256,512]{1,0:T(8,128)(2,1)} %bitcast.34), custom_call_target="tpu_custom_call" | custom-call | flops 1000000000 | bytes 1048576 | tf_op jit(solution)/shard_map/pallas_call | solution.py:358
  30.2 7.3 %all-to-all-start = ((bf16[128,2,512]{2,1,0:T(2,128)(2,1)}), bf16[128,2,512]{2,1,0:T(2,128)(2,1)S(1)}, u32[]{:S(2)}, u32[]{:S(2)}) async-start(bf16[128,2,512]{2,1,0:T(2,128)(2,1)} %get-tuple-element.51), calls=%async_computation | async-start | bytes 524288 | tf_op jit(solution)/shard_map/all_to_all | solution.py:304
  37.6 0.6 add_convert_fusion.1.edge
  38.2 0.6 copy-done.12
  38.8 0.6 copy-done.11
  39.4 9.4 %shard_map.148 = (bf16[8,8,512]{2,1,0:T(8,128)(2,1)}, bf16[8,8,512]{2,1,0:T(8,128)(2,1)}, bf16[8,8,512]{2,1,0:T(8,128)(2,1)}, bf16[8,8,512]{2,1,0:T(8,128)(2,1)}...) custom-call(s32[2]{0:T(128)} %add_convert_fusion.1.edge, ...), custom_call_target="tpu_custom_call" | custom-call | flops 8000000000 | bytes 1048576 | tf_op jit(solution)/shard_map/pallas_call | solution.py:370
  48.8 2.8 %collective-permute-start.3 = (bf16[8,8,512]{2,1,0:T(8,128)(2,1)}, bf16[8,8,512]{2,1,0:T(8,128)(2,1)S(1)}, u32[]{:S(2)}, u32[]{:S(2)}) collective-permute-start(bf16[8,8,512]{2,1,0:T(8,128)(2,1)} %get-tuple-element.53), channel_id=1, source_target_pairs={{0,17},{1,18},{2,19},{3,20},{4,21},{5,22},{6,23},{7,24},{8,25},{9,... | collective-permute-start | bytes 196616 | tf_op jit(solution)/shard_map/ppermute | solution.py:292
  51.6 3.5 %collective-permute-start.4 = (bf16[8,8,512]{2,1,0:T(8,128)(2,1)}, bf16[8,8,512]{2,1,0:T(8,128)(2,1)S(1)}, u32[]{:S(2)}, u32[]{:S(2)}) collective-permute-start(bf16[8,8,512]{2,1,0:T(8,128)(2,1)} %get-tuple-element.54), channel_id=1, source_target_pairs={{0,16},{16,32},{32,48},{48,64},{64,80},{80,96},{96,112},{112,0},{1... | collective-permute-start | bytes 196616 | tf_op jit(solution)/shard_map/ppermute | solution.py:284
  55.1 1.0 collective-permute-start.5
  56.1 1.8 collective-permute-done.3.att0
  57.9 1.7 collective-permute-done.4.att1
  59.6 0.6 collective-permute-done.5.att2
  60.2 0.6 copy-done.18
  60.8 2.4 %shard_map.149 = (bf16[128,2,512]{2,1,0:T(2,128)(2,1)}, bf16[256,512]{1,0:T(8,128)(2,1)}) custom-call(bf16[8,8,512]{2,1,0:T(8,128)(2,1)} %copy-done.16, bf16[8,8,512]{2,1,0:T(8,128)(2,1)} %copy-done.17, bf16[8,8,512]{2,1,0:T(8,128)(2,1)} %copy-done.18, bf16[8,8,512]{2,1,0:T(8,128)(2,1)} %get-tuple-element.60.att3, bf16[256,512]{1,0:T(8,128)(2,1)} %bitcast.30, ...), custom_call_target="tpu_custom_call" | custom-call | flops 1000000000 | bytes 1048576 | tf_op jit(solution)/shard_map/pallas_call | solution.py:392
  63.2 1.9 %collective-permute-start.6 = (bf16[2,1024,512]{2,1,0:T(8,128)(2,1)}, bf16[2,1024,512]{2,1,0:T(8,128)(2,1)S(1)}, u32[]{:S(2)}, u32[]{:S(2)}) collective-permute-start(bf16[2,1024,512]{2,1,0:T(8,128)(2,1)} %bitcast.32), channel_id=1, source_target_pairs={{0,1},{1,0},{2,3},{3,2},{4,5},{5,4},{6,7},{7,6},{8,9},{9,8},{10,11... | collective-permute-start | bytes 6291464 | tf_op jit(solution)/shard_map/ppermute | solution.py:314
  65.1 29.3 %all_to_all.20.rows = bf16[128,2,512]{2,1,0:T(2,128)(2,1)S(1)} all-to-all(bf16[128,2,512]{2,1,0:T(2,128)(2,1)} %get-tuple-element.63), channel_id=1, replica_groups=mesh['half'=4,'row'=8,'col'=16] {'row','col'}, dimensions={0} | all-to-all | bytes 524288 | tf_op jit(solution)/shard_map/all_to_all | solution.py:304
  94.4 0.8 reshape.79
  95.3 1.3 copy-done.9
  96.6 7.0 %shard_map.150 = (bf16[128,2,512]{2,1,0:T(2,128)(2,1)}, bf16[256,512]{1,0:T(8,128)(2,1)}, bf16[128,2,512]{2,1,0:T(2,128)(2,1)}) custom-call(bf16[128,2,512]{2,1,0:T(2,128)(2,1)} %copy-done, bf16[128,2,512]{2,1,0:T(2,128)(2,1)} %copy-done.5, f32[1,512]{1,0:T(1,128)} %bitcast.39, bf16[2,1024,512]{2,1,0:T(8,128)(2,1)} %bitcast.33, bf16[2,1024,512]{2,1,0:T(8,128)(2,1)} %copy-done.9), custom_call_target="tpu_custom_call" | custom-call | flops 2000000000 | bytes 1048576 | tf_op jit(solution)/shard_map/pallas_call | solution.py:399
  103.6 3.0 %collective-permute-start.8 = (bf16[256,512]{1,0:T(8,128)(2,1)}, bf16[256,512]{1,0:T(8,128)(2,1)S(1)}, u32[]{:S(2)}, u32[]{:S(2)}) collective-permute-start(bf16[256,512]{1,0:T(8,128)(2,1)} %get-tuple-element.70.grad0), channel_id=1, source_target_pairs={{0,2},{1,3},{2,0},{3,1},{4,6},{5,7},{6,4},{7,5},{8,10},{9,11},{10,... | collective-permute-start | bytes 786440 | tf_op jit(solution)/shard_map/ppermute | solution.py:314
  106.7 6.4 %all-to-all-start.2 = ((bf16[128,2,512]{2,1,0:T(2,128)(2,1)}), bf16[128,2,512]{2,1,0:T(2,128)(2,1)S(1)}, u32[]{:S(2)}, u32[]{:S(2)}) async-start(bf16[128,2,512]{2,1,0:T(2,128)(2,1)} %get-tuple-element.69), calls=%async_computation.2 | async-start | bytes 524288 | tf_op jit(solution)/shard_map/all_to_all | solution.py:304
  113.1 1.9 %collective-permute-start.7 = (bf16[256,512]{1,0:T(8,128)(2,1)}, bf16[256,512]{1,0:T(8,128)(2,1)S(1)}, u32[]{:S(2)}, u32[]{:S(2)}) collective-permute-start(bf16[256,512]{1,0:T(8,128)(2,1)} %get-tuple-element.70.grad0), channel_id=1, source_target_pairs={{0,1},{1,0},{2,3},{3,2},{4,5},{5,4},{6,7},{7,6},{8,9},{9,8},{10,11... | collective-permute-start | bytes 786440 | tf_op jit(solution)/shard_map/ppermute | solution.py:314
  115.0 6.0 %collective-permute-done.8.grad2 = bf16[256,512]{1,0:T(8,128)(2,1)S(1)} collective-permute-done((bf16[256,512]{1,0:T(8,128)(2,1)}, bf16[256,512]{1,0:T(8,128)(2,1)S(1)}, u32[]{:S(2)}, u32[]{:S(2)}) %collective-permute-start.8) | collective-permute-done | bytes 262176 | tf_op jit(solution)/shard_map/ppermute | solution.py:314
  121.1 1.9 %collective-permute-start.9 = (bf16[256,512]{1,0:T(8,128)(2,1)S(1)}, bf16[256,512]{1,0:T(8,128)(2,1)S(1)}, u32[]{:S(2)}, u32[]{:S(2)}) collective-permute-start(bf16[256,512]{1,0:T(8,128)(2,1)S(1)} %collective-permute-done.8.grad2), channel_id=1, source_target_pairs={{0,1},{1,0},{2,3},{3,2},{4,5},{5,4},{6,7},{7,6},{8,9},{9,8},{10,11... | collective-permute-start | bytes 786440 | tf_op jit(solution)/shard_map/ppermute | solution.py:314
  123.0 1.4 collective-permute-done.9.grad3
  124.5 0.7 copy-done.4
  125.2 6.2 %shard_map.151 = bf16[512,1024]{1,0:T(8,128)(2,1)} custom-call(s32[1]{0:T(128)} %bitcast.12.place, bf16[1024,512]{1,0:T(8,128)(2,1)} %all-gather.4.cloned.1.call-done.rows, bf16[256,512]{1,0:T(8,128)(2,1)} %get-tuple-element.70.grad0, bf16[256,512]{1,0:T(8,128)(2,1)} %copy-done.3, bf16[256,512]{1,0:T(8,128)(2,1)} %copy-done.2, bf16[256,512]{1,0:T(8,128)(2,1)} %copy-done.4, ...), custom_call_target="tpu_custom_call" | custom-call | flops 10000000 | bytes 1048576 | tf_op jit(solution)/shard_map/pallas_call | solution.py:410
  131.4 0.7 copy-done.6
  132.1 2.4 %shard_map.152 = (f32[256,512]{1,0:T(8,128)}, bf16[8,8,512]{2,1,0:T(8,128)(2,1)}, bf16[8,8,512]{2,1,0:T(8,128)(2,1)}, bf16[8,8,512]{2,1,0:T(8,128)(2,1)}, bf16[8,8,512]{2,1,0:T(8,128)(2,1)}) custom-call(bf16[256,512]{1,0:T(8,128)(2,1)} %get-tuple-element.62.att, f32[1,512]{1,0:T(1,128)} %bitcast.41, bf16[256,256]{1,0:T(8,128)(2,1)} %get-tuple-element.61.place, ...), custom_call_target="tpu_custom_call" | custom-call | flops 1000000000 | bytes 1048576 | tf_op jit(solution)/shard_map/pallas_call | solution.py:416
  134.5 2.0 %collective-permute-start.10 = (bf16[8,8,512]{2,1,0:T(8,128)(2,1)}, bf16[8,8,512]{2,1,0:T(8,128)(2,1)S(1)}, u32[]{:S(2)}, u32[]{:S(2)}) collective-permute-start(bf16[8,8,512]{2,1,0:T(8,128)(2,1)} %get-tuple-element.77), channel_id=1, source_target_pairs={{0,15},{1,0},{2,1},{3,2},{4,3},{5,4},{6,5},{7,6},{8,7},{9,8},{10,9... | collective-permute-start | bytes 196616 | tf_op jit(solution)/shard_map/ppermute | solution.py:286
  136.5 4.4 %collective-permute-start.11 = (bf16[8,8,512]{2,1,0:T(8,128)(2,1)}, bf16[8,8,512]{2,1,0:T(8,128)(2,1)S(1)}, u32[]{:S(2)}, u32[]{:S(2)}) collective-permute-start(bf16[8,8,512]{2,1,0:T(8,128)(2,1)} %get-tuple-element.78), channel_id=1, source_target_pairs={{0,112},{16,0},{32,16},{48,32},{64,48},{80,64},{96,80},{112,96},{1... | collective-permute-start | bytes 196616 | tf_op jit(solution)/shard_map/ppermute | solution.py:284
  140.9 2.0 %collective-permute-start.12 = (bf16[8,8,512]{2,1,0:T(8,128)(2,1)}, bf16[8,8,512]{2,1,0:T(8,128)(2,1)S(1)}, u32[]{:S(2)}, u32[]{:S(2)}) collective-permute-start(bf16[8,8,512]{2,1,0:T(8,128)(2,1)} %get-tuple-element.79), channel_id=1, source_target_pairs={{0,127},{1,112},{2,113},{3,114},{4,115},{5,116},{6,117},{7,118},{8... | collective-permute-start | bytes 196616 | tf_op jit(solution)/shard_map/ppermute | solution.py:292
  142.9 10.2 %all-to-all-start.3 = ((bf16[128,2,512]{2,1,0:T(2,128)(2,1)}), bf16[128,2,512]{2,1,0:T(2,128)(2,1)S(1)}, u32[]{:S(2)}, u32[]{:S(2)}) async-start(bf16[128,2,512]{2,1,0:T(2,128)(2,1)} %get-tuple-element.90), calls=%async_computation.3 | async-start | bytes 524288 | tf_op jit(solution)/shard_map/all_to_all | solution.py:304
  153.1 0.6 copy-done.13
  153.8 9.4 %shard_map.153 = (bf16[8,8,512]{2,1,0:T(8,128)(2,1)}, bf16[8,8,512]{2,1,0:T(8,128)(2,1)}, bf16[8,8,512]{2,1,0:T(8,128)(2,1)}, bf16[8,8,512]{2,1,0:T(8,128)(2,1)}) custom-call(f32[16]{0:T(128)} %scale.3, bf16[8,8,512]{2,1,0:T(8,128)(2,1)} %get-tuple-element.76.d0, bf16[8,8,512]{2,1,0:T(8,128)(2,1)} %copy-done.13, bf16[8,8,512]{2,1,0:T(8,128)(2,1)} %copy-done.14, ...), custom_call_target="tpu_custom_call" | custom-call | flops 8000000000 | bytes 1048576 | tf_op jit(solution)/shard_map/pallas_call | solution.py:421
  163.2 4.6 %all-to-all-done.3.mixed = bf16[128,2,512]{2,1,0:T(2,128)(2,1)S(1)} async-done(((bf16[128,2,512]{2,1,0:T(2,128)(2,1)}), bf16[128,2,512]{2,1,0:T(2,128)(2,1)S(1)}, u32[]{:S(2)}, u32[]{:S(2)}) %all-to-all-start.3) | async-done | bytes 262176 | tf_op jit(solution)/shard_map/all_to_all | solution.py:304
  167.9 2.7 %collective-permute-start.14 = (bf16[8,8,512]{2,1,0:T(8,128)(2,1)}, bf16[8,8,512]{2,1,0:T(8,128)(2,1)S(1)}, u32[]{:S(2)}, u32[]{:S(2)}) collective-permute-start(bf16[8,8,512]{2,1,0:T(8,128)(2,1)} %get-tuple-element.94), channel_id=1, source_target_pairs={{0,16},{16,32},{32,48},{48,64},{64,80},{80,96},{96,112},{112,0},{1... | collective-permute-start | bytes 196616 | tf_op jit(solution)/shard_map/ppermute | solution.py:284
  170.7 2.9 %collective-permute-start.13 = (bf16[8,8,512]{2,1,0:T(8,128)(2,1)}, bf16[8,8,512]{2,1,0:T(8,128)(2,1)S(1)}, u32[]{:S(2)}, u32[]{:S(2)}) collective-permute-start(bf16[8,8,512]{2,1,0:T(8,128)(2,1)} %get-tuple-element.93), channel_id=1, source_target_pairs={{0,17},{1,18},{2,19},{3,20},{4,21},{5,22},{6,23},{7,24},{8,25},{9,... | collective-permute-start | bytes 196616 | tf_op jit(solution)/shard_map/ppermute | solution.py:292
  173.5 2.3 %shard_map.154 = bf16[256,512]{1,0:T(8,128)(2,1)} custom-call(bf16[256,512]{1,0:T(8,128)(2,1)} %get-tuple-element.62.att, bf16[256,512]{1,0:T(8,128)(2,1)} %bitcast.31, f32[1,512]{1,0:T(1,128)} %bitcast.42, bf16[256,256]{1,0:T(8,128)(2,1)} %get-tuple-element.61.place, f32[16,16]{1,0:T(8,128)} %bitcast.38, bf16[128,2,512]{2,1,0:T(2,128)(2,1)} %copy-done.7), custom_call_target="tpu_custom_call" | custom-call | flops 1000000000 | bytes 1048576 | tf_op jit(solution)/shard_map/pallas_call | solution.py:430
  176.3 3.4 %collective-permute-done.13 = bf16[8,8,512]{2,1,0:T(8,128)(2,1)S(1)} collective-permute-done((bf16[8,8,512]{2,1,0:T(8,128)(2,1)}, bf16[8,8,512]{2,1,0:T(8,128)(2,1)S(1)}, u32[]{:S(2)}, u32[]{:S(2)}) %collective-permute-start.13) | collective-permute-done | bytes 65568 | tf_op jit(solution)/shard_map/ppermute | solution.py:292
  179.8 0.8 add_convert_fusion
  180.6 1.0 convert_element_type.29
  181.6 0.8 slice_bitcast_fusion
  (55 shorter events, 1.0 us)
Async XLA Ops:
  8.0 55.2 %all-gather.6.cloned.1.call-start = ((), (), s32[]{:S(2)}) async-start(), calls=%async_computation.7 | async-start | bytes 3145728 | tf_op jit(solution)/shard_map/all_gather | solution.py:320
  11.2 26.9 %collective-permute-start = (bf16[8,8,512]{2,1,0:T(8,128)(2,1)S(1)}, bf16[8,8,512]{2,1,0:T(8,128)(2,1)S(1)}, u32[]{:S(2)}, u32[]{:S(2)}) collective-permute-start(bf16[8,8,512]{2,1,0:T(8,128)(2,1)S(1)} %get-tuple-element.102), channel_id=1, source_target_pairs={{0,15},{1,0},{2,1},{3,2},{4,3},{5,4},{6,5},{7,6},{8,7},{9,8},{10,9... | collective-permute-start | bytes 196616 | tf_op jit(solution)/shard_map/ppermute | solution.py:286
  14.2 24.0 %collective-permute-start.1 = (bf16[8,8,512]{2,1,0:T(8,128)(2,1)S(1)}, bf16[8,8,512]{2,1,0:T(8,128)(2,1)S(1)}, u32[]{:S(2)}, u32[]{:S(2)}) collective-permute-start(bf16[8,8,512]{2,1,0:T(8,128)(2,1)S(1)} %get-tuple-element.101), channel_id=1, source_target_pairs={{0,112},{16,0},{32,16},{48,32},{64,48},{80,64},{96,80},{112,96},{1... | collective-permute-start | bytes 196616 | tf_op jit(solution)/shard_map/ppermute | solution.py:284
  25.1 13.1 %collective-permute-start.2 = (bf16[8,8,512]{2,1,0:T(8,128)(2,1)S(1)}, bf16[8,8,512]{2,1,0:T(8,128)(2,1)S(1)}, u32[]{:S(2)}, u32[]{:S(2)}) collective-permute-start(bf16[8,8,512]{2,1,0:T(8,128)(2,1)S(1)} %get-tuple-element.100), channel_id=1, source_target_pairs={{0,127},{1,112},{2,113},{3,114},{4,115},{5,116},{6,117},{7,118},{8... | collective-permute-start | bytes 196616 | tf_op jit(solution)/shard_map/ppermute | solution.py:292
  30.2 30.0 %all-to-all-start = ((bf16[128,2,512]{2,1,0:T(2,128)(2,1)}), bf16[128,2,512]{2,1,0:T(2,128)(2,1)S(1)}, u32[]{:S(2)}, u32[]{:S(2)}) async-start(bf16[128,2,512]{2,1,0:T(2,128)(2,1)} %get-tuple-element.51), calls=%async_computation | async-start | bytes 524288 | tf_op jit(solution)/shard_map/all_to_all | solution.py:304
  37.5 85.5 %all-gather.4.cloned.1.call-start = ((), (), s32[]{:S(2)}) async-start(), calls=%async_computation.5 | async-start | bytes 1310720 | tf_op jit(solution)/shard_map/all_gather | solution.py:310
  38.2 0.6 copy-start.12
  38.2 0.6 copy-start.10
  38.8 0.6 copy-start.11
  48.8 9.1 %collective-permute-start.3 = (bf16[8,8,512]{2,1,0:T(8,128)(2,1)}, bf16[8,8,512]{2,1,0:T(8,128)(2,1)S(1)}, u32[]{:S(2)}, u32[]{:S(2)}) collective-permute-start(bf16[8,8,512]{2,1,0:T(8,128)(2,1)} %get-tuple-element.53), channel_id=1, source_target_pairs={{0,17},{1,18},{2,19},{3,20},{4,21},{5,22},{6,23},{7,24},{8,25},{9,... | collective-permute-start | bytes 196616 | tf_op jit(solution)/shard_map/ppermute | solution.py:292
  51.6 8.0 %collective-permute-start.4 = (bf16[8,8,512]{2,1,0:T(8,128)(2,1)}, bf16[8,8,512]{2,1,0:T(8,128)(2,1)S(1)}, u32[]{:S(2)}, u32[]{:S(2)}) collective-permute-start(bf16[8,8,512]{2,1,0:T(8,128)(2,1)} %get-tuple-element.54), channel_id=1, source_target_pairs={{0,16},{16,32},{32,48},{48,64},{64,80},{80,96},{96,112},{112,0},{1... | collective-permute-start | bytes 196616 | tf_op jit(solution)/shard_map/ppermute | solution.py:284
  55.1 5.1 %collective-permute-start.5 = (bf16[8,8,512]{2,1,0:T(8,128)(2,1)}, bf16[8,8,512]{2,1,0:T(8,128)(2,1)S(1)}, u32[]{:S(2)}, u32[]{:S(2)}) collective-permute-start(bf16[8,8,512]{2,1,0:T(8,128)(2,1)} %get-tuple-element.55), channel_id=1, source_target_pairs={{0,1},{1,2},{2,3},{3,4},{4,5},{5,6},{6,7},{7,8},{8,9},{9,10},{10,1... | collective-permute-start | bytes 196616 | tf_op jit(solution)/shard_map/ppermute | solution.py:286
  57.9 2.3 %copy-start.16 = (bf16[8,8,512]{2,1,0:T(8,128)(2,1)}, bf16[8,8,512]{2,1,0:T(8,128)(2,1)S(1)}, u32[]{:S(2)}) copy-start(bf16[8,8,512]{2,1,0:T(8,128)(2,1)S(1)} %collective-permute-done.3.att0) | copy-start | bytes 196612
  59.6 0.6 copy-start.17
  60.2 0.6 copy-start.18
  60.2 34.2 %copy-start.5 = (bf16[128,2,512]{2,1,0:T(2,128)(2,1)}, bf16[128,2,512]{2,1,0:T(2,128)(2,1)S(1)}, u32[]{:S(2)}) copy-start(bf16[128,2,512]{2,1,0:T(2,128)(2,1)S(1)} %all-to-all-done.grad) | copy-start | bytes 786436
  63.2 32.1 %collective-permute-start.6 = (bf16[2,1024,512]{2,1,0:T(8,128)(2,1)}, bf16[2,1024,512]{2,1,0:T(8,128)(2,1)S(1)}, u32[]{:S(2)}, u32[]{:S(2)}) collective-permute-start(bf16[2,1024,512]{2,1,0:T(8,128)(2,1)} %bitcast.32), channel_id=1, source_target_pairs={{0,1},{1,0},{2,3},{3,2},{4,5},{5,4},{6,7},{7,6},{8,9},{9,8},{10,11... | collective-permute-start | bytes 6291464 | tf_op jit(solution)/shard_map/ppermute | solution.py:314
  94.4 0.8 copy-start
  95.3 1.4 copy-start.9
  103.6 17.4 %collective-permute-start.8 = (bf16[256,512]{1,0:T(8,128)(2,1)}, bf16[256,512]{1,0:T(8,128)(2,1)S(1)}, u32[]{:S(2)}, u32[]{:S(2)}) collective-permute-start(bf16[256,512]{1,0:T(8,128)(2,1)} %get-tuple-element.70.grad0), channel_id=1, source_target_pairs={{0,2},{1,3},{2,0},{3,1},{4,6},{5,7},{6,4},{7,5},{8,10},{9,11},{10,... | collective-permute-start | bytes 786440 | tf_op jit(solution)/shard_map/ppermute | solution.py:314
  106.7 24.7 %all-to-all-start.2 = ((bf16[128,2,512]{2,1,0:T(2,128)(2,1)}), bf16[128,2,512]{2,1,0:T(2,128)(2,1)S(1)}, u32[]{:S(2)}, u32[]{:S(2)}) async-start(bf16[128,2,512]{2,1,0:T(2,128)(2,1)} %get-tuple-element.69), calls=%async_computation.2 | async-start | bytes 524288 | tf_op jit(solution)/shard_map/all_to_all | solution.py:304
  113.0 67.5 %reduce-scatter.2.cloned.1.call-start = ((), (), s32[]{:S(2)}) async-start(), calls=%async_computation.6 | async-start | bytes 1310720 | tf_op jit(solution)/shard_map/reduce_scatter | solution.py:414
  113.1 9.9 %collective-permute-start.7 = (bf16[256,512]{1,0:T(8,128)(2,1)}, bf16[256,512]{1,0:T(8,128)(2,1)S(1)}, u32[]{:S(2)}, u32[]{:S(2)}) collective-permute-start(bf16[256,512]{1,0:T(8,128)(2,1)} %get-tuple-element.70.grad0), channel_id=1, source_target_pairs={{0,1},{1,0},{2,3},{3,2},{4,5},{5,4},{6,7},{7,6},{8,9},{9,8},{10,11... | collective-permute-start | bytes 786440 | tf_op jit(solution)/shard_map/ppermute | solution.py:314
  121.1 3.4 %copy-start.2 = (bf16[256,512]{1,0:T(8,128)(2,1)}, bf16[256,512]{1,0:T(8,128)(2,1)S(1)}, u32[]{:S(2)}) copy-start(bf16[256,512]{1,0:T(8,128)(2,1)S(1)} %collective-permute-done.8.grad2) | copy-start | bytes 786436
  121.1 3.4 %collective-permute-start.9 = (bf16[256,512]{1,0:T(8,128)(2,1)S(1)}, bf16[256,512]{1,0:T(8,128)(2,1)S(1)}, u32[]{:S(2)}, u32[]{:S(2)}) collective-permute-start(bf16[256,512]{1,0:T(8,128)(2,1)S(1)} %collective-permute-done.8.grad2), channel_id=1, source_target_pairs={{0,1},{1,0},{2,3},{3,2},{4,5},{5,4},{6,7},{7,6},{8,9},{9,8},{10,11... | collective-permute-start | bytes 786440 | tf_op jit(solution)/shard_map/ppermute | solution.py:314
  123.0 1.5 copy-start.3
  124.5 0.7 copy-start.4
  131.4 0.7 copy-start.6
  134.5 18.6 %collective-permute-start.10 = (bf16[8,8,512]{2,1,0:T(8,128)(2,1)}, bf16[8,8,512]{2,1,0:T(8,128)(2,1)S(1)}, u32[]{:S(2)}, u32[]{:S(2)}) collective-permute-start(bf16[8,8,512]{2,1,0:T(8,128)(2,1)} %get-tuple-element.77), channel_id=1, source_target_pairs={{0,15},{1,0},{2,1},{3,2},{4,3},{5,4},{6,5},{7,6},{8,7},{9,8},{10,9... | collective-permute-start | bytes 196616 | tf_op jit(solution)/shard_map/ppermute | solution.py:286
  136.5 16.6 %collective-permute-start.11 = (bf16[8,8,512]{2,1,0:T(8,128)(2,1)}, bf16[8,8,512]{2,1,0:T(8,128)(2,1)S(1)}, u32[]{:S(2)}, u32[]{:S(2)}) collective-permute-start(bf16[8,8,512]{2,1,0:T(8,128)(2,1)} %get-tuple-element.78), channel_id=1, source_target_pairs={{0,112},{16,0},{32,16},{48,32},{64,48},{80,64},{96,80},{112,96},{1... | collective-permute-start | bytes 196616 | tf_op jit(solution)/shard_map/ppermute | solution.py:284
  140.9 12.2 %collective-permute-start.12 = (bf16[8,8,512]{2,1,0:T(8,128)(2,1)}, bf16[8,8,512]{2,1,0:T(8,128)(2,1)S(1)}, u32[]{:S(2)}, u32[]{:S(2)}) collective-permute-start(bf16[8,8,512]{2,1,0:T(8,128)(2,1)} %get-tuple-element.79), channel_id=1, source_target_pairs={{0,127},{1,112},{2,113},{3,114},{4,115},{5,116},{6,117},{7,118},{8... | collective-permute-start | bytes 196616 | tf_op jit(solution)/shard_map/ppermute | solution.py:292
  142.9 24.9 %all-to-all-start.3 = ((bf16[128,2,512]{2,1,0:T(2,128)(2,1)}), bf16[128,2,512]{2,1,0:T(2,128)(2,1)S(1)}, u32[]{:S(2)}, u32[]{:S(2)}) async-start(bf16[128,2,512]{2,1,0:T(2,128)(2,1)} %get-tuple-element.90), calls=%async_computation.3 | async-start | bytes 524288 | tf_op jit(solution)/shard_map/all_to_all | solution.py:304
  153.1 0.6 copy-start.13
  153.1 0.6 copy-start.14
  153.1 0.6 copy-start.15
  163.2 12.7 %copy-start.8 = (bf16[8,8,512]{2,1,0:T(8,128)(2,1)S(1)}, bf16[8,8,512]{2,1,0:T(8,128)(2,1)}, u32[]{:S(2)}) copy-start(bf16[8,8,512]{2,1,0:T(8,128)(2,1)} %get-tuple-element.96) | copy-start | bytes 196612
  167.8 5.7 %copy-start.7 = (bf16[128,2,512]{2,1,0:T(2,128)(2,1)}, bf16[128,2,512]{2,1,0:T(2,128)(2,1)S(1)}, u32[]{:S(2)}) copy-start(bf16[128,2,512]{2,1,0:T(2,128)(2,1)S(1)} %all-to-all-done.3.mixed) | copy-start | bytes 786436
  167.8 12.0 %copy-start.1 = (f32[256,512]{1,0:T(8,128)S(1)}, f32[256,512]{1,0:T(8,128)}, u32[]{:S(2)}) copy-start(f32[256,512]{1,0:T(8,128)} %get-tuple-element.92) | copy-start | bytes 1572868
  167.8 8.1 %collective-permute-start.15 = (bf16[8,8,512]{2,1,0:T(8,128)(2,1)}, bf16[8,8,512]{2,1,0:T(8,128)(2,1)S(1)}, u32[]{:S(2)}, u32[]{:S(2)}) collective-permute-start(bf16[8,8,512]{2,1,0:T(8,128)(2,1)} %get-tuple-element.95), channel_id=1, source_target_pairs={{0,1},{1,2},{2,3},{3,4},{4,5},{5,6},{6,7},{7,8},{8,9},{9,10},{10,1... | collective-permute-start | bytes 196616 | tf_op jit(solution)/shard_map/ppermute | solution.py:286
  167.9 8.4 %collective-permute-start.14 = (bf16[8,8,512]{2,1,0:T(8,128)(2,1)}, bf16[8,8,512]{2,1,0:T(8,128)(2,1)S(1)}, u32[]{:S(2)}, u32[]{:S(2)}) collective-permute-start(bf16[8,8,512]{2,1,0:T(8,128)(2,1)} %get-tuple-element.94), channel_id=1, source_target_pairs={{0,16},{16,32},{32,48},{48,64},{64,80},{80,96},{96,112},{112,0},{1... | collective-permute-start | bytes 196616 | tf_op jit(solution)/shard_map/ppermute | solution.py:284
  170.7 9.1 %collective-permute-start.13 = (bf16[8,8,512]{2,1,0:T(8,128)(2,1)}, bf16[8,8,512]{2,1,0:T(8,128)(2,1)S(1)}, u32[]{:S(2)}, u32[]{:S(2)}) collective-permute-start(bf16[8,8,512]{2,1,0:T(8,128)(2,1)} %get-tuple-element.93), channel_id=1, source_target_pairs={{0,17},{1,18},{2,19},{3,20},{4,21},{5,22},{6,23},{7,24},{8,25},{9,... | collective-permute-start | bytes 196616 | tf_op jit(solution)/shard_map/ppermute | solution.py:292
Sparse Core Ops, SparseCore 0:
  11.4 51.2 all-gather.5
Sparse Core Ops, SparseCore 1:
  95.3 24.1 all-gather.3
  131.5 22.9 reduce-scatter.1
where the time goes:
time: 191 us; the launch traced here: 190 us
  starting transfers between devices  70.2 us (37%)
  Pallas kernels  41.8 us (22%)
  blocking collectives  29.3 us (15%)
  waiting for transfers between devices  20.2 us (11%)
  between operations  15.8 us (8%)
  local copies, waits for them, and re-layouts  7.78 us (4%)
  other arithmetic  4.62 us (2%)
    all_to_all x1, blocking collectives, exchange(): lax.all_to_all(parts, ('row', 'col'), split_axis=0, concat_axis=0, tiled=...  29.3 us
    all_to_all x3, starting transfers between devices, exchange(): lax.all_to_all(parts, ('row', 'col'), split_axis=0, concat_axis=0, tiled=...  23.9 us
    ppermute x4, starting transfers between devices, send(): lax.ppermute(piece, 'row', [(i, (i + down) % rows) for i in range(rows)])  21.5 us
    ppermute x4, starting transfers between devices, send(): return lax.ppermute(piece, ('row', 'col'), route)  9.91 us
    pallas_call x1, Pallas kernels, shards(): call(attention_backward, [(quarter, BF16)] * 4, [pltpu.VMEM((width, CELLS...  9.39 us
    pallas_call x1, Pallas kernels, shards(): call(attention_forward, [(quarter, BF16)] * 4 + [((width, CELLS), BF16)]...  9.36 us
    ppermute x4, starting transfers between devices, swap(): lax.ppermute(piece, 'col', [(i, i ^ bit) for i in range(lax.axis_size('co...  8.76 us
    ppermute x4, waiting for transfers between devices, swap(): lax.ppermute(piece, 'col', [(i, i ^ bit) for i in range(lax.axis_size('co...  7.49 us
  transfers between devices with their start and end apart: 22, of which 8 were waited for; matrix products, arithmetic and copies ran while one was open for 1% of the time, Pallas kernels for 22%

commit v1 on v0

--- a/solution.py
+++ b/solution.py
@@ -11,14 +11,18 @@
 CELLS = WIN * WIN
 HEAD_W = 32
 EPS = 1e-05
-TURNS = 2
+TURNS = 8
 BF16 = jnp.bfloat16
 F32 = jnp.float32
-VMEM_BYTES = 56 * 1024 * 1024
+VMEM_BYTES = 24 * 1024 * 1024
 
 
 def dotg(a, b, ca, cb):
     return lax.dot_general(a, b, (((ca,), (cb,)), ((), ())), preferred_element_type=F32)
+
+
+def in_vmem(*arrays):
+    return [pltpu.with_memory_space_constraint(a, pltpu.VMEM) for a in arrays]
 
 
 def call(body, outs, scratch=(), smem=0, total=0, gflop=1.0):
@@ -200,6 +204,17 @@
     return jnp.sum(jnp.where((row & (WIN - 1)) == col, rows, 0.0), 1, keepdims=True)
 
 
+def both_in(out, first, second):
+    shape = (out.shape[0], out.shape[1] // 2, out.shape[2])
+    out[...] = jnp.concatenate([first.reshape(shape), second.reshape(shape)], 1)
+
+
+def one_of(both, which):
+    count = both.shape[1] // 2
+    part = both[:, which * count : (which + 1) * count, :]
+    return part.reshape(part.shape[0] * count, part.shape[2])
+
+
 def place_tokens(ids, gate, grad, place, packed, experts, cap):
     expert = column(ids[...].astype(F32)).astype(jnp.int32)
     matches = expert == lax.broadcasted_iota(jnp.int32, (CELLS, experts), 1)
@@ -213,28 +228,28 @@
     where_to = jnp.where(target == slots, 1.0, 0.0).astype(BF16)
     place[...] = where_to
     weighted = (grad[...].astype(F32) * column(gate[...])).astype(BF16)
-    packed[...] = dotg(where_to, weighted, 0, 0).astype(BF16).reshape(packed.shape)
-
-
-def pack_residual(att0, att1, att2, att3, img, gain, place, packed, att):
+    packed[...] = dotg(where_to, weighted, 0, 0).astype(BF16)
+
+
+def pack_residual(att0, att1, att2, att3, img, gain, place, grad_packed, packed, att):
     attention = assemble((att0[...], att1[...], att2[...], att3[...]))
     att[...] = attention.astype(BF16)
     unit, _ = normal(attention)
     routed = (img[...].astype(F32) + unit * gain[...]).astype(BF16)
-    packed[...] = dotg(place[...], routed, 0, 0).astype(BF16).reshape(packed.shape)
+    both_in(packed, dotg(place[...], routed, 0, 0).astype(BF16), grad_packed[...])
 
 
 def residual_grad(att, gain, place, grad, back, d_resid, d0, d1, d2, d3):
     unit, rstd = normal(att[...].astype(F32))
-    total = grad[...].astype(F32) + dotg(place[...], back[...].reshape(grad.shape), 1, 0)
+    total = grad[...].astype(F32) + dotg(place[...], one_of(back[...], 0), 1, 0)
     d_resid[...] = total
     store_parts(norm_grad(unit, rstd, total * gain[...]), (d0, d1, d2, d3))
 
 
-def finish_block(att, img, gain, place, gate, mixed, out):
+def finish_block(att, img, gain, place, gate, back, out):
     unit, _ = normal(att[...].astype(F32))
     residual = img[...].astype(F32) + unit * gain[...]
-    added = column(gate[...]) * dotg(place[...], mixed[...].reshape(img.shape), 1, 0)
+    added = column(gate[...]) * dotg(place[...], one_of(back[...], 1), 1, 0)
     out[...] = (residual + added).astype(BF16)
 
 
@@ -244,32 +259,40 @@
     return hidden * cdf, cdf + hidden * pdf
 
 
-def expert_rows(rows, grad, gain, near, far, mixed, d_expert, d_rows, slope):
-    half = near.shape[1] // 2
+def expert_hidden(sent, block0, block1, block2, block3, rows, act, slope):
+    here = one_of(sent[...], 0)
+    rows[...] = here
+    for s, ref in enumerate((block0, block1, block2, block3)):
+        value, grad = gelu_parts(dotg(here, ref[...], 1, 0))
+        act[s] = value.astype(BF16)
+        slope[s] = grad.astype(BF16)
+
+
+def expert_rows(sent, gain, act, slope, *refs):
+    w_in, w_out = refs[0:2] + refs[4:6], refs[2:4] + refs[6:8]
+    d_expert, back = refs[8:]
     flat = d_expert.shape
-    here = rows[...].reshape(flat)
-    blocks = [(ref, i) for ref in (near, far) for i in range(2)]
+    grad = one_of(sent[...], 1)
     total = jnp.zeros(flat, F32)
-    for s, (ref, i) in enumerate(blocks):
-        act, slope[s] = gelu_parts(dotg(here, ref[i, :half, :], 1, 0))
-        total = total + dotg(act.astype(BF16), ref[i, half:, :], 1, 0).astype(BF16).astype(F32)
+    for s, v in enumerate(w_out):
+        total = total + dotg(act[s], v[...], 1, 0).astype(BF16).astype(F32)
     unit, rstd = normal(total)
-    mixed[...] = (unit * gain[...]).astype(BF16).reshape(mixed.shape)
-    d_out = norm_grad(unit, rstd, grad[...].reshape(flat).astype(F32) * gain[...]).astype(BF16)
+    mixed = (unit * gain[...]).astype(BF16)
+    d_out = norm_grad(unit, rstd, grad.astype(F32) * gain[...]).astype(BF16)
     d_expert[...] = d_out
     total = jnp.zeros(flat, F32)
-    for s, (ref, i) in enumerate(blocks):
-        d_hidden = (dotg(d_out, ref[i, half:, :], 1, 1) * slope[s]).astype(BF16)
-        total = total + dotg(d_hidden, ref[i, :half, :], 1, 1).astype(BF16).astype(F32)
-    d_rows[...] = total.astype(BF16).reshape(d_rows.shape)
-
-
-def expert_grads(place, rows, grad0, grad1, grad2, grad3, w_in, w_out, both):
-    count, width = grad0.shape
+    for s, (w, v) in enumerate(zip(w_in, w_out, strict=True)):
+        d_hidden = (dotg(d_out, v[...], 1, 1) * slope[s].astype(F32)).astype(BF16)
+        total = total + dotg(d_hidden, w[...], 1, 1).astype(BF16).astype(F32)
+    both_in(back, total.astype(BF16), mixed)
+
+
+def expert_grads(*refs):
+    rows, grads, (w_in, w_out, both) = refs[:SPLIT], refs[SPLIT : 2 * SPLIT], refs[2 * SPLIT :]
     d_in = jnp.zeros(w_in.shape, F32)
     d_out = jnp.zeros(w_out.shape, F32)
-    for s, grad in enumerate((grad0, grad1, grad2, grad3)):
-        part = rows[pl.ds(pl.multiple_of((place[0] ^ s) * count, count), count), :]
+    for part, grad in zip(rows, grads, strict=True):
+        part = part[...]
         act, slope = gelu_parts(dotg(part, w_in[...], 1, 0))
         d_out = d_out + dotg(act.astype(BF16), grad[...], 0, 0)
         d_hidden = (dotg(grad[...], w_out[...], 1, 1) * slope).astype(BF16)
@@ -304,20 +327,14 @@
     return lax.all_to_all(parts, ("row", "col"), split_axis=0, concat_axis=0, tiled=True)
 
 
-def group_gather(rows):
-    cols = lax.axis_size("col")
-    groups = [[g + i for i in range(SPLIT)] for g in range(0, cols, SPLIT)]
-    return lax.all_gather(rows, "col", axis_index_groups=groups, axis=0, tiled=True)
-
-
 def swap(piece, bit):
     return lax.ppermute(piece, "col", [(i, i ^ bit) for i in range(lax.axis_size("col"))])
 
 
-def gather_blocks(blocks):
+def pair_gather(block):
     cols = lax.axis_size("col")
     groups = [[g + i, g + i + 2] for g in range(0, cols, SPLIT) for i in range(2)]
-    return lax.all_gather(blocks, "col", axis_index_groups=groups, axis=0, tiled=False)
+    return lax.all_gather(block, "col", axis_index_groups=groups, axis=0, tiled=False)
 
 
 def shards(
@@ -344,7 +361,7 @@
     tile = (WIN, WIN, width)
     quarter = (HALF, HALF, width)
     flat = (CELLS, width)
-    parts = (devices, slots // devices, width)
+    parts = (devices, 2 * slots // devices, width)
     tile_img = image_map[0]
     img = tile_img.reshape(flat)
     grad = grad_out[0].reshape(flat)
@@ -355,18 +372,11 @@
 
     pieces = (tile_img[:HALF, :HALF], tile_img[:HALF, HALF:], tile_img[HALF:, :HALF])
     _, beside, below, corner = to_window(*pieces, None)
-    place, grad_packed = call(
-        lambda *refs: place_tokens(*refs, experts=experts, cap=cap),
-        [((CELLS, slots), BF16), (parts, BF16)],
-        total=3,
-    )(ids, gate, grad)
-    grad_slots = exchange(grad_packed)
     first_w, second_w, _ = lax.optimization_barrier((w_in[0], w_out[0], pieces))
-    near = gather_blocks(jnp.concatenate([first_w, second_w], 0))
+    near = pair_gather(jnp.concatenate([first_w, second_w], 0))
     edge = jnp.stack(
         [lax.axis_index("row") == row_count - 1, lax.axis_index("col") == col_count - 1]
     ).astype(jnp.int32)
-    corner, _ = lax.optimization_barrier((corner, grad_packed))
     *attn_parts, qs, ku, vt, weights, aux, ho = call(
         attention_forward,
         [(quarter, BF16)] * 4
@@ -386,38 +396,49 @@
         smem=2,
         total=9,
         gflop=8.0,
-    )(edge, head_scale, tile_img, beside, below, corner, qkv_weight, proj_weight, bias_table)
+    )(edge, head_scale, tile_img, *in_vmem(beside, below, corner), qkv_weight, proj_weight, bias_table)
     att_parts = from_window(*attn_parts)
-    *att_parts, grad_slots = lax.optimization_barrier((*att_parts, grad_slots))
-    packed, att = call(pack_residual, [(parts, BF16), (flat, BF16)], total=7)(
-        *att_parts, img, a_gain, place
+    ids, *_ = lax.optimization_barrier((ids, *attn_parts))
+    place, grad_packed = call(
+        lambda *refs: place_tokens(*refs, experts=experts, cap=cap),
+        [((CELLS, slots), BF16), ((slots, width), BF16)],
+        total=3,
+        gflop=2.0,
+    )(ids, gate, grad)
+    packed, att = call(pack_residual, [(parts, BF16), (flat, BF16)], total=8)(
+        *in_vmem(*att_parts), img, a_gain, place, grad_packed
     )
     near, _ = lax.optimization_barrier((near, packed))
-    far = swap(near, 1)
-    rows = exchange(packed)
-    all_rows = group_gather(rows.reshape(flat))
-    mixed, d_expert, d_rows = call(
-        expert_rows,
-        [(parts, BF16), (flat, BF16), (parts, BF16)],
-        [pltpu.VMEM((SPLIT,) + flat, F32)],
+    depth = w_in.shape[1]
+    near = lax.optimization_barrier(
+        (near[0, :depth], near[1, :depth], near[0, depth:], near[1, depth:])
+    )
+    far = [swap(block, 1) for block in near]
+    sent = exchange(packed)
+    rows, act, slope = call(
+        expert_hidden,
+        [(flat, BF16), ((SPLIT,) + flat, BF16), ((SPLIT,) + flat, BF16)],
         total=5,
         gflop=2.0,
-    )(rows, grad_slots, e_gain, near, far)
-    back = exchange(d_rows)
+    )(sent, *near[:2], *far[:2])
+    next_rows = swap(rows, 2)
+    d_expert, back = call(expert_rows, [(flat, BF16), (parts, BF16)], total=12, gflop=2.0)(
+        sent, e_gain, act, slope, *near, *far
+    )
+    back, rows, next_rows = lax.optimization_barrier((back, rows, next_rows))
+    back = exchange(back)
     across = swap(d_expert, 2)
     grads = (d_expert, swap(d_expert, 1), across, swap(across, 1))
-    place_in_group = (lax.axis_index("col") % SPLIT).astype(jnp.int32).reshape(1)
+    all_rows = (rows, swap(rows, 1), next_rows, swap(next_rows, 1))
     (both,) = call(
-        expert_grads, [((w_in.shape[1], 2 * w_in.shape[2]), BF16)], smem=1, total=8, gflop=0.01
-    )(place_in_group, all_rows, *grads, w_in[0], w_out[0])
+        expert_grads, [((w_in.shape[1], 2 * w_in.shape[2]), BF16)], total=10, gflop=7.0
+    )(*all_rows, *grads, w_in[0], w_out[0])
     back, both = lax.optimization_barrier((back, both))
     both = lax.psum_scatter(both, "half", scatter_dimension=0, tiled=True).astype(F32)
     grad_w_in, grad_w_out = both[None, :, : w_in.shape[2]], both[None, :, w_in.shape[2] :]
     d_resid, *d_att = call(residual_grad, [(flat, F32)] + [(quarter, BF16)] * 4, total=5)(
-        att, a_gain, place, grad, back
-    )
-    mixed, *d_att = lax.optimization_barrier((mixed, *d_att))
-    mixed_back = exchange(mixed)
+        att, a_gain, place, grad, *in_vmem(back)
+    )
     d_rolled = call(
         attention_backward,
         [(quarter, BF16)] * 4,
@@ -425,10 +446,10 @@
         smem=1,
         total=13,
         gflop=8.0,
-    )(head_scale, *to_window(*d_att), qkv_weight, proj_weight, qs, ku, vt, weights, aux, ho)
-    *d_rolled, mixed_back = lax.optimization_barrier((*d_rolled, mixed_back))
+    )(head_scale, d_att[3], *in_vmem(*to_window(*d_att)[1:]), qkv_weight, proj_weight, qs, ku, vt, weights, aux, ho)
+    back, *_ = lax.optimization_barrier((back, *d_rolled))
     (block_out,) = call(finish_block, [(flat, BF16)], total=6)(
-        att, img, a_gain, place, gate, mixed_back
+        att, img, a_gain, place, gate, back
     )
     top_left, top_right, bottom_left, bottom_right = from_window(*d_rolled)
     returned = jnp.concatenate(

time: 191 us -> 165 us (0.86)
  blocking collectives: 29.3 us -> 0 us
  Pallas kernels: 41.8 us -> 28.4 us
  local copies, waits for them, and re-layouts: 7.78 us -> 15.6 us
  waiting for transfers between devices: 20.2 us -> 26.6 us
  starting transfers between devices: 70.2 us -> 74.5 us
    all_to_all x1 -> x0, blocking collectives: 29.3 us -> none  [exchange(): lax.all_to_all(parts, ('row', 'col'), split_axis=0, concat_axis=0, tiled=...]
    ppermute x4 -> x10, starting transfers between devices: 8.76 us -> 23.4 us  [swap(): lax.ppermute(piece, 'col', [(i, i ^ bit) for i in range(lax.axis_size('co...]
    ppermute x4, starting transfers between devices: 9.91 us -> 19.7 us  [send(): return lax.ppermute(piece, ('row', 'col'), route)]
    ppermute x4, starting transfers between devices: 21.5 us -> 11.8 us  [send(): lax.ppermute(piece, 'row', [(i, (i + down) % rows) for i in range(rows)])]
    all_to_all x3 -> x2, starting transfers between devices: 23.9 us -> 16.7 us  [exchange(): lax.all_to_all(parts, ('row', 'col'), split_axis=0, concat_axis=0, tiled=...]
    unnamed x38 -> x86, local copies, waits for them, and re-layouts: 5.25 us -> 12 us
    ppermute x4 -> x10, waiting for transfers between devices: 7.49 us -> 1.34 us  [swap(): lax.ppermute(piece, 'col', [(i, i ^ bit) for i in range(lax.axis_size('co...]
    ppermute x4, waiting for transfers between devices: 5.28 us -> 10.3 us  [send(): return lax.ppermute(piece, ('row', 'col'), route)]
  transfers between devices with their start and end apart: 22 -> 26, of which waited for: 8 -> 9; matrix products, arithmetic and copies ran while one was open for 1% -> 2% of each run, Pallas kernels for 22% -> 17%
where the time goes in v1:
time: 165 us; the launch traced here: 164 us
  starting transfers between devices  74.5 us (45%)
  Pallas kernels  28.4 us (17%)
  waiting for transfers between devices  26.6 us (16%)
  local copies, waits for them, and re-layouts  15.6 us (9%)
  between operations  14.7 us (9%)
  other arithmetic  4.15 us (3%)
    ppermute x10, starting transfers between devices, swap(): lax.ppermute(piece, 'col', [(i, i ^ bit) for i in range(lax.axis_size('co...  23.4 us
    ppermute x4, starting transfers between devices, send(): return lax.ppermute(piece, ('row', 'col'), route)  19.7 us
    all_to_all x2, starting transfers between devices, exchange(): lax.all_to_all(parts, ('row', 'col'), split_axis=0, concat_axis=0, tiled=...  16.7 us
    unnamed x86, local copies, waits for them, and re-layouts  12 us
    ppermute x4, starting transfers between devices, send(): lax.ppermute(piece, 'row', [(i, (i + down) % rows) for i in range(rows)])  11.8 us
    ppermute x4, waiting for transfers between devices, send(): return lax.ppermute(piece, ('row', 'col'), route)  10.3 us
    all_to_all x2, waiting for transfers between devices, exchange(): lax.all_to_all(parts, ('row', 'col'), split_axis=0, concat_axis=0, tiled=...  8.9 us
    ppermute x4, waiting for transfers between devices, send(): lax.ppermute(piece, 'row', [(i, (i + down) % rows) for i in range(rows)])  6.03 us
  transfers between devices with their start and end apart: 26, of which 9 were waited for; matrix products, arithmetic and copies ran while one was open for 2% of the time, Pallas kernels for 17%

profile of v1, /device:TPU:2, one launch (start us, length us, event | category | flops | bytes accessed | tf_op | source)
XLA Modules:
  0.0 164.1 jit_solution(1475381425830682035)
XLA Ops:
  7.3 1.1 fusion
  8.3 2.3 %pad_maximum_fusion = bf16[1024,512]{1,0:T(8,128)(2,1)} fusion(bf16[512,512]{1,0:T(8,128)(2,1)} %bitcast.31, bf16[512,512]{1,0:T(8,128)(2,1)} %bitcast.33), kind=kLoop, calls=%fused_computation | loop fusion | flops 2097152 | bytes 2097152 | tf_op jit(solution)/shard_map/concatenate | solution.py:376
  10.6 13.3 %collective-permute-start.2 = (bf16[8,8,512]{2,1,0:T(8,128)(2,1)S(1)}, bf16[8,8,512]{2,1,0:T(8,128)(2,1)S(1)}, u32[]{:S(2)}, u32[]{:S(2)}) collective-permute-start(bf16[8,8,512]{2,1,0:T(8,128)(2,1)S(1)} %get-tuple-element.94), channel_id=1, source_target_pairs={{0,127},{1,112},{2,113},{3,114},{4,115},{5,116},{6,117},{7,118},{8... | collective-permute-start | bytes 196616 | tf_op jit(solution)/shard_map/ppermute | solution.py:315
  23.9 2.5 %collective-permute-start.1 = (bf16[8,8,512]{2,1,0:T(8,128)(2,1)S(1)}, bf16[8,8,512]{2,1,0:T(8,128)(2,1)S(1)}, u32[]{:S(2)}, u32[]{:S(2)}) collective-permute-start(bf16[8,8,512]{2,1,0:T(8,128)(2,1)S(1)} %get-tuple-element.95), channel_id=1, source_target_pairs={{0,112},{16,0},{32,16},{48,32},{64,48},{80,64},{96,80},{112,96},{1... | collective-permute-start | bytes 196616 | tf_op jit(solution)/shard_map/ppermute | solution.py:307
  27.1 3.0 %collective-permute-done.1.below = bf16[8,8,512]{2,1,0:T(8,128)(2,1)S(1)} collective-permute-done((bf16[8,8,512]{2,1,0:T(8,128)(2,1)S(1)}, bf16[8,8,512]{2,1,0:T(8,128)(2,1)S(1)}, u32[]{:S(2)}, u32[]{:S(2)}) %collective-permute-start.1) | collective-permute-done | bytes 65568 | tf_op jit(solution)/shard_map/ppermute | solution.py:307
  30.1 5.6 %shard_map.147 = (bf16[8,8,512]{2,1,0:T(8,128)(2,1)S(1)}, bf16[8,8,512]{2,1,0:T(8,128)(2,1)S(1)}, bf16[8,8,512]{2,1,0:T(8,128)(2,1)S(1)}, bf16[8,8,512]{2,1,0:T(...) custom-call(s32[2]{0:T(128)S(1)} %add_convert_fusion.1.edge, ...), custom_call_target="tpu_custom_call" | custom-call | flops 8000000000 | bytes 1048576 | tf_op jit(solution)/shard_map/pallas_call | solution.py:380
  35.8 1.3 copy-done.31
  37.1 1.9 %collective-permute-start.3 = (bf16[8,8,512]{2,1,0:T(8,128)(2,1)S(1)}, bf16[8,8,512]{2,1,0:T(8,128)(2,1)S(1)}, u32[]{:S(2)}, u32[]{:S(2)}) collective-permute-start(bf16[8,8,512]{2,1,0:T(8,128)(2,1)S(1)} %get-tuple-element.46), channel_id=1, source_target_pairs={{0,17},{1,18},{2,19},{3,20},{4,21},{5,22},{6,23},{7,24},{8,25},{9,... | collective-permute-start | bytes 196616 | tf_op jit(solution)/shard_map/ppermute | solution.py:315
  39.1 2.2 %collective-permute-start.4 = (bf16[8,8,512]{2,1,0:T(8,128)(2,1)S(1)}, bf16[8,8,512]{2,1,0:T(8,128)(2,1)S(1)}, u32[]{:S(2)}, u32[]{:S(2)}) collective-permute-start(bf16[8,8,512]{2,1,0:T(8,128)(2,1)S(1)} %get-tuple-element.47), channel_id=1, source_target_pairs={{0,16},{16,32},{32,48},{48,64},{64,80},{80,96},{96,112},{112,0},{1... | collective-permute-start | bytes 196616 | tf_op jit(solution)/shard_map/ppermute | solution.py:307
  41.3 1.1 shard_map.148
  42.4 3.6 %collective-permute-done.3.att0 = bf16[8,8,512]{2,1,0:T(8,128)(2,1)S(1)} collective-permute-done((bf16[8,8,512]{2,1,0:T(8,128)(2,1)S(1)}, bf16[8,8,512]{2,1,0:T(8,128)(2,1)S(1)}, u32[]{:S(2)}, u32[]{:S(2)}) %collective-permute-start.3) | collective-permute-done | bytes 65568 | tf_op jit(solution)/shard_map/ppermute | solution.py:315
  46.7 1.6 shard_map.149
  49.1 9.8 %all-to-all-start = ((bf16[128,4,512]{2,1,0:T(4,128)(2,1)}), bf16[128,4,512]{2,1,0:T(4,128)(2,1)S(1)}, u32[]{:S(2)}, u32[]{:S(2)}) async-start(bf16[128,4,512]{2,1,0:T(4,128)(2,1)} %get-tuple-element.54), calls=%async_computation | async-start | bytes 1048576 | tf_op jit(solution)/shard_map/all_to_all | solution.py:327
  58.9 1.7 %slice_bitcast_fusion = (bf16[512,512]{1,0:T(8,128)(2,1)S(1)}, bf16[512,512]{1,0:T(8,128)(2,1)S(1)}, bf16[512,512]{1,0:T(8,128)(2,1)S(1)}, bf16[512,512]{1,0:T(8,128)(2,1)S(1)}) fusion(bf16[2,1024,512]{2,1,0:T(8,128)(2,1)} %bitcast.48), kind=kLoop, calls=%fused_computation.2 | loop fusion | bytes 4194304 | tf_op jit(solution)/shard_map/squeeze | solution.py:414
  60.6 2.1 %collective-permute-start.6 = (bf16[512,512]{1,0:T(8,128)(2,1)S(1)}, bf16[512,512]{1,0:T(8,128)(2,1)S(1)}, u32[]{:S(2)}, u32[]{:S(2)}) collective-permute-start(bf16[512,512]{1,0:T(8,128)(2,1)S(1)} %get-tuple-element.58.block0.refs_0_), channel_id=1, source_target_pairs={{0,1},{1,0},{2,3},{3,2},{4,5},{5,4},{6,7},{7,6},{8,9},{9,8},{10,11... | collective-permute-start | bytes 1572872 | tf_op jit(solution)/shard_map/ppermute | solution.py:331
  62.7 2.4 %collective-permute-start.7 = (bf16[512,512]{1,0:T(8,128)(2,1)S(1)}, bf16[512,512]{1,0:T(8,128)(2,1)}, u32[]{:S(2)}, u32[]{:S(2)}) collective-permute-start(bf16[512,512]{1,0:T(8,128)(2,1)S(1)} %get-tuple-element.59.block1.refs_1_), channel_id=1, source_target_pairs={{0,1},{1,0},{2,3},{3,2},{4,5},{5,4},{6,7},{7,6},{8,9},{9,8},{10,11... | collective-permute-start | bytes 1572872 | tf_op jit(solution)/shard_map/ppermute | solution.py:331
  65.1 1.9 %collective-permute-start.8 = (bf16[512,512]{1,0:T(8,128)(2,1)S(1)}, bf16[512,512]{1,0:T(8,128)(2,1)}, u32[]{:S(2)}, u32[]{:S(2)}) collective-permute-start(bf16[512,512]{1,0:T(8,128)(2,1)S(1)} %get-tuple-element.62.refs_2_), channel_id=1, source_target_pairs={{0,1},{1,0},{2,3},{3,2},{4,5},{5,4},{6,7},{7,6},{8,9},{9,8},{10,11... | collective-permute-start | bytes 1572872 | tf_op jit(solution)/shard_map/ppermute | solution.py:331
  67.0 2.4 %collective-permute-start.9 = (bf16[512,512]{1,0:T(8,128)(2,1)S(1)}, bf16[512,512]{1,0:T(8,128)(2,1)}, u32[]{:S(2)}, u32[]{:S(2)}) collective-permute-start(bf16[512,512]{1,0:T(8,128)(2,1)S(1)} %get-tuple-element.63.refs_3_), channel_id=1, source_target_pairs={{0,1},{1,0},{2,3},{3,2},{4,5},{5,4},{6,7},{7,6},{8,9},{9,8},{10,11... | collective-permute-start | bytes 1572872 | tf_op jit(solution)/shard_map/ppermute | solution.py:331
  69.4 8.8 %all-to-all-done.sent = bf16[128,4,512]{2,1,0:T(4,128)(2,1)S(1)} async-done(((bf16[128,4,512]{2,1,0:T(4,128)(2,1)}), bf16[128,4,512]{2,1,0:T(4,128)(2,1)S(1)}, u32[]{:S(2)}, u32[]{:S(2)}) %all-to-all-start) | async-done | bytes 524320 | tf_op jit(solution)/shard_map/all_to_all | solution.py:327
  78.2 2.4 %shard_map.150 = (bf16[256,512]{1,0:T(8,128)(2,1)S(1)}, bf16[4,256,512]{2,1,0:T(8,128)(2,1)S(1)}, bf16[4,256,512]{2,1,0:T(8,128)(2,1)S(1)}) custom-call(bf16[128,4,512]{2,1,0:T(4,128)(2,1)S(1)} %all-to-all-done.sent, bf16[512,512]{1,0:T(8,128)(2,1)S(1)} %get-tuple-element.58.block0.refs_0_, bf16[512,512]{1,0:T(8,128)(2,1)S(1)} %get-tuple-element.59.block1.refs_1_, ...), custom_call_target="tpu_custom_call" | custom-call | flops 2000000000 | bytes 1048576 | tf_op jit(solution)/shard_map/pallas_call | solution.py:418
  80.7 4.0 %collective-permute-start.10 = (bf16[256,512]{1,0:T(8,128)(2,1)S(1)}, bf16[256,512]{1,0:T(8,128)(2,1)S(1)}, u32[]{:S(2)}, u32[]{:S(2)}) collective-permute-start(bf16[256,512]{1,0:T(8,128)(2,1)S(1)} %get-tuple-element.67.refs_0_), channel_id=1, source_target_pairs={{0,2},{1,3},{2,0},{3,1},{4,6},{5,7},{6,4},{7,5},{8,10},{9,11},{10,... | collective-permute-start | bytes 786440 | tf_op jit(solution)/shard_map/ppermute | solution.py:331
  84.7 1.0 copy-done.3
  85.7 1.0 copy-done.10
  86.7 5.4 %shard_map.151 = (bf16[256,512]{1,0:T(8,128)(2,1)}, bf16[128,4,512]{2,1,0:T(4,128)(2,1)}) custom-call(bf16[128,4,512]{2,1,0:T(4,128)(2,1)S(1)} %all-to-all-done.sent, f32[1,512]{1,0:T(1,128)S(1)} %bitcast.44, bf16[4,256,512]{2,1,0:T(8,128)(2,1)S(1)} %get-tuple-element.60.act, bf16[4,256,512]{2,1,0:T(8,128)(2,1)S(1)} %get-tuple-element.61.slope, ...), custom_call_target="tpu_custom_call" | custom-call | flops 2000000000 | bytes 1048576 | tf_op jit(solution)/shard_map/pallas_call | solution.py:425
  92.1 1.9 %collective-permute-start.14 = (bf16[256,512]{1,0:T(8,128)(2,1)}, bf16[256,512]{1,0:T(8,128)(2,1)S(1)}, u32[]{:S(2)}, u32[]{:S(2)}) collective-permute-start(bf16[256,512]{1,0:T(8,128)(2,1)} %get-tuple-element.69.refs_4_), channel_id=1, source_target_pairs={{0,2},{1,3},{2,0},{3,1},{4,6},{5,7},{6,4},{7,5},{8,10},{9,11},{10,... | collective-permute-start | bytes 786440 | tf_op jit(solution)/shard_map/ppermute | solution.py:331
  94.7 6.8 %all-to-all-start.1 = ((bf16[128,4,512]{2,1,0:T(4,128)(2,1)}), bf16[128,4,512]{2,1,0:T(4,128)(2,1)S(1)}, u32[]{:S(2)}, u32[]{:S(2)}) async-start(bf16[128,4,512]{2,1,0:T(4,128)(2,1)} %get-tuple-element.66), calls=%async_computation.1 | async-start | bytes 1048576 | tf_op jit(solution)/shard_map/all_to_all | solution.py:327
  101.7 2.1 %collective-permute-start.13 = (bf16[256,512]{1,0:T(8,128)(2,1)}, bf16[256,512]{1,0:T(8,128)(2,1)S(1)}, u32[]{:S(2)}, u32[]{:S(2)}) collective-permute-start(bf16[256,512]{1,0:T(8,128)(2,1)} %get-tuple-element.69.refs_4_), channel_id=1, source_target_pairs={{0,1},{1,0},{2,3},{3,2},{4,5},{5,4},{6,7},{7,6},{8,9},{9,8},{10,11... | collective-permute-start | bytes 786440 | tf_op jit(solution)/shard_map/ppermute | solution.py:331
  103.7 2.4 %collective-permute-start.11 = (bf16[256,512]{1,0:T(8,128)(2,1)}, bf16[256,512]{1,0:T(8,128)(2,1)S(1)}, u32[]{:S(2)}, u32[]{:S(2)}) collective-permute-start(bf16[256,512]{1,0:T(8,128)(2,1)} %copy-done.13), channel_id=1, source_target_pairs={{0,1},{1,0},{2,3},{3,2},{4,5},{5,4},{6,7},{7,6},{8,9},{9,8},{10,11... | collective-permute-start | bytes 786440 | tf_op jit(solution)/shard_map/ppermute | solution.py:331
  106.1 1.9 %collective-permute-start.15 = (bf16[256,512]{1,0:T(8,128)(2,1)S(1)}, bf16[256,512]{1,0:T(8,128)(2,1)S(1)}, u32[]{:S(2)}, u32[]{:S(2)}) collective-permute-start(bf16[256,512]{1,0:T(8,128)(2,1)S(1)} %collective-permute-done.14.refs_6_), channel_id=1, source_target_pairs={{0,1},{1,0},{2,3},{3,2},{4,5},{5,4},{6,7},{7,6},{8,9},{9,8},{10,11... | collective-permute-start | bytes 786440 | tf_op jit(solution)/shard_map/ppermute | solution.py:331
  108.8 2.4 %collective-permute-start.12 = (bf16[256,512]{1,0:T(8,128)(2,1)}, bf16[256,512]{1,0:T(8,128)(2,1)S(1)}, u32[]{:S(2)}, u32[]{:S(2)}) collective-permute-start(bf16[256,512]{1,0:T(8,128)(2,1)} %copy-done.15), channel_id=1, source_target_pairs={{0,1},{1,0},{2,3},{3,2},{4,5},{5,4},{6,7},{7,6},{8,9},{9,8},{10,11... | collective-permute-start | bytes 786440 | tf_op jit(solution)/shard_map/ppermute | solution.py:331
  111.2 1.3 collective-permute-done.12.refs_3_
  112.5 0.9 copy-done.14
  113.5 0.9 copy-done.16
  114.4 0.9 copy-done.18
  115.4 5.3 %shard_map.152 = bf16[512,1024]{1,0:T(8,128)(2,1)} custom-call(bf16[256,512]{1,0:T(8,128)(2,1)S(1)} %copy-done.14, bf16[256,512]{1,0:T(8,128)(2,1)S(1)} %collective-permute-done.11.refs_1_, bf16[256,512]{1,0:T(8,128)(2,1)S(1)} %copy-done.16, bf16[256,512]{1,0:T(8,128)(2,1)S(1)} %collective-permute-done.12.refs_3_, ...), custom_call_target="tpu_custom_call" | custom-call | flops 7000000000 | bytes 1048576 | tf_op jit(solution)/shard_map/pallas_call | solution.py:433
  120.9 1.1 copy-done.26
  123.4 2.2 %collective-permute-start.16 = (bf16[8,8,512]{2,1,0:T(8,128)(2,1)S(1)}, bf16[8,8,512]{2,1,0:T(8,128)(2,1)S(1)}, u32[]{:S(2)}, u32[]{:S(2)}) collective-permute-start(bf16[8,8,512]{2,1,0:T(8,128)(2,1)S(1)} %get-tuple-element.72), channel_id=1, source_target_pairs={{0,15},{1,0},{2,1},{3,2},{4,3},{5,4},{6,5},{7,6},{8,7},{9,8},{10,9... | collective-permute-start | bytes 196616 | tf_op jit(solution)/shard_map/ppermute | solution.py:309
  125.6 5.3 %collective-permute-start.17 = (bf16[8,8,512]{2,1,0:T(8,128)(2,1)S(1)}, bf16[8,8,512]{2,1,0:T(8,128)(2,1)S(1)}, u32[]{:S(2)}, u32[]{:S(2)}) collective-permute-start(bf16[8,8,512]{2,1,0:T(8,128)(2,1)S(1)} %get-tuple-element.73), channel_id=1, source_target_pairs={{0,112},{16,0},{32,16},{48,32},{64,48},{80,64},{96,80},{112,96},{1... | collective-permute-start | bytes 196616 | tf_op jit(solution)/shard_map/ppermute | solution.py:307
  130.9 2.6 %collective-permute-start.18 = (bf16[8,8,512]{2,1,0:T(8,128)(2,1)S(1)}, bf16[8,8,512]{2,1,0:T(8,128)(2,1)S(1)}, u32[]{:S(2)}, u32[]{:S(2)}) collective-permute-start(bf16[8,8,512]{2,1,0:T(8,128)(2,1)S(1)} %get-tuple-element.74), channel_id=1, source_target_pairs={{0,127},{1,112},{2,113},{3,114},{4,115},{5,116},{6,117},{7,118},{8... | collective-permute-start | bytes 196616 | tf_op jit(solution)/shard_map/ppermute | solution.py:315
  133.5 3.0 %collective-permute-done.18.d3 = bf16[8,8,512]{2,1,0:T(8,128)(2,1)S(1)} collective-permute-done((bf16[8,8,512]{2,1,0:T(8,128)(2,1)S(1)}, bf16[8,8,512]{2,1,0:T(8,128)(2,1)S(1)}, u32[]{:S(2)}, u32[]{:S(2)}) %collective-permute-start.18) | collective-permute-done | bytes 65568 | tf_op jit(solution)/shard_map/ppermute | solution.py:315
  136.5 1.6 copy-done.32
  138.1 5.3 %shard_map.154 = (bf16[8,8,512]{2,1,0:T(8,128)(2,1)S(1)}, bf16[8,8,512]{2,1,0:T(8,128)(2,1)S(1)}, bf16[8,8,512]{2,1,0:T(8,128)(2,1)S(1)}, bf16[8,8,512]{2,1,0:T(8,128)(2,1)S(1)}) custom-call(f32[16]{0:T(128)S(1)} %copy-done.24, bf16[8,8,512]{2,1,0:T(8,128)(2,1)S(1)} %get-tuple-element.71.d0, bf16[8,8,512]{2,1,0:T(8,128)(2,1)S(1)} %collective-permute-done.16.d1, ...), custom_call_target="tpu_custom_call" | custom-call | flops 8000000000 | bytes 1048576 | tf_op jit(solution)/shard_map/pallas_call | solution.py:442
  143.5 1.9 %collective-permute-start.20 = (bf16[8,8,512]{2,1,0:T(8,128)(2,1)S(1)}, bf16[8,8,512]{2,1,0:T(8,128)(2,1)S(1)}, u32[]{:S(2)}, u32[]{:S(2)}) collective-permute-start(bf16[8,8,512]{2,1,0:T(8,128)(2,1)S(1)} %get-tuple-element.83), channel_id=1, source_target_pairs={{0,16},{16,32},{32,48},{48,64},{64,80},{80,96},{96,112},{112,0},{1... | collective-permute-start | bytes 196616 | tf_op jit(solution)/shard_map/ppermute | solution.py:307
  145.4 1.9 %collective-permute-start.19 = (bf16[8,8,512]{2,1,0:T(8,128)(2,1)S(1)}, bf16[8,8,512]{2,1,0:T(8,128)(2,1)S(1)}, u32[]{:S(2)}, u32[]{:S(2)}) collective-permute-start(bf16[8,8,512]{2,1,0:T(8,128)(2,1)S(1)} %get-tuple-element.84), channel_id=1, source_target_pairs={{0,17},{1,18},{2,19},{3,20},{4,21},{5,22},{6,23},{7,24},{8,25},{9,... | collective-permute-start | bytes 196616 | tf_op jit(solution)/shard_map/ppermute | solution.py:315
  147.4 1.1 shard_map.155
  148.5 2.3 %collective-permute-done.20 = bf16[8,8,512]{2,1,0:T(8,128)(2,1)S(1)} collective-permute-done((bf16[8,8,512]{2,1,0:T(8,128)(2,1)S(1)}, bf16[8,8,512]{2,1,0:T(8,128)(2,1)S(1)}, u32[]{:S(2)}, u32[]{:S(2)}) %collective-permute-start.20) | collective-permute-done | bytes 65568 | tf_op jit(solution)/shard_map/ppermute | solution.py:307
  150.9 3.7 %collective-permute-done.19 = bf16[8,8,512]{2,1,0:T(8,128)(2,1)S(1)} collective-permute-done((bf16[8,8,512]{2,1,0:T(8,128)(2,1)S(1)}, bf16[8,8,512]{2,1,0:T(8,128)(2,1)S(1)}, u32[]{:S(2)}, u32[]{:S(2)}) %collective-permute-start.19) | collective-permute-done | bytes 65568 | tf_op jit(solution)/shard_map/ppermute | solution.py:315
  155.4 1.0 convert_element_type.29
  (110 shorter events, 6.9 us)
Async XLA Ops:
  7.2 22.9 %copy-start.4 = (bf16[1,16,16,512]{3,2,1,0:T(8,128)(2,1)S(1)}, bf16[1,16,16,512]{3,2,1,0:T(8,128)(2,1)}, u32[]{:S(2)}) copy-start(bf16[1,16,16,512]{3,2,1,0:T(8,128)(2,1)} %param.12) | copy-start | bytes 786436
  7.2 22.9 %copy-start.24 = (f32[16]{0:T(128)S(1)}, f32[16]{0:T(128)}, u32[]{:S(2)}) copy-start(f32[16]{0:T(128)} %scale.3) | copy-start | bytes 196
  7.2 22.9 %copy-start.7 = (bf16[512,512]{1,0:T(8,128)(2,1)S(1)}, bf16[512,512]{1,0:T(8,128)(2,1)}, u32[]{:S(2)}) copy-start(bf16[512,512]{1,0:T(8,128)(2,1)} %proj.3) | copy-start | bytes 1572868
  7.2 22.9 %copy-start.5 = (bf16[512,1536]{1,0:T(8,128)(2,1)S(1)}, bf16[512,1536]{1,0:T(8,128)(2,1)}, u32[]{:S(2)}) copy-start(bf16[512,1536]{1,0:T(8,128)(2,1)} %wqkv.3) | copy-start | bytes 4718596
  7.2 22.9 %copy-start.19 = (f32[16,961]{1,0:T(8,128)S(1)}, f32[16,961]{1,0:T(8,128)}, u32[]{:S(2)}) copy-start(f32[16,961]{1,0:T(8,128)} %table.1) | copy-start | bytes 184516
  7.2 51.7 %all-gather.3.cloned.1.call-start = ((), (), s32[]{:S(2)}) async-start(), calls=%async_computation.4 | async-start | bytes 3145728 | tf_op jit(solution)/shard_map/all_gather | solution.py:337
  10.6 16.4 %collective-permute-start.2 = (bf16[8,8,512]{2,1,0:T(8,128)(2,1)S(1)}, bf16[8,8,512]{2,1,0:T(8,128)(2,1)S(1)}, u32[]{:S(2)}, u32[]{:S(2)}) collective-permute-start(bf16[8,8,512]{2,1,0:T(8,128)(2,1)S(1)} %get-tuple-element.94), channel_id=1, source_target_pairs={{0,127},{1,112},{2,113},{3,114},{4,115},{5,116},{6,117},{7,118},{8... | collective-permute-start | bytes 196616 | tf_op jit(solution)/shard_map/ppermute | solution.py:315
  23.9 6.2 %collective-permute-start.1 = (bf16[8,8,512]{2,1,0:T(8,128)(2,1)S(1)}, bf16[8,8,512]{2,1,0:T(8,128)(2,1)S(1)}, u32[]{:S(2)}, u32[]{:S(2)}) collective-permute-start(bf16[8,8,512]{2,1,0:T(8,128)(2,1)S(1)} %get-tuple-element.95), channel_id=1, source_target_pairs={{0,112},{16,0},{32,16},{48,32},{64,48},{80,64},{96,80},{112,96},{1... | collective-permute-start | bytes 196616 | tf_op jit(solution)/shard_map/ppermute | solution.py:307
  26.4 3.7 %collective-permute-start = (bf16[8,8,512]{2,1,0:T(8,128)(2,1)S(1)}, bf16[8,8,512]{2,1,0:T(8,128)(2,1)S(1)}, u32[]{:S(2)}, u32[]{:S(2)}) collective-permute-start(bf16[8,8,512]{2,1,0:T(8,128)(2,1)S(1)} %get-tuple-element.96), channel_id=1, source_target_pairs={{0,15},{1,0},{2,1},{3,2},{4,3},{5,4},{6,5},{7,6},{8,7},{9,8},{10,9... | collective-permute-start | bytes 196616 | tf_op jit(solution)/shard_map/ppermute | solution.py:309
  27.1 14.2 %copy-start.11 = (bf16[1,16,16,512]{3,2,1,0:T(8,128)(2,1)S(1)}, bf16[1,16,16,512]{3,2,1,0:T(8,128)(2,1)}, u32[]{:S(2)}) copy-start(bf16[1,16,16,512]{3,2,1,0:T(8,128)(2,1)} %param.23) | copy-start | bytes 786436
  27.1 14.2 %copy-start.20 = (s32[1,16,16,1]{2,3,1,0:T(1,128)S(1)}, s32[1,16,16,1]{2,3,1,0:T(1,128)}, u32[]{:S(2)}) copy-start(s32[1,16,16,1]{2,3,1,0:T(1,128)} %param.18) | copy-start | bytes 3076
  27.1 14.2 %copy-start.21 = (f32[1,16,16]{2,1,0:T(8,128)S(1)}, f32[1,16,16]{2,1,0:T(8,128)}, u32[]{:S(2)}) copy-start(f32[1,16,16]{2,1,0:T(8,128)} %param.19) | copy-start | bytes 3076
  37.1 8.9 %collective-permute-start.3 = (bf16[8,8,512]{2,1,0:T(8,128)(2,1)S(1)}, bf16[8,8,512]{2,1,0:T(8,128)(2,1)S(1)}, u32[]{:S(2)}, u32[]{:S(2)}) collective-permute-start(bf16[8,8,512]{2,1,0:T(8,128)(2,1)S(1)} %get-tuple-element.46), channel_id=1, source_target_pairs={{0,17},{1,18},{2,19},{3,20},{4,21},{5,22},{6,23},{7,24},{8,25},{9,... | collective-permute-start | bytes 196616 | tf_op jit(solution)/shard_map/ppermute | solution.py:315
  39.1 7.7 %collective-permute-start.4 = (bf16[8,8,512]{2,1,0:T(8,128)(2,1)S(1)}, bf16[8,8,512]{2,1,0:T(8,128)(2,1)S(1)}, u32[]{:S(2)}, u32[]{:S(2)}) collective-permute-start(bf16[8,8,512]{2,1,0:T(8,128)(2,1)S(1)} %get-tuple-element.47), channel_id=1, source_target_pairs={{0,16},{16,32},{32,48},{48,64},{64,80},{80,96},{96,112},{112,0},{1... | collective-permute-start | bytes 196616 | tf_op jit(solution)/shard_map/ppermute | solution.py:307
  41.2 5.5 %collective-permute-start.5 = (bf16[8,8,512]{2,1,0:T(8,128)(2,1)S(1)}, bf16[8,8,512]{2,1,0:T(8,128)(2,1)S(1)}, u32[]{:S(2)}, u32[]{:S(2)}) collective-permute-start(bf16[8,8,512]{2,1,0:T(8,128)(2,1)S(1)} %get-tuple-element.48), channel_id=1, source_target_pairs={{0,1},{1,2},{2,3},{3,4},{4,5},{5,6},{6,7},{7,8},{8,9},{9,10},{10,1... | collective-permute-start | bytes 196616 | tf_op jit(solution)/shard_map/ppermute | solution.py:309
  49.1 29.1 %all-to-all-start = ((bf16[128,4,512]{2,1,0:T(4,128)(2,1)}), bf16[128,4,512]{2,1,0:T(4,128)(2,1)S(1)}, u32[]{:S(2)}, u32[]{:S(2)}) async-start(bf16[128,4,512]{2,1,0:T(4,128)(2,1)} %get-tuple-element.54), calls=%async_computation | async-start | bytes 1048576 | tf_op jit(solution)/shard_map/all_to_all | solution.py:327
  60.6 20.0 %copy-start.2 = (bf16[512,512]{1,0:T(8,128)(2,1)}, bf16[512,512]{1,0:T(8,128)(2,1)S(1)}, u32[]{:S(2)}) copy-start(bf16[512,512]{1,0:T(8,128)(2,1)S(1)} %get-tuple-element.58.block0.refs_0_) | copy-start | bytes 1572868
  60.6 24.0 %copy-start.22 = (f32[512]{0:T(512)S(1)}, f32[512]{0:T(512)}, u32[]{:S(2)}) copy-start(f32[512]{0:T(512)} %param.22) | copy-start | bytes 6148
  60.6 17.6 %collective-permute-start.6 = (bf16[512,512]{1,0:T(8,128)(2,1)S(1)}, bf16[512,512]{1,0:T(8,128)(2,1)S(1)}, u32[]{:S(2)}, u32[]{:S(2)}) collective-permute-start(bf16[512,512]{1,0:T(8,128)(2,1)S(1)} %get-tuple-element.58.block0.refs_0_), channel_id=1, source_target_pairs={{0,1},{1,0},{2,3},{3,2},{4,5},{5,4},{6,7},{7,6},{8,9},{9,8},{10,11... | collective-permute-start | bytes 1572872 | tf_op jit(solution)/shard_map/ppermute | solution.py:331
  62.7 15.5 %collective-permute-start.7 = (bf16[512,512]{1,0:T(8,128)(2,1)S(1)}, bf16[512,512]{1,0:T(8,128)(2,1)}, u32[]{:S(2)}, u32[]{:S(2)}) collective-permute-start(bf16[512,512]{1,0:T(8,128)(2,1)S(1)} %get-tuple-element.59.block1.refs_1_), channel_id=1, source_target_pairs={{0,1},{1,0},{2,3},{3,2},{4,5},{5,4},{6,7},{7,6},{8,9},{9,8},{10,11... | collective-permute-start | bytes 1572872 | tf_op jit(solution)/shard_map/ppermute | solution.py:331
  65.1 19.5 %collective-permute-start.8 = (bf16[512,512]{1,0:T(8,128)(2,1)S(1)}, bf16[512,512]{1,0:T(8,128)(2,1)}, u32[]{:S(2)}, u32[]{:S(2)}) collective-permute-start(bf16[512,512]{1,0:T(8,128)(2,1)S(1)} %get-tuple-element.62.refs_2_), channel_id=1, source_target_pairs={{0,1},{1,0},{2,3},{3,2},{4,5},{5,4},{6,7},{7,6},{8,9},{9,8},{10,11... | collective-permute-start | bytes 1572872 | tf_op jit(solution)/shard_map/ppermute | solution.py:331
  67.0 17.6 %collective-permute-start.9 = (bf16[512,512]{1,0:T(8,128)(2,1)S(1)}, bf16[512,512]{1,0:T(8,128)(2,1)}, u32[]{:S(2)}, u32[]{:S(2)}) collective-permute-start(bf16[512,512]{1,0:T(8,128)(2,1)S(1)} %get-tuple-element.63.refs_3_), channel_id=1, source_target_pairs={{0,1},{1,0},{2,3},{3,2},{4,5},{5,4},{6,7},{7,6},{8,9},{9,8},{10,11... | collective-permute-start | bytes 1572872 | tf_op jit(solution)/shard_map/ppermute | solution.py:331
  80.6 11.5 %copy-start.13 = (bf16[256,512]{1,0:T(8,128)(2,1)}, bf16[256,512]{1,0:T(8,128)(2,1)S(1)}, u32[]{:S(2)}) copy-start(bf16[256,512]{1,0:T(8,128)(2,1)S(1)} %get-tuple-element.67.refs_0_) | copy-start | bytes 786436
  80.7 13.4 %collective-permute-start.10 = (bf16[256,512]{1,0:T(8,128)(2,1)S(1)}, bf16[256,512]{1,0:T(8,128)(2,1)S(1)}, u32[]{:S(2)}, u32[]{:S(2)}) collective-permute-start(bf16[256,512]{1,0:T(8,128)(2,1)S(1)} %get-tuple-element.67.refs_0_), channel_id=1, source_target_pairs={{0,2},{1,3},{2,0},{3,1},{4,6},{5,7},{6,4},{7,5},{8,10},{9,11},{10,... | collective-permute-start | bytes 786440 | tf_op jit(solution)/shard_map/ppermute | solution.py:331
  86.7 25.8 %copy-start = (bf16[1,512,512]{2,1,0:T(8,128)(2,1)S(1)}, bf16[1,512,512]{2,1,0:T(8,128)(2,1)}, u32[]{:S(2)}) copy-start(bf16[1,512,512]{2,1,0:T(8,128)(2,1)} %param.21) | copy-start | bytes 1572868
  86.7 25.8 %copy-start.1 = (bf16[1,512,512]{2,1,0:T(8,128)(2,1)S(1)}, bf16[1,512,512]{2,1,0:T(8,128)(2,1)}, u32[]{:S(2)}) copy-start(bf16[1,512,512]{2,1,0:T(8,128)(2,1)} %param.20) | copy-start | bytes 1572868
  92.1 14.0 %collective-permute-start.14 = (bf16[256,512]{1,0:T(8,128)(2,1)}, bf16[256,512]{1,0:T(8,128)(2,1)S(1)}, u32[]{:S(2)}, u32[]{:S(2)}) collective-permute-start(bf16[256,512]{1,0:T(8,128)(2,1)} %get-tuple-element.69.refs_4_), channel_id=1, source_target_pairs={{0,2},{1,3},{2,0},{3,1},{4,6},{5,7},{6,4},{7,5},{8,10},{9,11},{10,... | collective-permute-start | bytes 786440 | tf_op jit(solution)/shard_map/ppermute | solution.py:331
  94.7 26.1 %all-to-all-start.1 = ((bf16[128,4,512]{2,1,0:T(4,128)(2,1)}), bf16[128,4,512]{2,1,0:T(4,128)(2,1)S(1)}, u32[]{:S(2)}, u32[]{:S(2)}) async-start(bf16[128,4,512]{2,1,0:T(4,128)(2,1)} %get-tuple-element.66), calls=%async_computation.1 | async-start | bytes 1048576 | tf_op jit(solution)/shard_map/all_to_all | solution.py:327
  101.6 19.3 %copy-start.12 = (bf16[1,16,16,512]{3,2,1,0:T(8,128)(2,1)S(1)}, bf16[1,16,16,512]{3,2,1,0:T(8,128)(2,1)}, u32[]{:S(2)}) copy-start(bf16[1,16,16,512]{3,2,1,0:T(8,128)(2,1)} %param.23) | copy-start | bytes 786436
  101.6 53.8 %reduce-scatter.2.cloned.1.call-start = ((), (), s32[]{:S(2)}) async-start(), calls=%async_computation.3 | async-start | bytes 1310720 | tf_op jit(solution)/shard_map/reduce_scatter | solution.py:437
  101.7 9.5 %collective-permute-start.13 = (bf16[256,512]{1,0:T(8,128)(2,1)}, bf16[256,512]{1,0:T(8,128)(2,1)S(1)}, u32[]{:S(2)}, u32[]{:S(2)}) collective-permute-start(bf16[256,512]{1,0:T(8,128)(2,1)} %get-tuple-element.69.refs_4_), channel_id=1, source_target_pairs={{0,1},{1,0},{2,3},{3,2},{4,5},{5,4},{6,7},{7,6},{8,9},{9,8},{10,11... | collective-permute-start | bytes 786440 | tf_op jit(solution)/shard_map/ppermute | solution.py:331
  103.7 7.5 %collective-permute-start.11 = (bf16[256,512]{1,0:T(8,128)(2,1)}, bf16[256,512]{1,0:T(8,128)(2,1)S(1)}, u32[]{:S(2)}, u32[]{:S(2)}) collective-permute-start(bf16[256,512]{1,0:T(8,128)(2,1)} %copy-done.13), channel_id=1, source_target_pairs={{0,1},{1,0},{2,3},{3,2},{4,5},{5,4},{6,7},{7,6},{8,9},{9,8},{10,11... | collective-permute-start | bytes 786440 | tf_op jit(solution)/shard_map/ppermute | solution.py:331
  106.1 5.1 %collective-permute-start.15 = (bf16[256,512]{1,0:T(8,128)(2,1)S(1)}, bf16[256,512]{1,0:T(8,128)(2,1)S(1)}, u32[]{:S(2)}, u32[]{:S(2)}) collective-permute-start(bf16[256,512]{1,0:T(8,128)(2,1)S(1)} %collective-permute-done.14.refs_6_), channel_id=1, source_target_pairs={{0,1},{1,0},{2,3},{3,2},{4,5},{5,4},{6,7},{7,6},{8,9},{9,8},{10,11... | collective-permute-start | bytes 786440 | tf_op jit(solution)/shard_map/ppermute | solution.py:331
  108.8 3.8 %collective-permute-start.12 = (bf16[256,512]{1,0:T(8,128)(2,1)}, bf16[256,512]{1,0:T(8,128)(2,1)S(1)}, u32[]{:S(2)}, u32[]{:S(2)}) collective-permute-start(bf16[256,512]{1,0:T(8,128)(2,1)} %copy-done.15), channel_id=1, source_target_pairs={{0,1},{1,0},{2,3},{3,2},{4,5},{5,4},{6,7},{7,6},{8,9},{9,8},{10,11... | collective-permute-start | bytes 786440 | tf_op jit(solution)/shard_map/ppermute | solution.py:331
  120.9 15.6 %copy-start.6 = (bf16[512,1536]{1,0:T(8,128)(2,1)S(1)}, bf16[512,1536]{1,0:T(8,128)(2,1)}, u32[]{:S(2)}) copy-start(bf16[512,1536]{1,0:T(8,128)(2,1)} %wqkv.3) | copy-start | bytes 4718596
  120.9 15.6 %copy-start.8 = (bf16[512,512]{1,0:T(8,128)(2,1)S(1)}, bf16[512,512]{1,0:T(8,128)(2,1)}, u32[]{:S(2)}) copy-start(bf16[512,512]{1,0:T(8,128)(2,1)} %proj.3) | copy-start | bytes 1572868
  122.9 13.6 %copy-start.34 = (bf16[512,256]{1,0:T(8,128)(2,1)S(1)}, bf16[512,256]{1,0:T(8,128)(2,1)}, u32[]{:S(2)}) copy-start(bf16[512,256]{1,0:T(8,128)(2,1)} %copy-done.33) | copy-start | bytes 786436
  122.9 13.6 %copy-start.36 = (bf16[512,256]{1,0:T(8,128)(2,1)S(1)}, bf16[512,256]{1,0:T(8,128)(2,1)}, u32[]{:S(2)}) copy-start(bf16[512,256]{1,0:T(8,128)(2,1)} %copy-done.35) | copy-start | bytes 786436
  122.9 13.6 %copy-start.38 = (bf16[512,256]{1,0:T(8,128)(2,1)S(1)}, bf16[512,256]{1,0:T(8,128)(2,1)}, u32[]{:S(2)}) copy-start(bf16[512,256]{1,0:T(8,128)(2,1)} %copy-done.37) | copy-start | bytes 786436
  122.9 13.6 %copy-start.40 = (bf16[512,256]{1,0:T(8,128)(2,1)S(1)}, bf16[512,256]{1,0:T(8,128)(2,1)}, u32[]{:S(2)}) copy-start(bf16[512,256]{1,0:T(8,128)(2,1)} %copy-done.39) | copy-start | bytes 786436
  122.9 13.6 %copy-start.42 = (f32[16,8,256]{2,1,0:T(8,128)S(1)}, f32[16,8,256]{2,1,0:T(8,128)}, u32[]{:S(2)}) copy-start(f32[16,8,256]{2,1,0:T(8,128)} %copy-done.41) | copy-start | bytes 393220
  123.4 10.1 %collective-permute-start.16 = (bf16[8,8,512]{2,1,0:T(8,128)(2,1)S(1)}, bf16[8,8,512]{2,1,0:T(8,128)(2,1)S(1)}, u32[]{:S(2)}, u32[]{:S(2)}) collective-permute-start(bf16[8,8,512]{2,1,0:T(8,128)(2,1)S(1)} %get-tuple-element.72), channel_id=1, source_target_pairs={{0,15},{1,0},{2,1},{3,2},{4,3},{5,4},{6,5},{7,6},{8,7},{9,8},{10,9... | collective-permute-start | bytes 196616 | tf_op jit(solution)/shard_map/ppermute | solution.py:309
  125.6 7.9 %collective-permute-start.17 = (bf16[8,8,512]{2,1,0:T(8,128)(2,1)S(1)}, bf16[8,8,512]{2,1,0:T(8,128)(2,1)S(1)}, u32[]{:S(2)}, u32[]{:S(2)}) collective-permute-start(bf16[8,8,512]{2,1,0:T(8,128)(2,1)S(1)} %get-tuple-element.73), channel_id=1, source_target_pairs={{0,112},{16,0},{32,16},{48,32},{64,48},{80,64},{96,80},{112,96},{1... | collective-permute-start | bytes 196616 | tf_op jit(solution)/shard_map/ppermute | solution.py:307
  130.9 5.6 %collective-permute-start.18 = (bf16[8,8,512]{2,1,0:T(8,128)(2,1)S(1)}, bf16[8,8,512]{2,1,0:T(8,128)(2,1)S(1)}, u32[]{:S(2)}, u32[]{:S(2)}) collective-permute-start(bf16[8,8,512]{2,1,0:T(8,128)(2,1)S(1)} %get-tuple-element.74), channel_id=1, source_target_pairs={{0,127},{1,112},{2,113},{3,114},{4,115},{5,116},{6,117},{7,118},{8... | collective-permute-start | bytes 196616 | tf_op jit(solution)/shard_map/ppermute | solution.py:315
  138.1 9.2 %copy-start.30 = (bf16[256,256]{1,0:T(8,128)(2,1)S(1)}, bf16[256,256]{1,0:T(8,128)(2,1)}, u32[]{:S(2)}) copy-start(bf16[256,256]{1,0:T(8,128)(2,1)} %copy-done.28) | copy-start | bytes 393220
  143.5 5.1 %collective-permute-start.21 = (bf16[8,8,512]{2,1,0:T(8,128)(2,1)S(1)}, bf16[8,8,512]{2,1,0:T(8,128)(2,1)S(1)}, u32[]{:S(2)}, u32[]{:S(2)}) collective-permute-start(bf16[8,8,512]{2,1,0:T(8,128)(2,1)S(1)} %get-tuple-element.82), channel_id=1, source_target_pairs={{0,1},{1,2},{2,3},{3,4},{4,5},{5,6},{6,7},{7,8},{8,9},{9,10},{10,1... | collective-permute-start | bytes 196616 | tf_op jit(solution)/shard_map/ppermute | solution.py:309
  143.5 7.4 %collective-permute-start.20 = (bf16[8,8,512]{2,1,0:T(8,128)(2,1)S(1)}, bf16[8,8,512]{2,1,0:T(8,128)(2,1)S(1)}, u32[]{:S(2)}, u32[]{:S(2)}) collective-permute-start(bf16[8,8,512]{2,1,0:T(8,128)(2,1)S(1)} %get-tuple-element.83), channel_id=1, source_target_pairs={{0,16},{16,32},{32,48},{48,64},{64,80},{80,96},{96,112},{112,0},{1... | collective-permute-start | bytes 196616 | tf_op jit(solution)/shard_map/ppermute | solution.py:307
  145.4 9.2 %collective-permute-start.19 = (bf16[8,8,512]{2,1,0:T(8,128)(2,1)S(1)}, bf16[8,8,512]{2,1,0:T(8,128)(2,1)S(1)}, u32[]{:S(2)}, u32[]{:S(2)}) collective-permute-start(bf16[8,8,512]{2,1,0:T(8,128)(2,1)S(1)} %get-tuple-element.84), channel_id=1, source_target_pairs={{0,17},{1,18},{2,19},{3,20},{4,21},{5,22},{6,23},{7,24},{8,25},{9,... | collective-permute-start | bytes 196616 | tf_op jit(solution)/shard_map/ppermute | solution.py:315
  (21 other events, 61.5 us)
Sparse Core Ops, SparseCore 0:
  10.8 45.6 all-gather.2
  121.0 27.4 reduce-scatter.1

commit v2 on v1

--- a/solution.py
+++ b/solution.py
@@ -25,12 +25,18 @@
     return [pltpu.with_memory_space_constraint(a, pltpu.VMEM) for a in arrays]
 
 
+def in_hbm(*arrays):
+    return [pltpu.with_memory_space_constraint(a, pltpu.HBM) for a in arrays]
+
+
 def call(body, outs, scratch=(), smem=0, total=0, gflop=1.0):
     in_specs = [pl.BlockSpec(memory_space=pltpu.SMEM)] * smem
     in_specs += [pl.BlockSpec(memory_space=pltpu.VMEM)] * (total - smem)
     return pl.pallas_call(
         body,
-        out_shape=tuple(jax.ShapeDtypeStruct(s, d) for s, d in outs),
+        out_shape=tuple(
+            jax.ShapeDtypeStruct(s, d) if not kept else pltpu.HBM(s, d) for s, d, *kept in outs
+        ),
         in_specs=in_specs,
         out_specs=tuple(pl.BlockSpec(memory_space=pltpu.VMEM) for _ in outs),
         scratch_shapes=list(scratch),
@@ -270,7 +276,7 @@
 
 def expert_rows(sent, gain, act, slope, *refs):
     w_in, w_out = refs[0:2] + refs[4:6], refs[2:4] + refs[6:8]
-    d_expert, back = refs[8:]
+    d_expert, own, back = refs[8:]
     flat = d_expert.shape
     grad = one_of(sent[...], 1)
     total = jnp.zeros(flat, F32)
@@ -280,6 +286,8 @@
     mixed = (unit * gain[...]).astype(BF16)
     d_out = norm_grad(unit, rstd, grad.astype(F32) * gain[...]).astype(BF16)
     d_expert[...] = d_out
+    own[0] = one_of(sent[...], 0)
+    own[1] = d_out
     total = jnp.zeros(flat, F32)
     for s, (w, v) in enumerate(zip(w_in, w_out, strict=True)):
         d_hidden = (dotg(d_out, v[...], 1, 1) * slope[s].astype(F32)).astype(BF16)
@@ -287,11 +295,11 @@
     both_in(back, total.astype(BF16), mixed)
 
 
-def expert_grads(*refs):
-    rows, grads, (w_in, w_out, both) = refs[:SPLIT], refs[SPLIT : 2 * SPLIT], refs[2 * SPLIT :]
+def expert_grads(own, beside, rows2, grad2, rows3, grad3, w_in, w_out, both):
     d_in = jnp.zeros(w_in.shape, F32)
     d_out = jnp.zeros(w_out.shape, F32)
-    for part, grad in zip(rows, grads, strict=True):
+    pairs = [(ref.at[0], ref.at[1]) for ref in (own, beside)] + [(rows2, grad2), (rows3, grad3)]
+    for part, grad in pairs:
         part = part[...]
         act, slope = gelu_parts(dotg(part, w_in[...], 1, 0))
         d_out = d_out + dotg(act.astype(BF16), grad[...], 0, 0)
@@ -382,7 +390,7 @@
         [(quarter, BF16)] * 4
         + [((width, CELLS), BF16)] * 3
         + [
-            ((heads, CELLS, CELLS), BF16),
+            ((heads, CELLS, CELLS), BF16, True),
             ((heads, 8, CELLS), F32),
             ((width, CELLS), BF16),
         ],
@@ -405,7 +413,7 @@
         total=3,
         gflop=2.0,
     )(ids, gate, grad)
-    packed, att = call(pack_residual, [(parts, BF16), (flat, BF16)], total=8)(
+    packed, att = call(pack_residual, [(parts, BF16), (flat, BF16, True)], total=8)(
         *in_vmem(*att_parts), img, a_gain, place, grad_packed
     )
     near, _ = lax.optimization_barrier((near, packed))
@@ -422,22 +430,23 @@
         gflop=2.0,
     )(sent, *near[:2], *far[:2])
     next_rows = swap(rows, 2)
-    d_expert, back = call(expert_rows, [(flat, BF16), (parts, BF16)], total=12, gflop=2.0)(
-        sent, e_gain, act, slope, *near, *far
-    )
-    back, rows, next_rows = lax.optimization_barrier((back, rows, next_rows))
+    d_expert, own, back = call(
+        expert_rows, [(flat, BF16), ((2,) + flat, BF16), (parts, BF16)], total=12, gflop=2.0
+    )(sent, e_gain, act, slope, *in_hbm(*near), *far)
+    back, next_rows = lax.optimization_barrier((back, next_rows))
     back = exchange(back)
     across = swap(d_expert, 2)
-    grads = (d_expert, swap(d_expert, 1), across, swap(across, 1))
-    all_rows = (rows, swap(rows, 1), next_rows, swap(next_rows, 1))
+    late, _ = lax.optimization_barrier((own, across))
+    both_rows = (own, swap(late, 1), next_rows, across, swap(next_rows, 1), swap(across, 1))
     (both,) = call(
-        expert_grads, [((w_in.shape[1], 2 * w_in.shape[2]), BF16)], total=10, gflop=7.0
-    )(*all_rows, *grads, w_in[0], w_out[0])
+        expert_grads, [((w_in.shape[1], 2 * w_in.shape[2]), BF16)], total=8, gflop=5.0
+    )(*in_hbm(*both_rows, w_in[0], w_out[0]))
     back, both = lax.optimization_barrier((back, both))
-    both = lax.psum_scatter(both, "half", scatter_dimension=0, tiled=True).astype(F32)
-    grad_w_in, grad_w_out = both[None, :, : w_in.shape[2]], both[None, :, w_in.shape[2] :]
+    both = lax.psum_scatter(both, "half", scatter_dimension=0, tiled=True)[None]
+    grad_w_in = both[:, :, : w_in.shape[2]].astype(F32)
+    grad_w_out = both[:, :, w_in.shape[2] :].astype(F32)
     d_resid, *d_att = call(residual_grad, [(flat, F32)] + [(quarter, BF16)] * 4, total=5)(
-        att, a_gain, place, grad, *in_vmem(back)
+        *in_hbm(att), a_gain, *in_hbm(place), grad, *in_vmem(back)
     )
     d_rolled = call(
         attention_backward,
@@ -446,10 +455,10 @@
         smem=1,
         total=13,
         gflop=8.0,
-    )(head_scale, d_att[3], *in_vmem(*to_window(*d_att)[1:]), qkv_weight, proj_weight, qs, ku, vt, weights, aux, ho)
+    )(head_scale, d_att[3], *in_vmem(*to_window(*d_att)[1:]), qkv_weight, proj_weight, qs, ku, vt, *in_hbm(weights), aux, ho)
     back, *_ = lax.optimization_barrier((back, *d_rolled))
     (block_out,) = call(finish_block, [(flat, BF16)], total=6)(
-        att, img, a_gain, place, gate, back
+        *in_hbm(att), img, a_gain, place, gate, back
     )
     top_left, top_right, bottom_left, bottom_right = from_window(*d_rolled)
     returned = jnp.concatenate(

time: 165 us -> 160 us (0.970)
  local copies, waits for them, and re-layouts: 15.6 us -> 7.35 us
  Pallas kernels: 28.4 us -> 34.2 us
  starting transfers between devices: 74.5 us -> 70.5 us
    unnamed x86 -> x64, local copies, waits for them, and re-layouts: 12 us -> 3.66 us
    ppermute x10 -> x9, starting transfers between devices: 23.4 us -> 20.9 us  [swap(): lax.ppermute(piece, 'col', [(i, i ^ bit) for i in range(lax.axis_size('co...]
    ppermute x4, waiting for transfers between devices: 6.03 us -> 4.26 us  [send(): lax.ppermute(piece, 'row', [(i, (i + down) % rows) for i in range(rows)])]
  transfers between devices with their start and end apart: 26 -> 25, of which waited for: 9 -> 10; matrix products, arithmetic and copies ran while one was open for 2% -> 2% of each run, Pallas kernels for 17% -> 22%
where the time goes in v2:
time: 160 us; the launch traced here: 159 us
  starting transfers between devices  70.5 us (44%)
  Pallas kernels  34.2 us (21%)
  waiting for transfers between devices  27.2 us (17%)
  between operations  14.6 us (9%)
  local copies, waits for them, and re-layouts  7.35 us (5%)
  other arithmetic  4.93 us (3%)
    ppermute x9, starting transfers between devices, swap(): lax.ppermute(piece, 'col', [(i, i ^ bit) for i in range(lax.axis_size('co...  20.9 us
    ppermute x4, starting transfers between devices, send(): return lax.ppermute(piece, ('row', 'col'), route)  20.9 us
    all_to_all x2, starting transfers between devices, exchange(): lax.all_to_all(parts, ('row', 'col'), split_axis=0, concat_axis=0, tiled=...  16.7 us
    ppermute x4, starting transfers between devices, send(): lax.ppermute(piece, 'row', [(i, (i + down) % rows) for i in range(rows)])  10.8 us
    ppermute x4, waiting for transfers between devices, send(): return lax.ppermute(piece, ('row', 'col'), route)  10.5 us
    all_to_all x2, waiting for transfers between devices, exchange(): lax.all_to_all(parts, ('row', 'col'), split_axis=0, concat_axis=0, tiled=...  10.5 us
    pallas_call x1, Pallas kernels, shards(): call(attention_forward, [(quarter, BF16)] * 4 + [((width, CELLS), BF16)]...  6.74 us
    pallas_call x1, Pallas kernels, shards(): call(attention_backward, [(quarter, BF16)] * 4, [pltpu.VMEM((width, CELLS...  6.46 us
  transfers between devices with their start and end apart: 25, of which 10 were waited for; matrix products, arithmetic and copies ran while one was open for 2% of the time, Pallas kernels for 22%

profile of v2, /device:TPU:2, one launch (start us, length us, event | category | flops | bytes accessed | tf_op | source)
XLA Modules:
  0.0 158.9 jit_solution(4056205144999285794)
XLA Ops:
  7.3 1.1 fusion
  8.3 2.2 %pad_maximum_fusion = bf16[1024,512]{1,0:T(8,128)(2,1)} fusion(bf16[512,512]{1,0:T(8,128)(2,1)} %bitcast.42, bf16[512,512]{1,0:T(8,128)(2,1)} %bitcast.44), kind=kLoop, calls=%fused_computation | loop fusion | flops 2097152 | bytes 2097152 | tf_op jit(solution)/shard_map/concatenate | solution.py:384
  10.6 13.3 %collective-permute-start.2 = (bf16[8,8,512]{2,1,0:T(8,128)(2,1)S(1)}, bf16[8,8,512]{2,1,0:T(8,128)(2,1)S(1)}, u32[]{:S(2)}, u32[]{:S(2)}) collective-permute-start(bf16[8,8,512]{2,1,0:T(8,128)(2,1)S(1)} %get-tuple-element.96), channel_id=1, source_target_pairs={{0,127},{1,112},{2,113},{3,114},{4,115},{5,116},{6,117},{7,118},{8... | collective-permute-start | bytes 196616 | tf_op jit(solution)/shard_map/ppermute | solution.py:323
  23.9 2.5 %collective-permute-start.1 = (bf16[8,8,512]{2,1,0:T(8,128)(2,1)S(1)}, bf16[8,8,512]{2,1,0:T(8,128)(2,1)S(1)}, u32[]{:S(2)}, u32[]{:S(2)}) collective-permute-start(bf16[8,8,512]{2,1,0:T(8,128)(2,1)S(1)} %get-tuple-element.97), channel_id=1, source_target_pairs={{0,112},{16,0},{32,16},{48,32},{64,48},{80,64},{96,80},{112,96},{1... | collective-permute-start | bytes 196616 | tf_op jit(solution)/shard_map/ppermute | solution.py:315
  26.4 0.6 collective-permute-start
  27.0 3.0 %collective-permute-done.1.below = bf16[8,8,512]{2,1,0:T(8,128)(2,1)S(1)} collective-permute-done((bf16[8,8,512]{2,1,0:T(8,128)(2,1)S(1)}, bf16[8,8,512]{2,1,0:T(8,128)(2,1)S(1)}, u32[]{:S(2)}, u32[]{:S(2)}) %collective-permute-start.1) | collective-permute-done | bytes 65568 | tf_op jit(solution)/shard_map/ppermute | solution.py:315
  30.1 6.7 %shard_map.147 = (bf16[8,8,512]{2,1,0:T(8,128)(2,1)S(1)}, bf16[8,8,512]{2,1,0:T(8,128)(2,1)S(1)}, bf16[8,8,512]{2,1,0:T(8,128)(2,1)S(1)}, bf16[8,8,512]{2,1,0:T(...) custom-call(s32[2]{0:T(128)S(1)} %add_convert_fusion.1.edge, ...), custom_call_target="tpu_custom_call" | custom-call | flops 8000000000 | bytes 1048576 | tf_op jit(solution)/shard_map/pallas_call | solution.py:388
  36.8 0.7 copy-done.25
  37.5 1.9 %collective-permute-start.3 = (bf16[8,8,512]{2,1,0:T(8,128)(2,1)S(1)}, bf16[8,8,512]{2,1,0:T(8,128)(2,1)S(1)}, u32[]{:S(2)}, u32[]{:S(2)}) collective-permute-start(bf16[8,8,512]{2,1,0:T(8,128)(2,1)S(1)} %get-tuple-element.47), channel_id=1, source_target_pairs={{0,17},{1,18},{2,19},{3,20},{4,21},{5,22},{6,23},{7,24},{8,25},{9,... | collective-permute-start | bytes 196616 | tf_op jit(solution)/shard_map/ppermute | solution.py:323
  39.4 2.2 %collective-permute-start.4 = (bf16[8,8,512]{2,1,0:T(8,128)(2,1)S(1)}, bf16[8,8,512]{2,1,0:T(8,128)(2,1)S(1)}, u32[]{:S(2)}, u32[]{:S(2)}) collective-permute-start(bf16[8,8,512]{2,1,0:T(8,128)(2,1)S(1)} %get-tuple-element.48), channel_id=1, source_target_pairs={{0,16},{16,32},{32,48},{48,64},{64,80},{80,96},{96,112},{112,0},{1... | collective-permute-start | bytes 196616 | tf_op jit(solution)/shard_map/ppermute | solution.py:315
  41.7 1.1 shard_map.148
  42.8 3.6 %collective-permute-done.3.att0 = bf16[8,8,512]{2,1,0:T(8,128)(2,1)S(1)} collective-permute-done((bf16[8,8,512]{2,1,0:T(8,128)(2,1)S(1)}, bf16[8,8,512]{2,1,0:T(8,128)(2,1)S(1)}, u32[]{:S(2)}, u32[]{:S(2)}) %collective-permute-start.3) | collective-permute-done | bytes 65568 | tf_op jit(solution)/shard_map/ppermute | solution.py:323
  46.4 0.7 collective-permute-done.4.att1
  47.1 1.6 %shard_map.149 = (bf16[128,4,512]{2,1,0:T(4,128)(2,1)}, bf16[256,512]{1,0:T(8,128)(2,1)}) custom-call(bf16[8,8,512]{2,1,0:T(8,128)(2,1)S(1)} %collective-permute-done.3.att0, bf16[8,8,512]{2,1,0:T(8,128)(2,1)S(1)} %collective-permute-done.4.att1, bf16[8,8,512]{2,1,0:T(8,128)(2,1)S(1)} %collective-permute-done.5.att2, ...), custom_call_target="tpu_custom_call" | custom-call | flops 1000000000 | bytes 1048576 | tf_op jit(solution)/shard_map/pallas_call | solution.py:416
  48.8 9.8 %all-to-all-start = ((bf16[128,4,512]{2,1,0:T(4,128)(2,1)}), bf16[128,4,512]{2,1,0:T(4,128)(2,1)S(1)}, u32[]{:S(2)}, u32[]{:S(2)}) async-start(bf16[128,4,512]{2,1,0:T(4,128)(2,1)} %get-tuple-element.55), calls=%async_computation | async-start | bytes 1048576 | tf_op jit(solution)/shard_map/all_to_all | solution.py:335
  58.6 2.6 %slice_bitcast_fusion = (bf16[512,512]{1,0:T(8,128)(2,1)}, bf16[512,512]{1,0:T(8,128)(2,1)}, bf16[512,512]{1,0:T(8,128)(2,1)S(1)}, bf16[512,512]{1,0:T(8,128)(2,1)S(1)}) fusion(bf16[2,1024,512]{2,1,0:T(8,128)(2,1)} %bitcast.41), kind=kLoop, calls=%fused_computation.2 | loop fusion | bytes 4194304 | tf_op jit(solution)/shard_map/squeeze | solution.py:422
  61.3 1.9 %collective-permute-start.6 = (bf16[512,512]{1,0:T(8,128)(2,1)S(1)}, bf16[512,512]{1,0:T(8,128)(2,1)}, u32[]{:S(2)}, u32[]{:S(2)}) collective-permute-start(bf16[512,512]{1,0:T(8,128)(2,1)S(1)} %get-tuple-element.59.block0.refs_0_), channel_id=1, source_target_pairs={{0,1},{1,0},{2,3},{3,2},{4,5},{5,4},{6,7},{7,6},{8,9},{9,8},{10,11... | collective-permute-start | bytes 1572872 | tf_op jit(solution)/shard_map/ppermute | solution.py:339
  63.2 2.4 %collective-permute-start.7 = (bf16[512,512]{1,0:T(8,128)(2,1)S(1)}, bf16[512,512]{1,0:T(8,128)(2,1)}, u32[]{:S(2)}, u32[]{:S(2)}) collective-permute-start(bf16[512,512]{1,0:T(8,128)(2,1)S(1)} %get-tuple-element.60.block1.refs_1_), channel_id=1, source_target_pairs={{0,1},{1,0},{2,3},{3,2},{4,5},{5,4},{6,7},{7,6},{8,9},{9,8},{10,11... | collective-permute-start | bytes 1572872 | tf_op jit(solution)/shard_map/ppermute | solution.py:339
  65.6 1.9 %collective-permute-start.8 = (bf16[512,512]{1,0:T(8,128)(2,1)}, bf16[512,512]{1,0:T(8,128)(2,1)}, u32[]{:S(2)}, u32[]{:S(2)}) collective-permute-start(bf16[512,512]{1,0:T(8,128)(2,1)} %get-tuple-element.63.refs_2_), channel_id=1, source_target_pairs={{0,1},{1,0},{2,3},{3,2},{4,5},{5,4},{6,7},{7,6},{8,9},{9,8},{10,11... | collective-permute-start | bytes 1572872 | tf_op jit(solution)/shard_map/ppermute | solution.py:339
  67.5 2.4 %collective-permute-start.9 = (bf16[512,512]{1,0:T(8,128)(2,1)}, bf16[512,512]{1,0:T(8,128)(2,1)}, u32[]{:S(2)}, u32[]{:S(2)}) collective-permute-start(bf16[512,512]{1,0:T(8,128)(2,1)} %get-tuple-element.64.refs_3_), channel_id=1, source_target_pairs={{0,1},{1,0},{2,3},{3,2},{4,5},{5,4},{6,7},{7,6},{8,9},{9,8},{10,11... | collective-permute-start | bytes 1572872 | tf_op jit(solution)/shard_map/ppermute | solution.py:339
  69.9 7.9 %all-to-all-done.sent = bf16[128,4,512]{2,1,0:T(4,128)(2,1)S(1)} async-done(((bf16[128,4,512]{2,1,0:T(4,128)(2,1)}), bf16[128,4,512]{2,1,0:T(4,128)(2,1)S(1)}, u32[]{:S(2)}, u32[]{:S(2)}) %all-to-all-start) | async-done | bytes 524320 | tf_op jit(solution)/shard_map/all_to_all | solution.py:335
  77.9 2.4 %shard_map.150 = (bf16[256,512]{1,0:T(8,128)(2,1)S(1)}, bf16[4,256,512]{2,1,0:T(8,128)(2,1)S(1)}, bf16[4,256,512]{2,1,0:T(8,128)(2,1)S(1)}) custom-call(bf16[128,4,512]{2,1,0:T(4,128)(2,1)S(1)} %all-to-all-done.sent, bf16[512,512]{1,0:T(8,128)(2,1)S(1)} %get-tuple-element.59.block0.refs_0_, bf16[512,512]{1,0:T(8,128)(2,1)S(1)} %get-tuple-element.60.block1.refs_1_, ...), custom_call_target="tpu_custom_call" | custom-call | flops 2000000000 | bytes 1048576 | tf_op jit(solution)/shard_map/pallas_call | solution.py:426
  80.3 4.0 %collective-permute-start.10 = (bf16[256,512]{1,0:T(8,128)(2,1)S(1)}, bf16[256,512]{1,0:T(8,128)(2,1)S(1)}, u32[]{:S(2)}, u32[]{:S(2)}) collective-permute-start(bf16[256,512]{1,0:T(8,128)(2,1)S(1)} %get-tuple-element.66), channel_id=1, source_target_pairs={{0,2},{1,3},{2,0},{3,1},{4,6},{5,7},{6,4},{7,5},{8,10},{9,11},{10,... | collective-permute-start | bytes 786440 | tf_op jit(solution)/shard_map/ppermute | solution.py:339
  84.3 6.1 %shard_map.151 = (bf16[256,512]{1,0:T(8,128)(2,1)S(1)}, bf16[2,256,512]{2,1,0:T(8,128)(2,1)S(1)}, bf16[128,4,512]{2,1,0:T(4,128)(2,1)}) custom-call(bf16[128,4,512]{2,1,0:T(4,128)(2,1)S(1)} %all-to-all-done.sent, f32[1,512]{1,0:T(1,128)S(1)} %bitcast.37, bf16[4,256,512]{2,1,0:T(8,128)(2,1)S(1)} %get-tuple-element.61.act, ...), custom_call_target="tpu_custom_call" | custom-call | flops 2000000000 | bytes 1048576 | tf_op jit(solution)/shard_map/pallas_call | solution.py:433
  90.4 1.9 %collective-permute-start.11 = (bf16[256,512]{1,0:T(8,128)(2,1)S(1)}, bf16[256,512]{1,0:T(8,128)(2,1)S(1)}, u32[]{:S(2)}, u32[]{:S(2)}) collective-permute-start(bf16[256,512]{1,0:T(8,128)(2,1)S(1)} %get-tuple-element.69), channel_id=1, source_target_pairs={{0,2},{1,3},{2,0},{3,1},{4,6},{5,7},{6,4},{7,5},{8,10},{9,11},{10,... | collective-permute-start | bytes 786440 | tf_op jit(solution)/shard_map/ppermute | solution.py:339
  92.3 0.7 copy-done.28
  93.0 6.9 %all-to-all-start.1 = ((bf16[128,4,512]{2,1,0:T(4,128)(2,1)}), bf16[128,4,512]{2,1,0:T(4,128)(2,1)S(1)}, u32[]{:S(2)}, u32[]{:S(2)}) async-start(bf16[128,4,512]{2,1,0:T(4,128)(2,1)} %get-tuple-element.67), calls=%async_computation.1 | async-start | bytes 1048576 | tf_op jit(solution)/shard_map/all_to_all | solution.py:335
  100.1 0.7 copy-done.29
  100.8 2.0 %collective-permute-start.12 = (bf16[2,256,512]{2,1,0:T(8,128)(2,1)S(1)}, bf16[2,256,512]{2,1,0:T(8,128)(2,1)S(1)}, u32[]{:S(2)}, u32[]{:S(2)}) collective-permute-start(bf16[2,256,512]{2,1,0:T(8,128)(2,1)S(1)} %get-tuple-element.70.own), channel_id=1, source_target_pairs={{0,1},{1,0},{2,3},{3,2},{4,5},{5,4},{6,7},{7,6},{8,9},{9,8},{10,11... | collective-permute-start | bytes 1572872 | tf_op jit(solution)/shard_map/ppermute | solution.py:339
  102.9 2.4 %collective-permute-start.14 = (bf16[256,512]{1,0:T(8,128)(2,1)}, bf16[256,512]{1,0:T(8,128)(2,1)S(1)}, u32[]{:S(2)}, u32[]{:S(2)}) collective-permute-start(bf16[256,512]{1,0:T(8,128)(2,1)} %copy-done.29), channel_id=1, source_target_pairs={{0,1},{1,0},{2,3},{3,2},{4,5},{5,4},{6,7},{7,6},{8,9},{9,8},{10,11... | collective-permute-start | bytes 786440 | tf_op jit(solution)/shard_map/ppermute | solution.py:339
  105.3 1.9 %collective-permute-start.13 = (bf16[256,512]{1,0:T(8,128)(2,1)}, bf16[256,512]{1,0:T(8,128)(2,1)S(1)}, u32[]{:S(2)}, u32[]{:S(2)}) collective-permute-start(bf16[256,512]{1,0:T(8,128)(2,1)} %copy-done.28), channel_id=1, source_target_pairs={{0,1},{1,0},{2,3},{3,2},{4,5},{5,4},{6,7},{7,6},{8,9},{9,8},{10,11... | collective-permute-start | bytes 786440 | tf_op jit(solution)/shard_map/ppermute | solution.py:339
  107.2 1.7 %collective-permute-done.13.rows3 = bf16[256,512]{1,0:T(8,128)(2,1)S(1)} collective-permute-done((bf16[256,512]{1,0:T(8,128)(2,1)}, bf16[256,512]{1,0:T(8,128)(2,1)S(1)}, u32[]{:S(2)}, u32[]{:S(2)}) %collective-permute-start.13) | collective-permute-done | bytes 262176 | tf_op jit(solution)/shard_map/ppermute | solution.py:339
  109.0 0.7 copy-done.31
  109.6 0.8 copy-done.27
  110.4 6.2 %shard_map.152 = bf16[512,1024]{1,0:T(8,128)(2,1)} custom-call(bf16[2,256,512]{2,1,0:T(8,128)(2,1)} %copy-done.6, bf16[2,256,512]{2,1,0:T(8,128)(2,1)} %copy-done.27, bf16[256,512]{1,0:T(8,128)(2,1)} %copy-done.28, bf16[256,512]{1,0:T(8,128)(2,1)} %copy-done.29, bf16[256,512]{1,0:T(8,128)(2,1)} %copy-done.31, bf16[256,512]{1,0:T(8,128)(2,1)} %copy-done.30, ...), custom_call_target="tpu_custom_call" | custom-call | flops 5000000000 | bytes 1048576 | tf_op jit(solution)/shard_map/pallas_call | solution.py:441
  116.6 2.5 %all-to-all-done.1.back = bf16[128,4,512]{2,1,0:T(4,128)(2,1)S(1)} async-done(((bf16[128,4,512]{2,1,0:T(4,128)(2,1)}), bf16[128,4,512]{2,1,0:T(4,128)(2,1)S(1)}, u32[]{:S(2)}, u32[]{:S(2)}) %all-to-all-start.1) | async-done | bytes 524320 | tf_op jit(solution)/shard_map/all_to_all | solution.py:335
  119.3 1.5 shard_map.153
  120.8 0.6 collective-permute-start.15
  121.4 4.1 %collective-permute-start.16 = (bf16[8,8,512]{2,1,0:T(8,128)(2,1)S(1)}, bf16[8,8,512]{2,1,0:T(8,128)(2,1)S(1)}, u32[]{:S(2)}, u32[]{:S(2)}) collective-permute-start(bf16[8,8,512]{2,1,0:T(8,128)(2,1)S(1)} %get-tuple-element.75), channel_id=1, source_target_pairs={{0,112},{16,0},{32,16},{48,32},{64,48},{80,64},{96,80},{112,96},{1... | collective-permute-start | bytes 196616 | tf_op jit(solution)/shard_map/ppermute | solution.py:315
  125.5 2.8 %collective-permute-start.17 = (bf16[8,8,512]{2,1,0:T(8,128)(2,1)S(1)}, bf16[8,8,512]{2,1,0:T(8,128)(2,1)S(1)}, u32[]{:S(2)}, u32[]{:S(2)}) collective-permute-start(bf16[8,8,512]{2,1,0:T(8,128)(2,1)S(1)} %get-tuple-element.76), channel_id=1, source_target_pairs={{0,127},{1,112},{2,113},{3,114},{4,115},{5,116},{6,117},{7,118},{8... | collective-permute-start | bytes 196616 | tf_op jit(solution)/shard_map/ppermute | solution.py:323
  128.4 3.5 %collective-permute-done.17.d3 = bf16[8,8,512]{2,1,0:T(8,128)(2,1)S(1)} collective-permute-done((bf16[8,8,512]{2,1,0:T(8,128)(2,1)S(1)}, bf16[8,8,512]{2,1,0:T(8,128)(2,1)S(1)}, u32[]{:S(2)}, u32[]{:S(2)}) %collective-permute-start.17) | collective-permute-done | bytes 65568 | tf_op jit(solution)/shard_map/ppermute | solution.py:323
  131.9 6.5 %shard_map.154 = (bf16[8,8,512]{2,1,0:T(8,128)(2,1)S(1)}, bf16[8,8,512]{2,1,0:T(8,128)(2,1)S(1)}, bf16[8,8,512]{2,1,0:T(8,128)(2,1)S(1)}, bf16[8,8,512]{2,1,0:T(8,128)(2,1)S(1)}) custom-call(f32[16]{0:T(128)S(1)} %copy-done.14, bf16[8,8,512]{2,1,0:T(8,128)(2,1)S(1)} %get-tuple-element.73.d0, bf16[8,8,512]{2,1,0:T(8,128)(2,1)S(1)} %collective-permute-done.15.d1, ...), custom_call_target="tpu_custom_call" | custom-call | flops 8000000000 | bytes 1048576 | tf_op jit(solution)/shard_map/pallas_call | solution.py:451
  138.4 2.1 %collective-permute-start.19 = (bf16[8,8,512]{2,1,0:T(8,128)(2,1)S(1)}, bf16[8,8,512]{2,1,0:T(8,128)(2,1)S(1)}, u32[]{:S(2)}, u32[]{:S(2)}) collective-permute-start(bf16[8,8,512]{2,1,0:T(8,128)(2,1)S(1)} %get-tuple-element.85), channel_id=1, source_target_pairs={{0,16},{16,32},{32,48},{48,64},{64,80},{80,96},{96,112},{112,0},{1... | collective-permute-start | bytes 196616 | tf_op jit(solution)/shard_map/ppermute | solution.py:315
  140.5 2.9 %collective-permute-start.18 = (bf16[8,8,512]{2,1,0:T(8,128)(2,1)S(1)}, bf16[8,8,512]{2,1,0:T(8,128)(2,1)S(1)}, u32[]{:S(2)}, u32[]{:S(2)}) collective-permute-start(bf16[8,8,512]{2,1,0:T(8,128)(2,1)S(1)} %get-tuple-element.86), channel_id=1, source_target_pairs={{0,17},{1,18},{2,19},{3,20},{4,21},{5,22},{6,23},{7,24},{8,25},{9,... | collective-permute-start | bytes 196616 | tf_op jit(solution)/shard_map/ppermute | solution.py:323
  143.4 2.1 %shard_map.155 = bf16[256,512]{1,0:T(8,128)(2,1)} custom-call(bf16[256,512]{1,0:T(8,128)(2,1)} %get-tuple-element.54.att, bf16[256,512]{1,0:T(8,128)(2,1)S(1)} %bitcast.31, f32[1,512]{1,0:T(1,128)S(1)} %bitcast.40, bf16[256,256]{1,0:T(8,128)(2,1)S(1)} %copy-done.16, f32[16,16]{1,0:T(8,128)S(1)} %bitcast.36, bf16[128,4,512]{2,1,0:T(4,128)(2,1)S(1)} %all-to-all-done.1.back), custom_call_target="tpu_custom_call" | custom-call | flops 1000000000 | bytes 1048576 | tf_op jit(solution)/shard_map/pallas_call | solution.py:460
  146.0 3.4 %collective-permute-done.18 = bf16[8,8,512]{2,1,0:T(8,128)(2,1)S(1)} collective-permute-done((bf16[8,8,512]{2,1,0:T(8,128)(2,1)S(1)}, bf16[8,8,512]{2,1,0:T(8,128)(2,1)S(1)}, u32[]{:S(2)}, u32[]{:S(2)}) %collective-permute-start.18) | collective-permute-done | bytes 65568 | tf_op jit(solution)/shard_map/ppermute | solution.py:323
  149.5 0.8 add_convert_fusion
  150.3 1.8 %slice_convert_fusion = (f32[1,128,512]{2,1,0:T(8,128)}, f32[1,128,512]{2,1,0:T(8,128)}) fusion(bf16[1,128,1024]{2,1,0:T(8,128)(2,1)} %bitcast.46), kind=kLoop, calls=%fused_computation.6 | loop fusion | flops 131072 | bytes 786432 | tf_op jit(solution)/shard_map/convert_element_type | solution.py:447
  (85 shorter events, 1.2 us)
Async XLA Ops:
  7.2 22.9 %copy-start.2 = (bf16[1,16,16,512]{3,2,1,0:T(8,128)(2,1)S(1)}, bf16[1,16,16,512]{3,2,1,0:T(8,128)(2,1)}, u32[]{:S(2)}) copy-start(bf16[1,16,16,512]{3,2,1,0:T(8,128)(2,1)} %param.12) | copy-start | bytes 786436
  7.2 22.9 %copy-start.14 = (f32[16]{0:T(128)S(1)}, f32[16]{0:T(128)}, u32[]{:S(2)}) copy-start(f32[16]{0:T(128)} %scale.3) | copy-start | bytes 196
  7.2 22.9 %copy-start.4 = (bf16[512,512]{1,0:T(8,128)(2,1)S(1)}, bf16[512,512]{1,0:T(8,128)(2,1)}, u32[]{:S(2)}) copy-start(bf16[512,512]{1,0:T(8,128)(2,1)} %proj.3) | copy-start | bytes 1572868
  7.2 22.9 %copy-start.3 = (bf16[512,1536]{1,0:T(8,128)(2,1)S(1)}, bf16[512,1536]{1,0:T(8,128)(2,1)}, u32[]{:S(2)}) copy-start(bf16[512,1536]{1,0:T(8,128)(2,1)} %wqkv.3) | copy-start | bytes 4718596
  7.2 22.9 %copy-start.9 = (f32[16,961]{1,0:T(8,128)S(1)}, f32[16,961]{1,0:T(8,128)}, u32[]{:S(2)}) copy-start(f32[16,961]{1,0:T(8,128)} %table.1) | copy-start | bytes 184516
  7.2 51.4 %all-gather.3.cloned.1.call-start = ((), (), s32[]{:S(2)}) async-start(), calls=%async_computation.4 | async-start | bytes 3145728 | tf_op jit(solution)/shard_map/all_gather | solution.py:345
  10.6 16.4 %collective-permute-start.2 = (bf16[8,8,512]{2,1,0:T(8,128)(2,1)S(1)}, bf16[8,8,512]{2,1,0:T(8,128)(2,1)S(1)}, u32[]{:S(2)}, u32[]{:S(2)}) collective-permute-start(bf16[8,8,512]{2,1,0:T(8,128)(2,1)S(1)} %get-tuple-element.96), channel_id=1, source_target_pairs={{0,127},{1,112},{2,113},{3,114},{4,115},{5,116},{6,117},{7,118},{8... | collective-permute-start | bytes 196616 | tf_op jit(solution)/shard_map/ppermute | solution.py:323
  23.9 6.2 %collective-permute-start.1 = (bf16[8,8,512]{2,1,0:T(8,128)(2,1)S(1)}, bf16[8,8,512]{2,1,0:T(8,128)(2,1)S(1)}, u32[]{:S(2)}, u32[]{:S(2)}) collective-permute-start(bf16[8,8,512]{2,1,0:T(8,128)(2,1)S(1)} %get-tuple-element.97), channel_id=1, source_target_pairs={{0,112},{16,0},{32,16},{48,32},{64,48},{80,64},{96,80},{112,96},{1... | collective-permute-start | bytes 196616 | tf_op jit(solution)/shard_map/ppermute | solution.py:315
  26.4 3.7 %collective-permute-start = (bf16[8,8,512]{2,1,0:T(8,128)(2,1)S(1)}, bf16[8,8,512]{2,1,0:T(8,128)(2,1)S(1)}, u32[]{:S(2)}, u32[]{:S(2)}) collective-permute-start(bf16[8,8,512]{2,1,0:T(8,128)(2,1)S(1)} %get-tuple-element.98), channel_id=1, source_target_pairs={{0,15},{1,0},{2,1},{3,2},{4,3},{5,4},{6,5},{7,6},{8,7},{9,8},{10,9... | collective-permute-start | bytes 196616 | tf_op jit(solution)/shard_map/ppermute | solution.py:317
  27.0 14.6 %copy-start.7 = (bf16[1,16,16,512]{3,2,1,0:T(8,128)(2,1)S(1)}, bf16[1,16,16,512]{3,2,1,0:T(8,128)(2,1)}, u32[]{:S(2)}) copy-start(bf16[1,16,16,512]{3,2,1,0:T(8,128)(2,1)} %param.23) | copy-start | bytes 786436
  27.0 14.6 %copy-start.10 = (s32[1,16,16,1]{2,3,1,0:T(1,128)S(1)}, s32[1,16,16,1]{2,3,1,0:T(1,128)}, u32[]{:S(2)}) copy-start(s32[1,16,16,1]{2,3,1,0:T(1,128)} %param.18) | copy-start | bytes 3076
  27.0 14.6 %copy-start.11 = (f32[1,16,16]{2,1,0:T(8,128)S(1)}, f32[1,16,16]{2,1,0:T(8,128)}, u32[]{:S(2)}) copy-start(f32[1,16,16]{2,1,0:T(8,128)} %param.19) | copy-start | bytes 3076
  37.5 5.3 %copy-start.23 = (bf16[512,256]{1,0:T(8,128)(2,1)}, bf16[512,256]{1,0:T(8,128)(2,1)S(1)}, u32[]{:S(2)}) copy-start(bf16[512,256]{1,0:T(8,128)(2,1)S(1)} %get-tuple-element.82.ho) | copy-start | bytes 786436
  37.5 8.9 %collective-permute-start.3 = (bf16[8,8,512]{2,1,0:T(8,128)(2,1)S(1)}, bf16[8,8,512]{2,1,0:T(8,128)(2,1)S(1)}, u32[]{:S(2)}, u32[]{:S(2)}) collective-permute-start(bf16[8,8,512]{2,1,0:T(8,128)(2,1)S(1)} %get-tuple-element.47), channel_id=1, source_target_pairs={{0,17},{1,18},{2,19},{3,20},{4,21},{5,22},{6,23},{7,24},{8,25},{9,... | collective-permute-start | bytes 196616 | tf_op jit(solution)/shard_map/ppermute | solution.py:323
  39.4 7.7 %collective-permute-start.4 = (bf16[8,8,512]{2,1,0:T(8,128)(2,1)S(1)}, bf16[8,8,512]{2,1,0:T(8,128)(2,1)S(1)}, u32[]{:S(2)}, u32[]{:S(2)}) collective-permute-start(bf16[8,8,512]{2,1,0:T(8,128)(2,1)S(1)} %get-tuple-element.48), channel_id=1, source_target_pairs={{0,16},{16,32},{32,48},{48,64},{64,80},{80,96},{96,112},{112,0},{1... | collective-permute-start | bytes 196616 | tf_op jit(solution)/shard_map/ppermute | solution.py:315
  41.6 5.5 %collective-permute-start.5 = (bf16[8,8,512]{2,1,0:T(8,128)(2,1)S(1)}, bf16[8,8,512]{2,1,0:T(8,128)(2,1)S(1)}, u32[]{:S(2)}, u32[]{:S(2)}) collective-permute-start(bf16[8,8,512]{2,1,0:T(8,128)(2,1)S(1)} %get-tuple-element.49), channel_id=1, source_target_pairs={{0,1},{1,2},{2,3},{3,4},{4,5},{5,6},{6,7},{7,8},{8,9},{9,10},{10,1... | collective-permute-start | bytes 196616 | tf_op jit(solution)/shard_map/ppermute | solution.py:317
  41.7 5.5 %copy-start.13 = (f32[512]{0:T(512)S(1)}, f32[512]{0:T(512)}, u32[]{:S(2)}) copy-start(f32[512]{0:T(512)} %param.17) | copy-start | bytes 6148
  42.8 6.0 %copy-start.15 = (bf16[256,256]{1,0:T(8,128)(2,1)}, bf16[256,256]{1,0:T(8,128)(2,1)S(1)}, u32[]{:S(2)}) copy-start(bf16[256,256]{1,0:T(8,128)(2,1)S(1)} %get-tuple-element.52.place) | copy-start | bytes 393220
  48.8 29.1 %all-to-all-start = ((bf16[128,4,512]{2,1,0:T(4,128)(2,1)}), bf16[128,4,512]{2,1,0:T(4,128)(2,1)S(1)}, u32[]{:S(2)}, u32[]{:S(2)}) async-start(bf16[128,4,512]{2,1,0:T(4,128)(2,1)} %get-tuple-element.55), calls=%async_computation | async-start | bytes 1048576 | tf_op jit(solution)/shard_map/all_to_all | solution.py:335
  61.2 19.0 %copy-start = (bf16[512,512]{1,0:T(8,128)(2,1)}, bf16[512,512]{1,0:T(8,128)(2,1)S(1)}, u32[]{:S(2)}) copy-start(bf16[512,512]{1,0:T(8,128)(2,1)S(1)} %get-tuple-element.60.block1.refs_1_) | copy-start | bytes 1572868
  61.2 19.1 %copy-start.1 = (bf16[512,512]{1,0:T(8,128)(2,1)}, bf16[512,512]{1,0:T(8,128)(2,1)S(1)}, u32[]{:S(2)}) copy-start(bf16[512,512]{1,0:T(8,128)(2,1)S(1)} %get-tuple-element.59.block0.refs_0_) | copy-start | bytes 1572868
  61.2 23.1 %copy-start.12 = (f32[512]{0:T(512)S(1)}, f32[512]{0:T(512)}, u32[]{:S(2)}) copy-start(f32[512]{0:T(512)} %param.22) | copy-start | bytes 6148
  61.3 16.6 %collective-permute-start.6 = (bf16[512,512]{1,0:T(8,128)(2,1)S(1)}, bf16[512,512]{1,0:T(8,128)(2,1)}, u32[]{:S(2)}, u32[]{:S(2)}) collective-permute-start(bf16[512,512]{1,0:T(8,128)(2,1)S(1)} %get-tuple-element.59.block0.refs_0_), channel_id=1, source_target_pairs={{0,1},{1,0},{2,3},{3,2},{4,5},{5,4},{6,7},{7,6},{8,9},{9,8},{10,11... | collective-permute-start | bytes 1572872 | tf_op jit(solution)/shard_map/ppermute | solution.py:339
  63.2 14.7 %collective-permute-start.7 = (bf16[512,512]{1,0:T(8,128)(2,1)S(1)}, bf16[512,512]{1,0:T(8,128)(2,1)}, u32[]{:S(2)}, u32[]{:S(2)}) collective-permute-start(bf16[512,512]{1,0:T(8,128)(2,1)S(1)} %get-tuple-element.60.block1.refs_1_), channel_id=1, source_target_pairs={{0,1},{1,0},{2,3},{3,2},{4,5},{5,4},{6,7},{7,6},{8,9},{9,8},{10,11... | collective-permute-start | bytes 1572872 | tf_op jit(solution)/shard_map/ppermute | solution.py:339
  65.6 18.7 %collective-permute-start.8 = (bf16[512,512]{1,0:T(8,128)(2,1)}, bf16[512,512]{1,0:T(8,128)(2,1)}, u32[]{:S(2)}, u32[]{:S(2)}) collective-permute-start(bf16[512,512]{1,0:T(8,128)(2,1)} %get-tuple-element.63.refs_2_), channel_id=1, source_target_pairs={{0,1},{1,0},{2,3},{3,2},{4,5},{5,4},{6,7},{7,6},{8,9},{9,8},{10,11... | collective-permute-start | bytes 1572872 | tf_op jit(solution)/shard_map/ppermute | solution.py:339
  67.5 16.8 %collective-permute-start.9 = (bf16[512,512]{1,0:T(8,128)(2,1)}, bf16[512,512]{1,0:T(8,128)(2,1)}, u32[]{:S(2)}, u32[]{:S(2)}) collective-permute-start(bf16[512,512]{1,0:T(8,128)(2,1)} %get-tuple-element.64.refs_3_), channel_id=1, source_target_pairs={{0,1},{1,0},{2,3},{3,2},{4,5},{5,4},{6,7},{7,6},{8,9},{9,8},{10,11... | collective-permute-start | bytes 1572872 | tf_op jit(solution)/shard_map/ppermute | solution.py:339
  80.3 12.0 %collective-permute-start.10 = (bf16[256,512]{1,0:T(8,128)(2,1)S(1)}, bf16[256,512]{1,0:T(8,128)(2,1)S(1)}, u32[]{:S(2)}, u32[]{:S(2)}) collective-permute-start(bf16[256,512]{1,0:T(8,128)(2,1)S(1)} %get-tuple-element.66), channel_id=1, source_target_pairs={{0,2},{1,3},{2,0},{3,1},{4,6},{5,7},{6,4},{7,5},{8,10},{9,11},{10,... | collective-permute-start | bytes 786440 | tf_op jit(solution)/shard_map/ppermute | solution.py:339
  90.4 18.6 %copy-start.6 = (bf16[2,256,512]{2,1,0:T(8,128)(2,1)}, bf16[2,256,512]{2,1,0:T(8,128)(2,1)S(1)}, u32[]{:S(2)}) copy-start(bf16[2,256,512]{2,1,0:T(8,128)(2,1)S(1)} %get-tuple-element.70.own) | copy-start | bytes 1572868
  90.4 9.7 %collective-permute-start.11 = (bf16[256,512]{1,0:T(8,128)(2,1)S(1)}, bf16[256,512]{1,0:T(8,128)(2,1)S(1)}, u32[]{:S(2)}, u32[]{:S(2)}) collective-permute-start(bf16[256,512]{1,0:T(8,128)(2,1)S(1)} %get-tuple-element.69), channel_id=1, source_target_pairs={{0,2},{1,3},{2,0},{3,1},{4,6},{5,7},{6,4},{7,5},{8,10},{9,11},{10,... | collective-permute-start | bytes 786440 | tf_op jit(solution)/shard_map/ppermute | solution.py:339
  93.0 26.1 %all-to-all-start.1 = ((bf16[128,4,512]{2,1,0:T(4,128)(2,1)}), bf16[128,4,512]{2,1,0:T(4,128)(2,1)S(1)}, u32[]{:S(2)}, u32[]{:S(2)}) async-start(bf16[128,4,512]{2,1,0:T(4,128)(2,1)} %get-tuple-element.67), calls=%async_computation.1 | async-start | bytes 1048576 | tf_op jit(solution)/shard_map/all_to_all | solution.py:335
  99.9 50.4 %reduce-scatter.2.cloned.1.call-start = ((), (), s32[]{:S(2)}) async-start(), calls=%async_computation.3 | async-start | bytes 1310720 | tf_op jit(solution)/shard_map/reduce_scatter | solution.py:445
  100.8 18.4 %copy-start.8 = (bf16[1,16,16,512]{3,2,1,0:T(8,128)(2,1)S(1)}, bf16[1,16,16,512]{3,2,1,0:T(8,128)(2,1)}, u32[]{:S(2)}) copy-start(bf16[1,16,16,512]{3,2,1,0:T(8,128)(2,1)} %param.23) | copy-start | bytes 786436
  100.8 8.1 %collective-permute-start.12 = (bf16[2,256,512]{2,1,0:T(8,128)(2,1)S(1)}, bf16[2,256,512]{2,1,0:T(8,128)(2,1)S(1)}, u32[]{:S(2)}, u32[]{:S(2)}) collective-permute-start(bf16[2,256,512]{2,1,0:T(8,128)(2,1)S(1)} %get-tuple-element.70.own), channel_id=1, source_target_pairs={{0,1},{1,0},{2,3},{3,2},{4,5},{5,4},{6,7},{7,6},{8,9},{9,8},{10,11... | collective-permute-start | bytes 1572872 | tf_op jit(solution)/shard_map/ppermute | solution.py:339
  102.9 4.3 %collective-permute-start.14 = (bf16[256,512]{1,0:T(8,128)(2,1)}, bf16[256,512]{1,0:T(8,128)(2,1)S(1)}, u32[]{:S(2)}, u32[]{:S(2)}) collective-permute-start(bf16[256,512]{1,0:T(8,128)(2,1)} %copy-done.29), channel_id=1, source_target_pairs={{0,1},{1,0},{2,3},{3,2},{4,5},{5,4},{6,7},{7,6},{8,9},{9,8},{10,11... | collective-permute-start | bytes 786440 | tf_op jit(solution)/shard_map/ppermute | solution.py:339
  105.3 3.6 %collective-permute-start.13 = (bf16[256,512]{1,0:T(8,128)(2,1)}, bf16[256,512]{1,0:T(8,128)(2,1)S(1)}, u32[]{:S(2)}, u32[]{:S(2)}) collective-permute-start(bf16[256,512]{1,0:T(8,128)(2,1)} %copy-done.28), channel_id=1, source_target_pairs={{0,1},{1,0},{2,3},{3,2},{4,5},{5,4},{6,7},{7,6},{8,9},{9,8},{10,11... | collective-permute-start | bytes 786440 | tf_op jit(solution)/shard_map/ppermute | solution.py:339
  119.2 12.6 %copy-start.5 = (bf16[512,512]{1,0:T(8,128)(2,1)S(1)}, bf16[512,512]{1,0:T(8,128)(2,1)}, u32[]{:S(2)}) copy-start(bf16[512,512]{1,0:T(8,128)(2,1)} %proj.3) | copy-start | bytes 1572868
  119.2 12.6 %copy-start.18 = (bf16[512,256]{1,0:T(8,128)(2,1)S(1)}, bf16[512,256]{1,0:T(8,128)(2,1)}, u32[]{:S(2)}) copy-start(bf16[512,256]{1,0:T(8,128)(2,1)} %copy-done.17) | copy-start | bytes 786436
  119.2 12.6 %copy-start.20 = (bf16[512,256]{1,0:T(8,128)(2,1)S(1)}, bf16[512,256]{1,0:T(8,128)(2,1)}, u32[]{:S(2)}) copy-start(bf16[512,256]{1,0:T(8,128)(2,1)} %copy-done.19) | copy-start | bytes 786436
  119.2 12.6 %copy-start.22 = (bf16[512,256]{1,0:T(8,128)(2,1)S(1)}, bf16[512,256]{1,0:T(8,128)(2,1)}, u32[]{:S(2)}) copy-start(bf16[512,256]{1,0:T(8,128)(2,1)} %copy-done.21) | copy-start | bytes 786436
  119.2 12.6 %copy-start.24 = (bf16[512,256]{1,0:T(8,128)(2,1)S(1)}, bf16[512,256]{1,0:T(8,128)(2,1)}, u32[]{:S(2)}) copy-start(bf16[512,256]{1,0:T(8,128)(2,1)} %copy-done.23) | copy-start | bytes 786436
  119.3 12.6 %copy-start.26 = (f32[16,8,256]{2,1,0:T(8,128)S(1)}, f32[16,8,256]{2,1,0:T(8,128)}, u32[]{:S(2)}) copy-start(f32[16,8,256]{2,1,0:T(8,128)} %copy-done.25) | copy-start | bytes 393220
  120.8 7.5 %collective-permute-start.15 = (bf16[8,8,512]{2,1,0:T(8,128)(2,1)S(1)}, bf16[8,8,512]{2,1,0:T(8,128)(2,1)S(1)}, u32[]{:S(2)}, u32[]{:S(2)}) collective-permute-start(bf16[8,8,512]{2,1,0:T(8,128)(2,1)S(1)} %get-tuple-element.74), channel_id=1, source_target_pairs={{0,15},{1,0},{2,1},{3,2},{4,3},{5,4},{6,5},{7,6},{8,7},{9,8},{10,9... | collective-permute-start | bytes 196616 | tf_op jit(solution)/shard_map/ppermute | solution.py:317
  121.4 7.0 %collective-permute-start.16 = (bf16[8,8,512]{2,1,0:T(8,128)(2,1)S(1)}, bf16[8,8,512]{2,1,0:T(8,128)(2,1)S(1)}, u32[]{:S(2)}, u32[]{:S(2)}) collective-permute-start(bf16[8,8,512]{2,1,0:T(8,128)(2,1)S(1)} %get-tuple-element.75), channel_id=1, source_target_pairs={{0,112},{16,0},{32,16},{48,32},{64,48},{80,64},{96,80},{112,96},{1... | collective-permute-start | bytes 196616 | tf_op jit(solution)/shard_map/ppermute | solution.py:315
  125.5 6.3 %collective-permute-start.17 = (bf16[8,8,512]{2,1,0:T(8,128)(2,1)S(1)}, bf16[8,8,512]{2,1,0:T(8,128)(2,1)S(1)}, u32[]{:S(2)}, u32[]{:S(2)}) collective-permute-start(bf16[8,8,512]{2,1,0:T(8,128)(2,1)S(1)} %get-tuple-element.76), channel_id=1, source_target_pairs={{0,127},{1,112},{2,113},{3,114},{4,115},{5,116},{6,117},{7,118},{8... | collective-permute-start | bytes 196616 | tf_op jit(solution)/shard_map/ppermute | solution.py:323
  131.9 11.5 %copy-start.16 = (bf16[256,256]{1,0:T(8,128)(2,1)S(1)}, bf16[256,256]{1,0:T(8,128)(2,1)}, u32[]{:S(2)}) copy-start(bf16[256,256]{1,0:T(8,128)(2,1)} %copy-done.15) | copy-start | bytes 393220
  138.4 7.1 %collective-permute-start.20 = (bf16[8,8,512]{2,1,0:T(8,128)(2,1)S(1)}, bf16[8,8,512]{2,1,0:T(8,128)(2,1)S(1)}, u32[]{:S(2)}, u32[]{:S(2)}) collective-permute-start(bf16[8,8,512]{2,1,0:T(8,128)(2,1)S(1)} %get-tuple-element.84), channel_id=1, source_target_pairs={{0,1},{1,2},{2,3},{3,4},{4,5},{5,6},{6,7},{7,8},{8,9},{9,10},{10,1... | collective-permute-start | bytes 196616 | tf_op jit(solution)/shard_map/ppermute | solution.py:317
  138.4 7.7 %collective-permute-start.19 = (bf16[8,8,512]{2,1,0:T(8,128)(2,1)S(1)}, bf16[8,8,512]{2,1,0:T(8,128)(2,1)S(1)}, u32[]{:S(2)}, u32[]{:S(2)}) collective-permute-start(bf16[8,8,512]{2,1,0:T(8,128)(2,1)S(1)} %get-tuple-element.85), channel_id=1, source_target_pairs={{0,16},{16,32},{32,48},{48,64},{64,80},{80,96},{96,112},{112,0},{1... | collective-permute-start | bytes 196616 | tf_op jit(solution)/shard_map/ppermute | solution.py:315
  140.5 9.0 %collective-permute-start.18 = (bf16[8,8,512]{2,1,0:T(8,128)(2,1)S(1)}, bf16[8,8,512]{2,1,0:T(8,128)(2,1)S(1)}, u32[]{:S(2)}, u32[]{:S(2)}) collective-permute-start(bf16[8,8,512]{2,1,0:T(8,128)(2,1)S(1)} %get-tuple-element.86), channel_id=1, source_target_pairs={{0,17},{1,18},{2,19},{3,20},{4,21},{5,22},{6,23},{7,24},{8,25},{9,... | collective-permute-start | bytes 196616 | tf_op jit(solution)/shard_map/ppermute | solution.py:323
  (9 other events, 21.1 us)
Sparse Core Ops, SparseCore 0:
  10.7 45.6 all-gather.2
  119.3 24.8 reduce-scatter.1

commit v3 on v2

--- a/solution.py
+++ b/solution.py
@@ -11,7 +11,7 @@
 CELLS = WIN * WIN
 HEAD_W = 32
 EPS = 1e-05
-TURNS = 8
+TURNS = 16
 BF16 = jnp.bfloat16
 F32 = jnp.float32
 VMEM_BYTES = 24 * 1024 * 1024
@@ -391,7 +391,7 @@
         + [((width, CELLS), BF16)] * 3
         + [
             ((heads, CELLS, CELLS), BF16, True),
-            ((heads, 8, CELLS), F32),
+            ((heads, 8, CELLS), F32, True),
             ((width, CELLS), BF16),
         ],
         [
@@ -455,7 +455,7 @@
         smem=1,
         total=13,
         gflop=8.0,
-    )(head_scale, d_att[3], *in_vmem(*to_window(*d_att)[1:]), qkv_weight, proj_weight, qs, ku, vt, *in_hbm(weights), aux, ho)
+    )(head_scale, d_att[3], *in_vmem(*to_window(*d_att)[1:]), qkv_weight, proj_weight, qs, ku, vt, *in_hbm(weights, aux), ho)
     back, *_ = lax.optimization_barrier((back, *d_rolled))
     (block_out,) = call(finish_block, [(flat, BF16)], total=6)(
         *in_hbm(att), img, a_gain, place, gate, back

time: 160 us -> 159 us (level)
    unnamed x64 -> x60, local copies, waits for them, and re-layouts: 3.66 us -> 3.02 us
  transfers between devices with their start and end apart: 25 -> 25, of which waited for: 10 -> 10; matrix products, arithmetic and copies ran while one was open for 2% -> 2% of each run, Pallas kernels for 22% -> 21%
where the time goes in v3:
time: 159 us; the launch traced here: 158 us
  starting transfers between devices  70.5 us (44%)
  Pallas kernels  33.7 us (21%)
  waiting for transfers between devices  27.2 us (17%)
  between operations  14.6 us (9%)
  local copies, waits for them, and re-layouts  6.72 us (4%)
  other arithmetic  4.94 us (3%)
    ppermute x9, starting transfers between devices, swap(): lax.ppermute(piece, 'col', [(i, i ^ bit) for i in range(lax.axis_size('co...  21.1 us
    ppermute x4, starting transfers between devices, send(): return lax.ppermute(piece, ('row', 'col'), route)  20.9 us
    all_to_all x2, starting transfers between devices, exchange(): lax.all_to_all(parts, ('row', 'col'), split_axis=0, concat_axis=0, tiled=...  16.5 us
    ppermute x4, starting transfers between devices, send(): lax.ppermute(piece, 'row', [(i, (i + down) % rows) for i in range(rows)])  10.9 us
    ppermute x4, waiting for transfers between devices, send(): return lax.ppermute(piece, ('row', 'col'), route)  10.5 us
    all_to_all x2, waiting for transfers between devices, exchange(): lax.all_to_all(parts, ('row', 'col'), split_axis=0, concat_axis=0, tiled=...  10.3 us
    pallas_call x1, Pallas kernels, shards(): call(attention_forward, [(quarter, BF16)] * 4 + [((width, CELLS), BF16)]...  6.38 us
    pallas_call x1, Pallas kernels, shards(): call(attention_backward, [(quarter, BF16)] * 4, [pltpu.VMEM((width, CELLS...  6.28 us
  transfers between devices with their start and end apart: 25, of which 10 were waited for; matrix products, arithmetic and copies ran while one was open for 2% of the time, Pallas kernels for 21%

profile of v3, /device:TPU:2, one launch (start us, length us, event | category | flops | bytes accessed | tf_op | source)
XLA Modules:
  0.0 157.7 jit_solution(13688711563116986882)
XLA Ops:
  7.3 1.1 fusion
  8.3 2.3 %pad_maximum_fusion = bf16[1024,512]{1,0:T(8,128)(2,1)} fusion(bf16[512,512]{1,0:T(8,128)(2,1)} %bitcast.42, bf16[512,512]{1,0:T(8,128)(2,1)} %bitcast.44), kind=kLoop, calls=%fused_computation | loop fusion | flops 2097152 | bytes 2097152 | tf_op jit(solution)/shard_map/concatenate | solution.py:384
  10.6 13.3 %collective-permute-start.2 = (bf16[8,8,512]{2,1,0:T(8,128)(2,1)S(1)}, bf16[8,8,512]{2,1,0:T(8,128)(2,1)S(1)}, u32[]{:S(2)}, u32[]{:S(2)}) collective-permute-start(bf16[8,8,512]{2,1,0:T(8,128)(2,1)S(1)} %get-tuple-element.96), channel_id=1, source_target_pairs={{0,127},{1,112},{2,113},{3,114},{4,115},{5,116},{6,117},{7,118},{8... | collective-permute-start | bytes 196616 | tf_op jit(solution)/shard_map/ppermute | solution.py:323
  23.9 2.5 %collective-permute-start.1 = (bf16[8,8,512]{2,1,0:T(8,128)(2,1)S(1)}, bf16[8,8,512]{2,1,0:T(8,128)(2,1)S(1)}, u32[]{:S(2)}, u32[]{:S(2)}) collective-permute-start(bf16[8,8,512]{2,1,0:T(8,128)(2,1)S(1)} %get-tuple-element.97), channel_id=1, source_target_pairs={{0,112},{16,0},{32,16},{48,32},{64,48},{80,64},{96,80},{112,96},{1... | collective-permute-start | bytes 196616 | tf_op jit(solution)/shard_map/ppermute | solution.py:315
  26.4 0.6 collective-permute-start
  27.0 3.0 %collective-permute-done.1.below = bf16[8,8,512]{2,1,0:T(8,128)(2,1)S(1)} collective-permute-done((bf16[8,8,512]{2,1,0:T(8,128)(2,1)S(1)}, bf16[8,8,512]{2,1,0:T(8,128)(2,1)S(1)}, u32[]{:S(2)}, u32[]{:S(2)}) %collective-permute-start.1) | collective-permute-done | bytes 65568 | tf_op jit(solution)/shard_map/ppermute | solution.py:315
  30.1 6.4 %shard_map.147 = (bf16[8,8,512]{2,1,0:T(8,128)(2,1)S(1)}, bf16[8,8,512]{2,1,0:T(8,128)(2,1)S(1)}, bf16[8,8,512]{2,1,0:T(8,128)(2,1)S(1)}, bf16[8,8,512]{2,1,0:T(...) custom-call(s32[2]{0:T(128)S(1)} %add_convert_fusion.1.edge, ...), custom_call_target="tpu_custom_call" | custom-call | flops 8000000000 | bytes 1048576 | tf_op jit(solution)/shard_map/pallas_call | solution.py:388
  36.5 1.9 %collective-permute-start.3 = (bf16[8,8,512]{2,1,0:T(8,128)(2,1)S(1)}, bf16[8,8,512]{2,1,0:T(8,128)(2,1)S(1)}, u32[]{:S(2)}, u32[]{:S(2)}) collective-permute-start(bf16[8,8,512]{2,1,0:T(8,128)(2,1)S(1)} %get-tuple-element.47), channel_id=1, source_target_pairs={{0,17},{1,18},{2,19},{3,20},{4,21},{5,22},{6,23},{7,24},{8,25},{9,... | collective-permute-start | bytes 196616 | tf_op jit(solution)/shard_map/ppermute | solution.py:323
  38.4 2.2 %collective-permute-start.4 = (bf16[8,8,512]{2,1,0:T(8,128)(2,1)S(1)}, bf16[8,8,512]{2,1,0:T(8,128)(2,1)S(1)}, u32[]{:S(2)}, u32[]{:S(2)}) collective-permute-start(bf16[8,8,512]{2,1,0:T(8,128)(2,1)S(1)} %get-tuple-element.48), channel_id=1, source_target_pairs={{0,16},{16,32},{32,48},{48,64},{64,80},{80,96},{96,112},{112,0},{1... | collective-permute-start | bytes 196616 | tf_op jit(solution)/shard_map/ppermute | solution.py:315
  40.7 1.1 shard_map.148
  41.8 3.6 %collective-permute-done.3.att0 = bf16[8,8,512]{2,1,0:T(8,128)(2,1)S(1)} collective-permute-done((bf16[8,8,512]{2,1,0:T(8,128)(2,1)S(1)}, bf16[8,8,512]{2,1,0:T(8,128)(2,1)S(1)}, u32[]{:S(2)}, u32[]{:S(2)}) %collective-permute-start.3) | collective-permute-done | bytes 65568 | tf_op jit(solution)/shard_map/ppermute | solution.py:323
  45.5 0.7 collective-permute-done.4.att1
  46.1 1.6 %shard_map.149 = (bf16[128,4,512]{2,1,0:T(4,128)(2,1)}, bf16[256,512]{1,0:T(8,128)(2,1)}) custom-call(bf16[8,8,512]{2,1,0:T(8,128)(2,1)S(1)} %collective-permute-done.3.att0, bf16[8,8,512]{2,1,0:T(8,128)(2,1)S(1)} %collective-permute-done.4.att1, bf16[8,8,512]{2,1,0:T(8,128)(2,1)S(1)} %collective-permute-done.5.att2, ...), custom_call_target="tpu_custom_call" | custom-call | flops 1000000000 | bytes 1048576 | tf_op jit(solution)/shard_map/pallas_call | solution.py:416
  47.8 9.8 %all-to-all-start = ((bf16[128,4,512]{2,1,0:T(4,128)(2,1)}), bf16[128,4,512]{2,1,0:T(4,128)(2,1)S(1)}, u32[]{:S(2)}, u32[]{:S(2)}) async-start(bf16[128,4,512]{2,1,0:T(4,128)(2,1)} %get-tuple-element.55), calls=%async_computation | async-start | bytes 1048576 | tf_op jit(solution)/shard_map/all_to_all | solution.py:335
  57.6 2.6 %slice_bitcast_fusion = (bf16[512,512]{1,0:T(8,128)(2,1)}, bf16[512,512]{1,0:T(8,128)(2,1)}, bf16[512,512]{1,0:T(8,128)(2,1)S(1)}, bf16[512,512]{1,0:T(8,128)(2,1)S(1)}) fusion(bf16[2,1024,512]{2,1,0:T(8,128)(2,1)} %bitcast.41), kind=kLoop, calls=%fused_computation.2 | loop fusion | bytes 4194304 | tf_op jit(solution)/shard_map/squeeze | solution.py:422
  60.3 1.9 %collective-permute-start.6 = (bf16[512,512]{1,0:T(8,128)(2,1)S(1)}, bf16[512,512]{1,0:T(8,128)(2,1)}, u32[]{:S(2)}, u32[]{:S(2)}) collective-permute-start(bf16[512,512]{1,0:T(8,128)(2,1)S(1)} %get-tuple-element.59.block0.refs_0_), channel_id=1, source_target_pairs={{0,1},{1,0},{2,3},{3,2},{4,5},{5,4},{6,7},{7,6},{8,9},{9,8},{10,11... | collective-permute-start | bytes 1572872 | tf_op jit(solution)/shard_map/ppermute | solution.py:339
  62.2 2.4 %collective-permute-start.7 = (bf16[512,512]{1,0:T(8,128)(2,1)S(1)}, bf16[512,512]{1,0:T(8,128)(2,1)}, u32[]{:S(2)}, u32[]{:S(2)}) collective-permute-start(bf16[512,512]{1,0:T(8,128)(2,1)S(1)} %get-tuple-element.60.block1.refs_1_), channel_id=1, source_target_pairs={{0,1},{1,0},{2,3},{3,2},{4,5},{5,4},{6,7},{7,6},{8,9},{9,8},{10,11... | collective-permute-start | bytes 1572872 | tf_op jit(solution)/shard_map/ppermute | solution.py:339
  64.6 1.9 %collective-permute-start.8 = (bf16[512,512]{1,0:T(8,128)(2,1)}, bf16[512,512]{1,0:T(8,128)(2,1)}, u32[]{:S(2)}, u32[]{:S(2)}) collective-permute-start(bf16[512,512]{1,0:T(8,128)(2,1)} %get-tuple-element.63.refs_2_), channel_id=1, source_target_pairs={{0,1},{1,0},{2,3},{3,2},{4,5},{5,4},{6,7},{7,6},{8,9},{9,8},{10,11... | collective-permute-start | bytes 1572872 | tf_op jit(solution)/shard_map/ppermute | solution.py:339
  66.5 2.4 %collective-permute-start.9 = (bf16[512,512]{1,0:T(8,128)(2,1)}, bf16[512,512]{1,0:T(8,128)(2,1)}, u32[]{:S(2)}, u32[]{:S(2)}) collective-permute-start(bf16[512,512]{1,0:T(8,128)(2,1)} %get-tuple-element.64.refs_3_), channel_id=1, source_target_pairs={{0,1},{1,0},{2,3},{3,2},{4,5},{5,4},{6,7},{7,6},{8,9},{9,8},{10,11... | collective-permute-start | bytes 1572872 | tf_op jit(solution)/shard_map/ppermute | solution.py:339
  68.9 7.9 %all-to-all-done.sent = bf16[128,4,512]{2,1,0:T(4,128)(2,1)S(1)} async-done(((bf16[128,4,512]{2,1,0:T(4,128)(2,1)}), bf16[128,4,512]{2,1,0:T(4,128)(2,1)S(1)}, u32[]{:S(2)}, u32[]{:S(2)}) %all-to-all-start) | async-done | bytes 524320 | tf_op jit(solution)/shard_map/all_to_all | solution.py:335
  76.9 2.4 %shard_map.150 = (bf16[256,512]{1,0:T(8,128)(2,1)S(1)}, bf16[4,256,512]{2,1,0:T(8,128)(2,1)S(1)}, bf16[4,256,512]{2,1,0:T(8,128)(2,1)S(1)}) custom-call(bf16[128,4,512]{2,1,0:T(4,128)(2,1)S(1)} %all-to-all-done.sent, bf16[512,512]{1,0:T(8,128)(2,1)S(1)} %get-tuple-element.59.block0.refs_0_, bf16[512,512]{1,0:T(8,128)(2,1)S(1)} %get-tuple-element.60.block1.refs_1_, ...), custom_call_target="tpu_custom_call" | custom-call | flops 2000000000 | bytes 1048576 | tf_op jit(solution)/shard_map/pallas_call | solution.py:426
  79.3 4.1 %collective-permute-start.10 = (bf16[256,512]{1,0:T(8,128)(2,1)S(1)}, bf16[256,512]{1,0:T(8,128)(2,1)S(1)}, u32[]{:S(2)}, u32[]{:S(2)}) collective-permute-start(bf16[256,512]{1,0:T(8,128)(2,1)S(1)} %get-tuple-element.66), channel_id=1, source_target_pairs={{0,2},{1,3},{2,0},{3,1},{4,6},{5,7},{6,4},{7,5},{8,10},{9,11},{10,... | collective-permute-start | bytes 786440 | tf_op jit(solution)/shard_map/ppermute | solution.py:339
  83.5 6.1 %shard_map.151 = (bf16[256,512]{1,0:T(8,128)(2,1)S(1)}, bf16[2,256,512]{2,1,0:T(8,128)(2,1)S(1)}, bf16[128,4,512]{2,1,0:T(4,128)(2,1)}) custom-call(bf16[128,4,512]{2,1,0:T(4,128)(2,1)S(1)} %all-to-all-done.sent, f32[1,512]{1,0:T(1,128)S(1)} %bitcast.37, bf16[4,256,512]{2,1,0:T(8,128)(2,1)S(1)} %get-tuple-element.61.act, ...), custom_call_target="tpu_custom_call" | custom-call | flops 2000000000 | bytes 1048576 | tf_op jit(solution)/shard_map/pallas_call | solution.py:433
  89.6 1.9 %collective-permute-start.11 = (bf16[256,512]{1,0:T(8,128)(2,1)S(1)}, bf16[256,512]{1,0:T(8,128)(2,1)S(1)}, u32[]{:S(2)}, u32[]{:S(2)}) collective-permute-start(bf16[256,512]{1,0:T(8,128)(2,1)S(1)} %get-tuple-element.69), channel_id=1, source_target_pairs={{0,2},{1,3},{2,0},{3,1},{4,6},{5,7},{6,4},{7,5},{8,10},{9,11},{10,... | collective-permute-start | bytes 786440 | tf_op jit(solution)/shard_map/ppermute | solution.py:339
  91.5 0.7 copy-done.26
  92.2 6.7 %all-to-all-start.1 = ((bf16[128,4,512]{2,1,0:T(4,128)(2,1)}), bf16[128,4,512]{2,1,0:T(4,128)(2,1)S(1)}, u32[]{:S(2)}, u32[]{:S(2)}) async-start(bf16[128,4,512]{2,1,0:T(4,128)(2,1)} %get-tuple-element.67), calls=%async_computation.1 | async-start | bytes 1048576 | tf_op jit(solution)/shard_map/all_to_all | solution.py:335
  99.3 0.7 copy-done.27
  100.0 2.0 %collective-permute-start.12 = (bf16[2,256,512]{2,1,0:T(8,128)(2,1)S(1)}, bf16[2,256,512]{2,1,0:T(8,128)(2,1)S(1)}, u32[]{:S(2)}, u32[]{:S(2)}) collective-permute-start(bf16[2,256,512]{2,1,0:T(8,128)(2,1)S(1)} %get-tuple-element.70.own), channel_id=1, source_target_pairs={{0,1},{1,0},{2,3},{3,2},{4,5},{5,4},{6,7},{7,6},{8,9},{9,8},{10,11... | collective-permute-start | bytes 1572872 | tf_op jit(solution)/shard_map/ppermute | solution.py:339
  102.1 2.4 %collective-permute-start.14 = (bf16[256,512]{1,0:T(8,128)(2,1)}, bf16[256,512]{1,0:T(8,128)(2,1)S(1)}, u32[]{:S(2)}, u32[]{:S(2)}) collective-permute-start(bf16[256,512]{1,0:T(8,128)(2,1)} %copy-done.27), channel_id=1, source_target_pairs={{0,1},{1,0},{2,3},{3,2},{4,5},{5,4},{6,7},{7,6},{8,9},{9,8},{10,11... | collective-permute-start | bytes 786440 | tf_op jit(solution)/shard_map/ppermute | solution.py:339
  104.5 1.9 %collective-permute-start.13 = (bf16[256,512]{1,0:T(8,128)(2,1)}, bf16[256,512]{1,0:T(8,128)(2,1)S(1)}, u32[]{:S(2)}, u32[]{:S(2)}) collective-permute-start(bf16[256,512]{1,0:T(8,128)(2,1)} %copy-done.26), channel_id=1, source_target_pairs={{0,1},{1,0},{2,3},{3,2},{4,5},{5,4},{6,7},{7,6},{8,9},{9,8},{10,11... | collective-permute-start | bytes 786440 | tf_op jit(solution)/shard_map/ppermute | solution.py:339
  106.4 1.7 %collective-permute-done.13.rows3 = bf16[256,512]{1,0:T(8,128)(2,1)S(1)} collective-permute-done((bf16[256,512]{1,0:T(8,128)(2,1)}, bf16[256,512]{1,0:T(8,128)(2,1)S(1)}, u32[]{:S(2)}, u32[]{:S(2)}) %collective-permute-start.13) | collective-permute-done | bytes 262176 | tf_op jit(solution)/shard_map/ppermute | solution.py:339
  108.1 0.7 copy-done.29
  108.8 0.8 copy-done.25
  109.6 6.2 %shard_map.152 = bf16[512,1024]{1,0:T(8,128)(2,1)} custom-call(bf16[2,256,512]{2,1,0:T(8,128)(2,1)} %copy-done.6, bf16[2,256,512]{2,1,0:T(8,128)(2,1)} %copy-done.25, bf16[256,512]{1,0:T(8,128)(2,1)} %copy-done.26, bf16[256,512]{1,0:T(8,128)(2,1)} %copy-done.27, bf16[256,512]{1,0:T(8,128)(2,1)} %copy-done.29, bf16[256,512]{1,0:T(8,128)(2,1)} %copy-done.28, ...), custom_call_target="tpu_custom_call" | custom-call | flops 5000000000 | bytes 1048576 | tf_op jit(solution)/shard_map/pallas_call | solution.py:441
  115.8 2.3 %all-to-all-done.1.back = bf16[128,4,512]{2,1,0:T(4,128)(2,1)S(1)} async-done(((bf16[128,4,512]{2,1,0:T(4,128)(2,1)}), bf16[128,4,512]{2,1,0:T(4,128)(2,1)S(1)}, u32[]{:S(2)}, u32[]{:S(2)}) %all-to-all-start.1) | async-done | bytes 524320 | tf_op jit(solution)/shard_map/all_to_all | solution.py:335
  118.3 1.5 shard_map.153
  119.8 0.6 collective-permute-start.15
  120.4 4.2 %collective-permute-start.16 = (bf16[8,8,512]{2,1,0:T(8,128)(2,1)S(1)}, bf16[8,8,512]{2,1,0:T(8,128)(2,1)S(1)}, u32[]{:S(2)}, u32[]{:S(2)}) collective-permute-start(bf16[8,8,512]{2,1,0:T(8,128)(2,1)S(1)} %get-tuple-element.75), channel_id=1, source_target_pairs={{0,112},{16,0},{32,16},{48,32},{64,48},{80,64},{96,80},{112,96},{1... | collective-permute-start | bytes 196616 | tf_op jit(solution)/shard_map/ppermute | solution.py:315
  124.6 2.8 %collective-permute-start.17 = (bf16[8,8,512]{2,1,0:T(8,128)(2,1)S(1)}, bf16[8,8,512]{2,1,0:T(8,128)(2,1)S(1)}, u32[]{:S(2)}, u32[]{:S(2)}) collective-permute-start(bf16[8,8,512]{2,1,0:T(8,128)(2,1)S(1)} %get-tuple-element.76), channel_id=1, source_target_pairs={{0,127},{1,112},{2,113},{3,114},{4,115},{5,116},{6,117},{7,118},{8... | collective-permute-start | bytes 196616 | tf_op jit(solution)/shard_map/ppermute | solution.py:323
  127.4 3.5 %collective-permute-done.17.d3 = bf16[8,8,512]{2,1,0:T(8,128)(2,1)S(1)} collective-permute-done((bf16[8,8,512]{2,1,0:T(8,128)(2,1)S(1)}, bf16[8,8,512]{2,1,0:T(8,128)(2,1)S(1)}, u32[]{:S(2)}, u32[]{:S(2)}) %collective-permute-start.17) | collective-permute-done | bytes 65568 | tf_op jit(solution)/shard_map/ppermute | solution.py:323
  130.9 6.3 %shard_map.154 = (bf16[8,8,512]{2,1,0:T(8,128)(2,1)S(1)}, bf16[8,8,512]{2,1,0:T(8,128)(2,1)S(1)}, bf16[8,8,512]{2,1,0:T(8,128)(2,1)S(1)}, bf16[8,8,512]{2,1,0:T(8,128)(2,1)S(1)}) custom-call(f32[16]{0:T(128)S(1)} %copy-done.14, bf16[8,8,512]{2,1,0:T(8,128)(2,1)S(1)} %get-tuple-element.73.d0, bf16[8,8,512]{2,1,0:T(8,128)(2,1)S(1)} %collective-permute-done.15.d1, ...), custom_call_target="tpu_custom_call" | custom-call | flops 8000000000 | bytes 1048576 | tf_op jit(solution)/shard_map/pallas_call | solution.py:451
  137.2 2.1 %collective-permute-start.19 = (bf16[8,8,512]{2,1,0:T(8,128)(2,1)S(1)}, bf16[8,8,512]{2,1,0:T(8,128)(2,1)S(1)}, u32[]{:S(2)}, u32[]{:S(2)}) collective-permute-start(bf16[8,8,512]{2,1,0:T(8,128)(2,1)S(1)} %get-tuple-element.85), channel_id=1, source_target_pairs={{0,16},{16,32},{32,48},{48,64},{64,80},{80,96},{96,112},{112,0},{1... | collective-permute-start | bytes 196616 | tf_op jit(solution)/shard_map/ppermute | solution.py:315
  139.3 2.9 %collective-permute-start.18 = (bf16[8,8,512]{2,1,0:T(8,128)(2,1)S(1)}, bf16[8,8,512]{2,1,0:T(8,128)(2,1)S(1)}, u32[]{:S(2)}, u32[]{:S(2)}) collective-permute-start(bf16[8,8,512]{2,1,0:T(8,128)(2,1)S(1)} %get-tuple-element.86), channel_id=1, source_target_pairs={{0,17},{1,18},{2,19},{3,20},{4,21},{5,22},{6,23},{7,24},{8,25},{9,... | collective-permute-start | bytes 196616 | tf_op jit(solution)/shard_map/ppermute | solution.py:323
  142.2 2.1 %shard_map.155 = bf16[256,512]{1,0:T(8,128)(2,1)} custom-call(bf16[256,512]{1,0:T(8,128)(2,1)} %get-tuple-element.54.att, bf16[256,512]{1,0:T(8,128)(2,1)S(1)} %bitcast.31, f32[1,512]{1,0:T(1,128)S(1)} %bitcast.40, bf16[256,256]{1,0:T(8,128)(2,1)S(1)} %copy-done.16, f32[16,16]{1,0:T(8,128)S(1)} %bitcast.36, bf16[128,4,512]{2,1,0:T(4,128)(2,1)S(1)} %all-to-all-done.1.back), custom_call_target="tpu_custom_call" | custom-call | flops 1000000000 | bytes 1048576 | tf_op jit(solution)/shard_map/pallas_call | solution.py:460
  144.3 0.6 collective-permute-done.19
  144.9 3.4 %collective-permute-done.18 = bf16[8,8,512]{2,1,0:T(8,128)(2,1)S(1)} collective-permute-done((bf16[8,8,512]{2,1,0:T(8,128)(2,1)S(1)}, bf16[8,8,512]{2,1,0:T(8,128)(2,1)S(1)}, u32[]{:S(2)}, u32[]{:S(2)}) %collective-permute-start.18) | collective-permute-done | bytes 65568 | tf_op jit(solution)/shard_map/ppermute | solution.py:323
  148.3 0.8 add_convert_fusion
  149.1 1.8 %slice_convert_fusion = (f32[1,128,512]{2,1,0:T(8,128)}, f32[1,128,512]{2,1,0:T(8,128)}) fusion(bf16[1,128,1024]{2,1,0:T(8,128)(2,1)} %bitcast.46), kind=kLoop, calls=%fused_computation.6 | loop fusion | flops 131072 | bytes 786432 | tf_op jit(solution)/shard_map/convert_element_type | solution.py:447
  (81 shorter events, 0.8 us)
Async XLA Ops:
  7.2 22.9 %copy-start.2 = (bf16[1,16,16,512]{3,2,1,0:T(8,128)(2,1)S(1)}, bf16[1,16,16,512]{3,2,1,0:T(8,128)(2,1)}, u32[]{:S(2)}) copy-start(bf16[1,16,16,512]{3,2,1,0:T(8,128)(2,1)} %param.12) | copy-start | bytes 786436
  7.2 22.9 %copy-start.14 = (f32[16]{0:T(128)S(1)}, f32[16]{0:T(128)}, u32[]{:S(2)}) copy-start(f32[16]{0:T(128)} %scale.3) | copy-start | bytes 196
  7.2 22.9 %copy-start.4 = (bf16[512,512]{1,0:T(8,128)(2,1)S(1)}, bf16[512,512]{1,0:T(8,128)(2,1)}, u32[]{:S(2)}) copy-start(bf16[512,512]{1,0:T(8,128)(2,1)} %proj.3) | copy-start | bytes 1572868
  7.2 22.9 %copy-start.3 = (bf16[512,1536]{1,0:T(8,128)(2,1)S(1)}, bf16[512,1536]{1,0:T(8,128)(2,1)}, u32[]{:S(2)}) copy-start(bf16[512,1536]{1,0:T(8,128)(2,1)} %wqkv.3) | copy-start | bytes 4718596
  7.2 22.9 %copy-start.9 = (f32[16,961]{1,0:T(8,128)S(1)}, f32[16,961]{1,0:T(8,128)}, u32[]{:S(2)}) copy-start(f32[16,961]{1,0:T(8,128)} %table.1) | copy-start | bytes 184516
  7.2 50.4 %all-gather.3.cloned.1.call-start = ((), (), s32[]{:S(2)}) async-start(), calls=%async_computation.4 | async-start | bytes 3145728 | tf_op jit(solution)/shard_map/all_gather | solution.py:345
  10.6 16.4 %collective-permute-start.2 = (bf16[8,8,512]{2,1,0:T(8,128)(2,1)S(1)}, bf16[8,8,512]{2,1,0:T(8,128)(2,1)S(1)}, u32[]{:S(2)}, u32[]{:S(2)}) collective-permute-start(bf16[8,8,512]{2,1,0:T(8,128)(2,1)S(1)} %get-tuple-element.96), channel_id=1, source_target_pairs={{0,127},{1,112},{2,113},{3,114},{4,115},{5,116},{6,117},{7,118},{8... | collective-permute-start | bytes 196616 | tf_op jit(solution)/shard_map/ppermute | solution.py:323
  23.9 6.2 %collective-permute-start.1 = (bf16[8,8,512]{2,1,0:T(8,128)(2,1)S(1)}, bf16[8,8,512]{2,1,0:T(8,128)(2,1)S(1)}, u32[]{:S(2)}, u32[]{:S(2)}) collective-permute-start(bf16[8,8,512]{2,1,0:T(8,128)(2,1)S(1)} %get-tuple-element.97), channel_id=1, source_target_pairs={{0,112},{16,0},{32,16},{48,32},{64,48},{80,64},{96,80},{112,96},{1... | collective-permute-start | bytes 196616 | tf_op jit(solution)/shard_map/ppermute | solution.py:315
  26.4 3.7 %collective-permute-start = (bf16[8,8,512]{2,1,0:T(8,128)(2,1)S(1)}, bf16[8,8,512]{2,1,0:T(8,128)(2,1)S(1)}, u32[]{:S(2)}, u32[]{:S(2)}) collective-permute-start(bf16[8,8,512]{2,1,0:T(8,128)(2,1)S(1)} %get-tuple-element.98), channel_id=1, source_target_pairs={{0,15},{1,0},{2,1},{3,2},{4,3},{5,4},{6,5},{7,6},{8,7},{9,8},{10,9... | collective-permute-start | bytes 196616 | tf_op jit(solution)/shard_map/ppermute | solution.py:317
  27.0 13.6 %copy-start.7 = (bf16[1,16,16,512]{3,2,1,0:T(8,128)(2,1)S(1)}, bf16[1,16,16,512]{3,2,1,0:T(8,128)(2,1)}, u32[]{:S(2)}) copy-start(bf16[1,16,16,512]{3,2,1,0:T(8,128)(2,1)} %param.23) | copy-start | bytes 786436
  27.0 13.6 %copy-start.10 = (s32[1,16,16,1]{2,3,1,0:T(1,128)S(1)}, s32[1,16,16,1]{2,3,1,0:T(1,128)}, u32[]{:S(2)}) copy-start(s32[1,16,16,1]{2,3,1,0:T(1,128)} %param.18) | copy-start | bytes 3076
  27.0 13.6 %copy-start.11 = (f32[1,16,16]{2,1,0:T(8,128)S(1)}, f32[1,16,16]{2,1,0:T(8,128)}, u32[]{:S(2)}) copy-start(f32[1,16,16]{2,1,0:T(8,128)} %param.19) | copy-start | bytes 3076
  36.5 5.3 %copy-start.21 = (bf16[512,256]{1,0:T(8,128)(2,1)}, bf16[512,256]{1,0:T(8,128)(2,1)S(1)}, u32[]{:S(2)}) copy-start(bf16[512,256]{1,0:T(8,128)(2,1)S(1)} %get-tuple-element.79.vt) | copy-start | bytes 786436
  36.5 5.3 %copy-start.23 = (bf16[512,256]{1,0:T(8,128)(2,1)}, bf16[512,256]{1,0:T(8,128)(2,1)S(1)}, u32[]{:S(2)}) copy-start(bf16[512,256]{1,0:T(8,128)(2,1)S(1)} %get-tuple-element.82.ho) | copy-start | bytes 786436
  36.5 8.9 %collective-permute-start.3 = (bf16[8,8,512]{2,1,0:T(8,128)(2,1)S(1)}, bf16[8,8,512]{2,1,0:T(8,128)(2,1)S(1)}, u32[]{:S(2)}, u32[]{:S(2)}) collective-permute-start(bf16[8,8,512]{2,1,0:T(8,128)(2,1)S(1)} %get-tuple-element.47), channel_id=1, source_target_pairs={{0,17},{1,18},{2,19},{3,20},{4,21},{5,22},{6,23},{7,24},{8,25},{9,... | collective-permute-start | bytes 196616 | tf_op jit(solution)/shard_map/ppermute | solution.py:323
  38.4 7.7 %collective-permute-start.4 = (bf16[8,8,512]{2,1,0:T(8,128)(2,1)S(1)}, bf16[8,8,512]{2,1,0:T(8,128)(2,1)S(1)}, u32[]{:S(2)}, u32[]{:S(2)}) collective-permute-start(bf16[8,8,512]{2,1,0:T(8,128)(2,1)S(1)} %get-tuple-element.48), channel_id=1, source_target_pairs={{0,16},{16,32},{32,48},{48,64},{64,80},{80,96},{96,112},{112,0},{1... | collective-permute-start | bytes 196616 | tf_op jit(solution)/shard_map/ppermute | solution.py:315
  40.6 5.5 %collective-permute-start.5 = (bf16[8,8,512]{2,1,0:T(8,128)(2,1)S(1)}, bf16[8,8,512]{2,1,0:T(8,128)(2,1)S(1)}, u32[]{:S(2)}, u32[]{:S(2)}) collective-permute-start(bf16[8,8,512]{2,1,0:T(8,128)(2,1)S(1)} %get-tuple-element.49), channel_id=1, source_target_pairs={{0,1},{1,2},{2,3},{3,4},{4,5},{5,6},{6,7},{7,8},{8,9},{9,10},{10,1... | collective-permute-start | bytes 196616 | tf_op jit(solution)/shard_map/ppermute | solution.py:317
  40.7 5.5 %copy-start.13 = (f32[512]{0:T(512)S(1)}, f32[512]{0:T(512)}, u32[]{:S(2)}) copy-start(f32[512]{0:T(512)} %param.17) | copy-start | bytes 6148
  41.8 6.0 %copy-start.15 = (bf16[256,256]{1,0:T(8,128)(2,1)}, bf16[256,256]{1,0:T(8,128)(2,1)S(1)}, u32[]{:S(2)}) copy-start(bf16[256,256]{1,0:T(8,128)(2,1)S(1)} %get-tuple-element.52.place) | copy-start | bytes 393220
  47.8 29.1 %all-to-all-start = ((bf16[128,4,512]{2,1,0:T(4,128)(2,1)}), bf16[128,4,512]{2,1,0:T(4,128)(2,1)S(1)}, u32[]{:S(2)}, u32[]{:S(2)}) async-start(bf16[128,4,512]{2,1,0:T(4,128)(2,1)} %get-tuple-element.55), calls=%async_computation | async-start | bytes 1048576 | tf_op jit(solution)/shard_map/all_to_all | solution.py:335
  60.2 19.0 %copy-start = (bf16[512,512]{1,0:T(8,128)(2,1)}, bf16[512,512]{1,0:T(8,128)(2,1)S(1)}, u32[]{:S(2)}) copy-start(bf16[512,512]{1,0:T(8,128)(2,1)S(1)} %get-tuple-element.60.block1.refs_1_) | copy-start | bytes 1572868
  60.3 19.1 %copy-start.1 = (bf16[512,512]{1,0:T(8,128)(2,1)}, bf16[512,512]{1,0:T(8,128)(2,1)S(1)}, u32[]{:S(2)}) copy-start(bf16[512,512]{1,0:T(8,128)(2,1)S(1)} %get-tuple-element.59.block0.refs_0_) | copy-start | bytes 1572868
  60.3 23.2 %copy-start.12 = (f32[512]{0:T(512)S(1)}, f32[512]{0:T(512)}, u32[]{:S(2)}) copy-start(f32[512]{0:T(512)} %param.22) | copy-start | bytes 6148
  60.3 16.6 %collective-permute-start.6 = (bf16[512,512]{1,0:T(8,128)(2,1)S(1)}, bf16[512,512]{1,0:T(8,128)(2,1)}, u32[]{:S(2)}, u32[]{:S(2)}) collective-permute-start(bf16[512,512]{1,0:T(8,128)(2,1)S(1)} %get-tuple-element.59.block0.refs_0_), channel_id=1, source_target_pairs={{0,1},{1,0},{2,3},{3,2},{4,5},{5,4},{6,7},{7,6},{8,9},{9,8},{10,11... | collective-permute-start | bytes 1572872 | tf_op jit(solution)/shard_map/ppermute | solution.py:339
  62.2 14.7 %collective-permute-start.7 = (bf16[512,512]{1,0:T(8,128)(2,1)S(1)}, bf16[512,512]{1,0:T(8,128)(2,1)}, u32[]{:S(2)}, u32[]{:S(2)}) collective-permute-start(bf16[512,512]{1,0:T(8,128)(2,1)S(1)} %get-tuple-element.60.block1.refs_1_), channel_id=1, source_target_pairs={{0,1},{1,0},{2,3},{3,2},{4,5},{5,4},{6,7},{7,6},{8,9},{9,8},{10,11... | collective-permute-start | bytes 1572872 | tf_op jit(solution)/shard_map/ppermute | solution.py:339
  64.6 18.9 %collective-permute-start.8 = (bf16[512,512]{1,0:T(8,128)(2,1)}, bf16[512,512]{1,0:T(8,128)(2,1)}, u32[]{:S(2)}, u32[]{:S(2)}) collective-permute-start(bf16[512,512]{1,0:T(8,128)(2,1)} %get-tuple-element.63.refs_2_), channel_id=1, source_target_pairs={{0,1},{1,0},{2,3},{3,2},{4,5},{5,4},{6,7},{7,6},{8,9},{9,8},{10,11... | collective-permute-start | bytes 1572872 | tf_op jit(solution)/shard_map/ppermute | solution.py:339
  66.5 16.9 %collective-permute-start.9 = (bf16[512,512]{1,0:T(8,128)(2,1)}, bf16[512,512]{1,0:T(8,128)(2,1)}, u32[]{:S(2)}, u32[]{:S(2)}) collective-permute-start(bf16[512,512]{1,0:T(8,128)(2,1)} %get-tuple-element.64.refs_3_), channel_id=1, source_target_pairs={{0,1},{1,0},{2,3},{3,2},{4,5},{5,4},{6,7},{7,6},{8,9},{9,8},{10,11... | collective-permute-start | bytes 1572872 | tf_op jit(solution)/shard_map/ppermute | solution.py:339
  79.3 12.2 %collective-permute-start.10 = (bf16[256,512]{1,0:T(8,128)(2,1)S(1)}, bf16[256,512]{1,0:T(8,128)(2,1)S(1)}, u32[]{:S(2)}, u32[]{:S(2)}) collective-permute-start(bf16[256,512]{1,0:T(8,128)(2,1)S(1)} %get-tuple-element.66), channel_id=1, source_target_pairs={{0,2},{1,3},{2,0},{3,1},{4,6},{5,7},{6,4},{7,5},{8,10},{9,11},{10,... | collective-permute-start | bytes 786440 | tf_op jit(solution)/shard_map/ppermute | solution.py:339
  89.6 18.6 %copy-start.6 = (bf16[2,256,512]{2,1,0:T(8,128)(2,1)}, bf16[2,256,512]{2,1,0:T(8,128)(2,1)S(1)}, u32[]{:S(2)}) copy-start(bf16[2,256,512]{2,1,0:T(8,128)(2,1)S(1)} %get-tuple-element.70.own) | copy-start | bytes 1572868
  89.6 9.7 %collective-permute-start.11 = (bf16[256,512]{1,0:T(8,128)(2,1)S(1)}, bf16[256,512]{1,0:T(8,128)(2,1)S(1)}, u32[]{:S(2)}, u32[]{:S(2)}) collective-permute-start(bf16[256,512]{1,0:T(8,128)(2,1)S(1)} %get-tuple-element.69), channel_id=1, source_target_pairs={{0,2},{1,3},{2,0},{3,1},{4,6},{5,7},{6,4},{7,5},{8,10},{9,11},{10,... | collective-permute-start | bytes 786440 | tf_op jit(solution)/shard_map/ppermute | solution.py:339
  92.2 26.0 %all-to-all-start.1 = ((bf16[128,4,512]{2,1,0:T(4,128)(2,1)}), bf16[128,4,512]{2,1,0:T(4,128)(2,1)S(1)}, u32[]{:S(2)}, u32[]{:S(2)}) async-start(bf16[128,4,512]{2,1,0:T(4,128)(2,1)} %get-tuple-element.67), calls=%async_computation.1 | async-start | bytes 1048576 | tf_op jit(solution)/shard_map/all_to_all | solution.py:335
  98.9 50.2 %reduce-scatter.2.cloned.1.call-start = ((), (), s32[]{:S(2)}) async-start(), calls=%async_computation.3 | async-start | bytes 1310720 | tf_op jit(solution)/shard_map/reduce_scatter | solution.py:445
  100.0 18.2 %copy-start.8 = (bf16[1,16,16,512]{3,2,1,0:T(8,128)(2,1)S(1)}, bf16[1,16,16,512]{3,2,1,0:T(8,128)(2,1)}, u32[]{:S(2)}) copy-start(bf16[1,16,16,512]{3,2,1,0:T(8,128)(2,1)} %param.23) | copy-start | bytes 786436
  100.0 8.1 %collective-permute-start.12 = (bf16[2,256,512]{2,1,0:T(8,128)(2,1)S(1)}, bf16[2,256,512]{2,1,0:T(8,128)(2,1)S(1)}, u32[]{:S(2)}, u32[]{:S(2)}) collective-permute-start(bf16[2,256,512]{2,1,0:T(8,128)(2,1)S(1)} %get-tuple-element.70.own), channel_id=1, source_target_pairs={{0,1},{1,0},{2,3},{3,2},{4,5},{5,4},{6,7},{7,6},{8,9},{9,8},{10,11... | collective-permute-start | bytes 1572872 | tf_op jit(solution)/shard_map/ppermute | solution.py:339
  102.1 4.3 %collective-permute-start.14 = (bf16[256,512]{1,0:T(8,128)(2,1)}, bf16[256,512]{1,0:T(8,128)(2,1)S(1)}, u32[]{:S(2)}, u32[]{:S(2)}) collective-permute-start(bf16[256,512]{1,0:T(8,128)(2,1)} %copy-done.27), channel_id=1, source_target_pairs={{0,1},{1,0},{2,3},{3,2},{4,5},{5,4},{6,7},{7,6},{8,9},{9,8},{10,11... | collective-permute-start | bytes 786440 | tf_op jit(solution)/shard_map/ppermute | solution.py:339
  104.5 3.6 %collective-permute-start.13 = (bf16[256,512]{1,0:T(8,128)(2,1)}, bf16[256,512]{1,0:T(8,128)(2,1)S(1)}, u32[]{:S(2)}, u32[]{:S(2)}) collective-permute-start(bf16[256,512]{1,0:T(8,128)(2,1)} %copy-done.26), channel_id=1, source_target_pairs={{0,1},{1,0},{2,3},{3,2},{4,5},{5,4},{6,7},{7,6},{8,9},{9,8},{10,11... | collective-permute-start | bytes 786440 | tf_op jit(solution)/shard_map/ppermute | solution.py:339
  118.2 12.6 %copy-start.5 = (bf16[512,512]{1,0:T(8,128)(2,1)S(1)}, bf16[512,512]{1,0:T(8,128)(2,1)}, u32[]{:S(2)}) copy-start(bf16[512,512]{1,0:T(8,128)(2,1)} %proj.3) | copy-start | bytes 1572868
  118.2 12.6 %copy-start.18 = (bf16[512,256]{1,0:T(8,128)(2,1)S(1)}, bf16[512,256]{1,0:T(8,128)(2,1)}, u32[]{:S(2)}) copy-start(bf16[512,256]{1,0:T(8,128)(2,1)} %copy-done.17) | copy-start | bytes 786436
  118.2 12.6 %copy-start.20 = (bf16[512,256]{1,0:T(8,128)(2,1)S(1)}, bf16[512,256]{1,0:T(8,128)(2,1)}, u32[]{:S(2)}) copy-start(bf16[512,256]{1,0:T(8,128)(2,1)} %copy-done.19) | copy-start | bytes 786436
  118.2 12.6 %copy-start.22 = (bf16[512,256]{1,0:T(8,128)(2,1)S(1)}, bf16[512,256]{1,0:T(8,128)(2,1)}, u32[]{:S(2)}) copy-start(bf16[512,256]{1,0:T(8,128)(2,1)} %copy-done.21) | copy-start | bytes 786436
  118.2 12.6 %copy-start.24 = (bf16[512,256]{1,0:T(8,128)(2,1)S(1)}, bf16[512,256]{1,0:T(8,128)(2,1)}, u32[]{:S(2)}) copy-start(bf16[512,256]{1,0:T(8,128)(2,1)} %copy-done.23) | copy-start | bytes 786436
  119.8 7.5 %collective-permute-start.15 = (bf16[8,8,512]{2,1,0:T(8,128)(2,1)S(1)}, bf16[8,8,512]{2,1,0:T(8,128)(2,1)S(1)}, u32[]{:S(2)}, u32[]{:S(2)}) collective-permute-start(bf16[8,8,512]{2,1,0:T(8,128)(2,1)S(1)} %get-tuple-element.74), channel_id=1, source_target_pairs={{0,15},{1,0},{2,1},{3,2},{4,3},{5,4},{6,5},{7,6},{8,7},{9,8},{10,9... | collective-permute-start | bytes 196616 | tf_op jit(solution)/shard_map/ppermute | solution.py:317
  120.4 7.0 %collective-permute-start.16 = (bf16[8,8,512]{2,1,0:T(8,128)(2,1)S(1)}, bf16[8,8,512]{2,1,0:T(8,128)(2,1)S(1)}, u32[]{:S(2)}, u32[]{:S(2)}) collective-permute-start(bf16[8,8,512]{2,1,0:T(8,128)(2,1)S(1)} %get-tuple-element.75), channel_id=1, source_target_pairs={{0,112},{16,0},{32,16},{48,32},{64,48},{80,64},{96,80},{112,96},{1... | collective-permute-start | bytes 196616 | tf_op jit(solution)/shard_map/ppermute | solution.py:315
  124.6 6.3 %collective-permute-start.17 = (bf16[8,8,512]{2,1,0:T(8,128)(2,1)S(1)}, bf16[8,8,512]{2,1,0:T(8,128)(2,1)S(1)}, u32[]{:S(2)}, u32[]{:S(2)}) collective-permute-start(bf16[8,8,512]{2,1,0:T(8,128)(2,1)S(1)} %get-tuple-element.76), channel_id=1, source_target_pairs={{0,127},{1,112},{2,113},{3,114},{4,115},{5,116},{6,117},{7,118},{8... | collective-permute-start | bytes 196616 | tf_op jit(solution)/shard_map/ppermute | solution.py:323
  130.9 11.3 %copy-start.16 = (bf16[256,256]{1,0:T(8,128)(2,1)S(1)}, bf16[256,256]{1,0:T(8,128)(2,1)}, u32[]{:S(2)}) copy-start(bf16[256,256]{1,0:T(8,128)(2,1)} %copy-done.15) | copy-start | bytes 393220
  137.2 7.1 %collective-permute-start.20 = (bf16[8,8,512]{2,1,0:T(8,128)(2,1)S(1)}, bf16[8,8,512]{2,1,0:T(8,128)(2,1)S(1)}, u32[]{:S(2)}, u32[]{:S(2)}) collective-permute-start(bf16[8,8,512]{2,1,0:T(8,128)(2,1)S(1)} %get-tuple-element.84), channel_id=1, source_target_pairs={{0,1},{1,2},{2,3},{3,4},{4,5},{5,6},{6,7},{7,8},{8,9},{9,10},{10,1... | collective-permute-start | bytes 196616 | tf_op jit(solution)/shard_map/ppermute | solution.py:317
  137.2 7.7 %collective-permute-start.19 = (bf16[8,8,512]{2,1,0:T(8,128)(2,1)S(1)}, bf16[8,8,512]{2,1,0:T(8,128)(2,1)S(1)}, u32[]{:S(2)}, u32[]{:S(2)}) collective-permute-start(bf16[8,8,512]{2,1,0:T(8,128)(2,1)S(1)} %get-tuple-element.85), channel_id=1, source_target_pairs={{0,16},{16,32},{32,48},{48,64},{64,80},{80,96},{96,112},{112,0},{1... | collective-permute-start | bytes 196616 | tf_op jit(solution)/shard_map/ppermute | solution.py:315
  139.3 9.0 %collective-permute-start.18 = (bf16[8,8,512]{2,1,0:T(8,128)(2,1)S(1)}, bf16[8,8,512]{2,1,0:T(8,128)(2,1)S(1)}, u32[]{:S(2)}, u32[]{:S(2)}) collective-permute-start(bf16[8,8,512]{2,1,0:T(8,128)(2,1)S(1)} %get-tuple-element.86), channel_id=1, source_target_pairs={{0,17},{1,18},{2,19},{3,20},{4,21},{5,22},{6,23},{7,24},{8,25},{9,... | collective-permute-start | bytes 196616 | tf_op jit(solution)/shard_map/ppermute | solution.py:323
  (7 other events, 15.2 us)
Sparse Core Ops, SparseCore 0:
  10.7 45.6 all-gather.2
  118.3 24.8 reduce-scatter.1
